TPU v7x, 32 devices: a whole 2x2x4 slice. The times are simulated.
32 devices in a mesh: groups: 2 (over y), series: 2 (over core), tm: 8 (over z, x).
Axes of the slice: x: 2, y: 2, z: 4, core: 2. Of those that a mesh axis runs over, the one named last changes fastest.
Arguments:
- history: bfloat16 [4, 8192, 512], P(('groups', 'series'), 'tm'), parts along dimension 0, may hold values from -6 to 6
- convolution_taps: float32 [2, 3, 512], replicated, may hold values from -3 to 3
- norm_gain_pair: float32 [2, 512], replicated, may hold values from 0.25 to 1.75
- up_projection: bfloat16 [2, 512, 1024], replicated, may hold values from -0.25 to 0.25
- down_projection: bfloat16 [2, 1024, 512], replicated, may hold values from -0.1875 to 0.1875
- w_kv: bfloat16 [512, 1024], replicated, may hold values from -0.25 to 0.25
- readout_matrix: bfloat16 [512, 512], replicated, may hold values from -0.25 to 0.25
- queries: bfloat16 [128, 512], replicated, may hold values from -64 to 64
Outputs:
- prediction_matrix: bfloat16 [4, 128, 512], P(('groups', 'series'), 'tm'), parts along dimension 0
There are 2 independent parts, one for each index of `groups`. A program takes and returns all parts, laid end to end along the dimension named above; an argument that names none is the same for every part. Nothing has to cross between parts.
All inputs are finite; a program needn't handle non-finite values.
Results may differ from a plain program's by a relative error of at most 0.033.
Values may be sent and summed in bfloat16 or wider, within the bound.
No kernel may reach another device: no remote copies, remote signals or barrier semaphores. Data moves between devices by JAX's collectives and lax.ppermute only.
A program may use at most 128 MiB of HBM per device.

v0:
```python
import jax
import jax.numpy as jnp
from jax import lax
from jax.sharding import PartitionSpec as P

HEADS = 8
FIRST_DILATION = 256
SECOND_DILATION = 512


def from_behind(value, axis, steps):
    count = lax.axis_size(axis)
    leading, last = (max(0, -steps), min(count, count - steps))
    return lax.ppermute(value, axis, [(source, source + steps) for source in range(leading, last)])


def merged(part, axis, combine):
    gathered = jax.tree.map(lambda a: lax.all_gather(a, axis), part)

    def take(source):
        return jax.tree.map(lambda a: lax.dynamic_index_in_dim(a, source, 0, False), gathered)

    return lax.fori_loop(
        1, lax.axis_size(axis), lambda source, state: combine(state, take(source)), take(0)
    )


def combine_parts(first_output, second_output):
    heads = first_output[0].shape[1]
    repeat = first_output[2].shape[-1] // heads
    top = jnp.maximum(first_output[0], second_output[0])
    left = jnp.exp(first_output[0] - top)
    right = jnp.exp(second_output[0] - top)
    total = first_output[1] * left + second_output[1] * right
    left_rows = jnp.repeat(left.transpose(0, 2, 1), repeat, axis=-1)
    right_rows = jnp.repeat(right.transpose(0, 2, 1), repeat, axis=-1)
    context = first_output[2] * left_rows + second_output[2] * right_rows
    return (top, total, context)


def on_device(
    history,
    convolution_taps,
    norm_gain_pair,
    up_projection,
    down_projection,
    w_kv,
    readout_matrix,
    queries,
):
    sample_group_signal, receptive_span, feature_dimension = history.shape
    horizon = queries.shape[0]

    def apply_block(extended, index, dilation):
        values = extended.astype(jnp.float32)
        rows = extended.shape[1] - 2 * dilation
        running_state = values[:, 2 * dilation :, :]
        mixed = convolution_taps[index, 0] * running_state
        mixed = mixed + convolution_taps[index, 1] * values[:, dilation : dilation + rows, :]
        mixed = mixed + convolution_taps[index, 2] * values[:, :rows, :]
        scaled = (
            mixed
            * lax.rsqrt(jnp.mean(mixed * mixed, axis=-1, keepdims=True) + 1e-05)
            * norm_gain_pair[index]
        )
        normed = scaled.astype(jnp.bfloat16).reshape(sample_group_signal * rows, feature_dimension)
        lifted = jnp.dot(normed, up_projection[index], preferred_element_type=jnp.float32)
        inner = jax.nn.gelu(lifted, approximate=True).astype(jnp.bfloat16)
        lowered = jnp.dot(inner, down_projection[index], preferred_element_type=jnp.float32)
        result = running_state.reshape(sample_group_signal * rows, feature_dimension) + lowered
        return result.astype(jnp.bfloat16).reshape(sample_group_signal, rows, feature_dimension)

    earlier_values = from_behind(history[:, receptive_span - 2 * FIRST_DILATION :, :], "tm", 1)
    first_output = apply_block(
        jnp.concatenate([earlier_values, history], axis=1), 0, FIRST_DILATION
    )
    earlier_twice = from_behind(first_output, "tm", 1)
    second_output = apply_block(
        jnp.concatenate([earlier_twice, first_output], axis=1), 1, SECOND_DILATION
    )
    flat = second_output.reshape(sample_group_signal * receptive_span, feature_dimension)
    pairs = jnp.dot(flat, w_kv, preferred_element_type=jnp.float32).astype(jnp.bfloat16)
    head_size = feature_dimension // HEADS
    keys = pairs[:, :feature_dimension].reshape(
        sample_group_signal, receptive_span, HEADS, head_size
    )
    values = pairs[:, feature_dimension:].reshape(
        sample_group_signal, receptive_span, HEADS, head_size
    )
    asked = queries.reshape(horizon, HEADS, head_size)
    scores = jnp.einsum(
        "qhd,bthd->bhqt", asked, keys, preferred_element_type=jnp.float32
    ) * head_size ** (-0.5)
    top = jnp.max(scores, axis=-1)
    expo = jnp.exp(scores - top[..., None])
    total = jnp.sum(expo, axis=-1)
    weights = expo.astype(jnp.bfloat16)
    context = jnp.einsum("bhqt,bthd->bqhd", weights, values, preferred_element_type=jnp.float32)
    context = context.reshape(sample_group_signal, horizon, feature_dimension)
    common_fraction = horizon // lax.axis_size("tm")
    top, total, context = merged((top, total, context), "tm", combine_parts)
    first_row = lax.axis_index("tm") * common_fraction
    total = lax.dynamic_slice_in_dim(total, first_row, common_fraction, 2).transpose(0, 2, 1)
    context = lax.dynamic_slice_in_dim(context, first_row, common_fraction, 1)
    blended_past_signal = (context / jnp.repeat(total, head_size, axis=-1)).astype(jnp.bfloat16)
    blended_past_signal = blended_past_signal.reshape(
        sample_group_signal * common_fraction, feature_dimension
    )
    prediction_matrix = jnp.dot(
        blended_past_signal, readout_matrix, preferred_element_type=jnp.float32
    )
    return prediction_matrix.astype(jnp.bfloat16).reshape(
        sample_group_signal, common_fraction, feature_dimension
    )


def solution(mesh):
    placed = (P(("groups", "series"), "tm", None), P(), P(), P(), P(), P(), P(), P())
    return jax.shard_map(
        on_device,
        mesh=mesh,
        in_specs=placed,
        out_specs=P(("groups", "series"), "tm", None),
        check_vma=False,
    )
```

profile of v0, /device:TPU:0, one launch (start us, length us, event | category | flops | bytes accessed | tf_op | source)
XLA Modules:
  0.0 159.9 jit_solution(8090833688869278741)
XLA Ops:
  6.5 1.2 slice.66
  7.7 4.9 %collective-permute-start = (bf16[1,512,512]{2,1,0:T(8,128)(2,1)S(1)}, bf16[1,512,512]{2,1,0:T(8,128)(2,1)S(1)}, u32[]{:S(2)}, u32[]{:S(2)}) collective-permute-start(bf16[1,512,512]{2,1,0:T(8,128)(2,1)S(1)} %slice.66), channel_id=1, source_target_pairs={{0,1},{1,2},{2,3},{3,4},{4,5},{5,6},{6,7},{8,9},{9,10},{10,11},{11... | collective-permute-start | bytes 1572872 | tf_op jit(solution)/shard_map/ppermute | solution.py:14
  12.6 0.8 fusion.80
  13.4 0.8 fusion.79
  14.1 9.6 %collective-permute-done = bf16[1,512,512]{2,1,0:T(8,128)(2,1)S(1)} collective-permute-done((bf16[1,512,512]{2,1,0:T(8,128)(2,1)S(1)}, bf16[1,512,512]{2,1,0:T(8,128)(2,1)S(1)}, u32[]{:S(2)}, u32[]{:S(2)}) %collective-permute-start) | collective-permute-done | bytes 524320 | tf_op jit(solution)/shard_map/ppermute | solution.py:14
  23.7 1.7 %maximum_convert_fusion.1 = f32[1,1536,512]{2,1,0:T(8,128)S(1)} fusion(bf16[1,1024,512]{2,1,0:T(8,128)(2,1)} %param.10, bf16[1,512,512]{2,1,0:T(8,128)(2,1)S(1)} %collective-permute-done), kind=kLoop, calls=%fused_computation.57 | loop fusion | flops 3145728 | bytes 4718592 | tf_op jit(solution)/shard_map/convert_element_type | solution.py:55
  25.4 0.6 multiply_reduce_fusion.1
  26.0 1.1 copy-done.2
  27.0 5.7 %fusion.37 = bf16[1,1024,512]{2,1,0:T(8,128)(2,1)} fusion(f32[1,1536,512]{2,1,0:T(8,128)} %copy-done.2, f32[1,1024,512]{2,1,0:T(8,128)S(1)} %get-tuple-element.210, bf16[2,1024,512]{2,1,0:T(8,128)(2,1)} %param.14, bf16[2,512,1024]{2,1,0:T(8,128)(2,1)} %param.13, f32[512]{0:T(512)S(1)} %bitcast.151, f32[1024]{0:T(1024)S(1)} %add_rsqrt_fusion.1), kind=kOutput, calls=%fused_computation.60 | convolution fusion | flops 2159542272 | bytes 7346176 | tf_op jit(solution)/shard_map/dot_general | solution.py:69
  32.8 4.4 %collective-permute-start.1 = (bf16[1,1024,512]{2,1,0:T(8,128)(2,1)}, bf16[1,1024,512]{2,1,0:T(8,128)(2,1)S(1)}, u32[]{:S(2)}, u32[]{:S(2)}) collective-permute-start(bf16[1,1024,512]{2,1,0:T(8,128)(2,1)} %fusion.37), channel_id=1, source_target_pairs={{0,1},{1,2},{2,3},{3,4},{4,5},{5,6},{6,7},{8,9},{9,10},{10,11},{11... | collective-permute-start | bytes 3145736 | tf_op jit(solution)/shard_map/ppermute | solution.py:14
  37.2 0.1 copy.17
  37.3 21.6 %collective-permute-done.1 = bf16[1,1024,512]{2,1,0:T(8,128)(2,1)S(1)} collective-permute-done((bf16[1,1024,512]{2,1,0:T(8,128)(2,1)}, bf16[1,1024,512]{2,1,0:T(8,128)(2,1)S(1)}, u32[]{:S(2)}, u32[]{:S(2)}) %collective-permute-start.1) | collective-permute-done | bytes 1048608 | tf_op jit(solution)/shard_map/ppermute | solution.py:14
  59.0 1.8 %maximum_convert_fusion = f32[1,2048,512]{2,1,0:T(8,128)S(1)} fusion(bf16[1,1024,512]{2,1,0:T(8,128)(2,1)} %fusion.37, bf16[1,1024,512]{2,1,0:T(8,128)(2,1)S(1)} %collective-permute-done.1), kind=kLoop, calls=%fused_computation.45 | loop fusion | flops 4194304 | bytes 6291456 | tf_op jit(solution)/shard_map/convert_element_type | solution.py:55
  60.8 0.6 multiply_reduce_fusion
  61.4 1.4 copy-done.3
  62.7 5.7 %fusion.31 = bf16[1024,512]{1,0:T(8,128)(2,1)} fusion(f32[1,2048,512]{2,1,0:T(8,128)} %copy-done.3, f32[1,1024,512]{2,1,0:T(8,128)S(1)} %get-tuple-element.208, bf16[2,1024,512]{2,1,0:T(8,128)(2,1)} %param.14, bf16[2,512,1024]{2,1,0:T(8,128)(2,1)} %param.13, f32[512]{0:T(512)S(1)} %bitcast.150, f32[1024]{0:T(1024)S(1)} %add_rsqrt_fusion), kind=kOutput, calls=%fused_computation.47 | convolution fusion | flops 2159542272 | bytes 7346176 | tf_op jit(solution)/shard_map/dot_general | solution.py:69
  68.4 2.5 %convolution_convert_fusion = bf16[1024,1024]{0,1:T(8,128)(2,1)S(1)} fusion(bf16[1024,512]{1,0:T(8,128)(2,1)} %fusion.31, bf16[512,1024]{1,0:T(8,128)(2,1)S(1)} %copy-done), kind=kOutput, calls=%fused_computation.56 | convolution fusion | flops 1074790400 | bytes 4194304 | tf_op jit(solution)/shard_map/dot_general | solution.py:82
  70.9 0.2 fusion.78
  71.1 0.8 bitcast_reduce_fusion
  72.0 0.9 fusion.25
  72.8 1.1 copy-done.1
  73.9 0.8 copy.19
  74.8 33.5 %all-gather = f32[64,128]{1,0:T(8,128)S(1)} all-gather(f32[8,128]{1,0:T(8,128)S(1)} %get-tuple-element.223), channel_id=2, replica_groups=mesh['groups'=2,'series'=2,'tm'=8] {'tm'}, dimensions={0}, use_global_device_ids=true | all-gather | bytes 36864 | tf_op jit(solution)/shard_map/all_gather | solution.py:18
  108.2 2.9 %fusion.23 = f32[8,128]{1,0:T(8,128)S(1)} fusion(f32[8,1024,128]{2,1,0:T(8,128)} %copy-done.1, f32[8,128]{1,0:T(8,128)S(1)} %get-tuple-element.223), kind=kLoop, calls=%fused_computation.34 | loop fusion | flops 3144704 | bytes 4202496 | tf_op jit(solution)/shard_map/reduce_sum | solution.py:96
  111.1 30.7 %all-gather.1 = f32[64,128]{1,0:T(8,128)S(1)} all-gather(f32[8,128]{1,0:T(8,128)S(1)} %fusion.23), channel_id=3, replica_groups=mesh['groups'=2,'series'=2,'tm'=8] {'tm'}, dimensions={0}, use_global_device_ids=true | all-gather | bytes 36864 | tf_op jit(solution)/shard_map/all_gather | solution.py:18
  141.8 1.0 slice_bitcast_fusion
  142.8 0.1 copy.20
  142.9 9.1 %while.19 = (s32[]{:T(128)}, f32[1,8,128]{2,1,0:T(8,128)S(1)}, f32[1,8,128]{2,1,0:T(8,128)S(1)}, f32[1,128,512]{1,2,0:T(8,128)S(1)}, f32[8,1,8,128]{3,2,1,0:T(8,...) while((s32[]{:T(128)}, f32[1,8,128]{2,1,0:T(8,128)S(1)}, ...), condition=%wide.region_5.6_spmd, body=%wide.region_4.5_spmd.sunk | while | flops 203781 | bytes 1896603 | solution.py:23
  143.0 1.0 constant_dynamic-slice_fusion.2
  144.0 0.1 copy.25
  144.1 0.1 fusion.92
  144.3 1.0 constant_dynamic-slice_fusion.2
  145.3 0.1 copy.25
  145.4 0.1 fusion.92
  145.6 1.0 constant_dynamic-slice_fusion.2
  146.6 0.1 copy.25
  146.7 0.1 fusion.92
  146.9 1.0 constant_dynamic-slice_fusion.2
  147.9 0.1 copy.25
  148.0 0.1 fusion.92
  148.2 1.0 constant_dynamic-slice_fusion.2
  149.1 0.1 copy.25
  149.5 1.0 constant_dynamic-slice_fusion.2
  150.4 0.1 copy.25
  150.7 1.0 constant_dynamic-slice_fusion.2
  151.7 0.1 copy.25
  152.1 0.1 fusion.65
  152.2 0.8 fusion.38
  (41 shorter events, 0.7 us)
Async XLA Ops:
  6.5 61.9 %copy-start = (bf16[512,1024]{1,0:T(8,128)(2,1)S(1)}, bf16[512,1024]{1,0:T(8,128)(2,1)}, u32[]{:S(2)}) copy-start(bf16[512,1024]{1,0:T(8,128)(2,1)} %param.15) | copy-start | bytes 3145732
  6.5 135.3 %all-gather.4.cloned.1.call-start = ((), (), s32[]{:S(2)}) async-start(), calls=%async_computation | async-start | bytes 2359296 | tf_op jit(solution)/shard_map/all_gather | solution.py:18
  7.7 16.0 %collective-permute-start = (bf16[1,512,512]{2,1,0:T(8,128)(2,1)S(1)}, bf16[1,512,512]{2,1,0:T(8,128)(2,1)S(1)}, u32[]{:S(2)}, u32[]{:S(2)}) collective-permute-start(bf16[1,512,512]{2,1,0:T(8,128)(2,1)S(1)} %slice.66), channel_id=1, source_target_pairs={{0,1},{1,2},{2,3},{3,4},{4,5},{5,6},{6,7},{8,9},{9,10},{10,11},{11... | collective-permute-start | bytes 1572872 | tf_op jit(solution)/shard_map/ppermute | solution.py:14
  25.4 1.6 %copy-start.2 = (f32[1,1536,512]{2,1,0:T(8,128)}, f32[1,1536,512]{2,1,0:T(8,128)S(1)}, u32[]{:S(2)}) copy-start(f32[1,1536,512]{2,1,0:T(8,128)S(1)} %maximum_convert_fusion.1) | copy-start | bytes 9437188
  27.0 10.2 %copy-start.5 = (bf16[128,512]{1,0:T(8,128)(2,1)S(1)}, bf16[128,512]{1,0:T(8,128)(2,1)}, u32[]{:S(2)}) copy-start(bf16[128,512]{1,0:T(8,128)(2,1)} %param.17) | copy-start | bytes 393220
  32.8 26.2 %collective-permute-start.1 = (bf16[1,1024,512]{2,1,0:T(8,128)(2,1)}, bf16[1,1024,512]{2,1,0:T(8,128)(2,1)S(1)}, u32[]{:S(2)}, u32[]{:S(2)}) collective-permute-start(bf16[1,1024,512]{2,1,0:T(8,128)(2,1)} %fusion.37), channel_id=1, source_target_pairs={{0,1},{1,2},{2,3},{3,4},{4,5},{5,6},{6,7},{8,9},{9,10},{10,11},{11... | collective-permute-start | bytes 3145736 | tf_op jit(solution)/shard_map/ppermute | solution.py:14
  60.8 1.9 %copy-start.3 = (f32[1,2048,512]{2,1,0:T(8,128)}, f32[1,2048,512]{2,1,0:T(8,128)S(1)}, u32[]{:S(2)}) copy-start(f32[1,2048,512]{2,1,0:T(8,128)S(1)} %maximum_convert_fusion) | copy-start | bytes 12582916
  72.0 1.9 %copy-start.1 = (f32[8,1024,128]{2,1,0:T(8,128)}, f32[8,1024,128]{2,1,0:T(8,128)S(1)}, u32[]{:S(2)}) copy-start(f32[8,1024,128]{2,1,0:T(8,128)S(1)} %get-tuple-element.224) | copy-start | bytes 12582916
  142.9 9.3 %copy-start.4 = (bf16[512,512]{1,0:T(8,128)(2,1)S(1)}, bf16[512,512]{1,0:T(8,128)(2,1)}, u32[]{:S(2)}) copy-start(bf16[512,512]{1,0:T(8,128)(2,1)} %param.16) | copy-start | bytes 1572868
Sparse Core Ops, SparseCore 0:
  74.9 52.7 all-gather.3
where the time goes:
time: 161 us; the launch traced here: 160 us
  blocking collectives  64.1 us (40%)
  waiting for transfers between devices  31.2 us (19%)
  matrix products  16.4 us (10%)
  local copies, waits for them, and re-layouts  16.3 us (10%)
  between operations  13.5 us (8%)
  starting transfers between devices  9.32 us (6%)
  other arithmetic  8.57 us (5%)
    all_gather x2, blocking collectives, merged(): gathered = jax.tree.map(lambda a: lax.all_gather(a, axis), part)  64.1 us
    ppermute x2, waiting for transfers between devices, from_behind(): lax.ppermute(value, axis, [(source, source + steps) for source in range(l...  31.2 us
    dot_general x2, matrix products, apply_block(): jnp.dot(inner, down_projection[index], preferred_element_type=jnp.float32)  11.4 us
    ppermute x2, starting transfers between devices, from_behind(): lax.ppermute(value, axis, [(source, source + steps) for source in range(l...  9.32 us
    dynamic_slice x14, local copies, waits for them, and re-layouts, take(): lax.dynamic_index_in_dim(a, source, 0, False)  7.72 us
    unnamed x13, local copies, waits for them, and re-layouts  3.63 us
    convert_element_type x2, other arithmetic, apply_block(): values = extended.astype(jnp.float32)  3.46 us
  transfers between devices with their start and end apart: 3, of which 2 were waited for; matrix products, arithmetic and copies ran while one was open for 3% of the time, Pallas kernels for 0%

commit v1 on v0

v1 whole, which is shorter than its diff:
```python
import functools

import jax
import jax.numpy as jnp
from jax import lax
from jax.experimental import pallas as pl
from jax.experimental.pallas import tpu as pltpu
from jax.sharding import PartitionSpec as P

HEADS = 8
STEP = 256
HALF = STEP // 2
BF16, F32 = jnp.bfloat16, jnp.float32
ANY = pl.BlockSpec(memory_space=pl.ANY)
VMEM = pl.BlockSpec(memory_space=pltpu.VMEM)


def dot(a, b):
    return jnp.dot(a, b, preferred_element_type=F32)


def gelu(u):
    return 0.5 * u * (1.0 + jnp.tanh(0.7978845608028654 * (u + 0.044715 * (u * u * u))))


def mix(src, first, steps, dilation, taps, gain, up, down, factors):
    rows, kept = [], []
    for j in range(steps):
        w1, w2 = factors[j]
        at = [(first + j - k * dilation) * HALF for k in range(3)]
        now = src[at[0] : at[0] + HALF, :].astype(F32)
        conv = taps[0:1, :] * now
        conv = conv + (taps[1:2, :] * w1) * src[at[1] : at[1] + HALF, :].astype(F32)
        conv = conv + (taps[2:3, :] * w2) * src[at[2] : at[2] + HALF, :].astype(F32)
        scale = lax.rsqrt(jnp.mean(conv * conv, axis=-1, keepdims=True) + 1e-05)
        rows.append((conv * scale * gain).astype(BF16))
        kept.append(now)
    inner = gelu(dot(jnp.concatenate(rows, 0), up)).astype(BF16)
    return (jnp.concatenate(kept, 0) + dot(inner, down)).astype(BF16)


def attend(x2, w_kv, queries):
    pairs = dot(x2, w_kv).astype(BF16)
    horizon, width = queries.shape
    low = lax.broadcasted_iota(jnp.int32, (horizon, 128), 1) < 64
    zero = jnp.zeros((horizon, 128), BF16)
    acc, top, total = [], [], []
    for p in range(width // 128):
        lanes = slice(128 * p, 128 * p + 128)
        q = queries[:, lanes] * jnp.asarray(0.125, BF16)
        q2 = jnp.concatenate([jnp.where(low, q, zero), jnp.where(low, zero, q)], 0)
        scores = lax.dot_general(q2, pairs[:, lanes], (((1,), (1,)), ((), ())), preferred_element_type=F32)
        m = jnp.max(scores, axis=-1, keepdims=True)
        e = jnp.exp(scores - m)
        s = jnp.sum(e, axis=-1, keepdims=True)
        c = dot(e.astype(BF16), pairs[:, width + 128 * p : width + 128 * p + 128])
        acc.append(jnp.where(low, c[:horizon], c[horizon:]))
        top.append(jnp.where(low, m[:horizon], m[horizon:]))
        total.append(jnp.where(low, s[:horizon], s[horizon:]))
    return jnp.concatenate(acc, 1), jnp.concatenate(top, 1), jnp.concatenate(total, 1)


def encode(context, lse):
    width = lse.shape[1]
    row = lax.broadcasted_iota(jnp.int32, (width, 128), 0)
    col = lax.broadcasted_iota(jnp.int32, (width, 128), 1)
    stats, rest = jnp.zeros((lse.shape[0], 128), F32), lse
    for piece in range(3):
        part = rest.astype(BF16)
        pick = (row == 64 * (col - 8 * piece)) & (col >= 8 * piece) & (col < 8 * piece + 8)
        stats = stats + dot(part, pick.astype(BF16))
        rest = rest - part.astype(F32)
    return jnp.concatenate([context.astype(BF16), stats.astype(BF16)], 1)


def decode(rows):
    width = rows.shape[1] - 128
    row = lax.broadcasted_iota(jnp.int32, (128, width), 0)
    col = lax.broadcasted_iota(jnp.int32, (128, width), 1)
    spread = ((row % 8 == col // 64) & (row < 24)).astype(BF16)
    return rows[:, :width].astype(F32), dot(rows[:, width:], spread)


def combine(parts):
    top = functools.reduce(jnp.maximum, [l for _, l in parts])
    weights = [jnp.exp(l - top) for _, l in parts]
    total = functools.reduce(jnp.add, weights)
    context = functools.reduce(jnp.add, [w * c for w, (c, _) in zip(weights, parts)])
    return context / total, top + jnp.log(total)


def valid(side):
    here, count = lax.axis_index("tm"), lax.axis_size("tm")
    return jnp.where(here == count - 2 + side, 0.0, 1.0).astype(F32)


def early_kernel(hist, got, near, taps, gains, up, down, w_kv, queries, tail, acc, top, total,
                 x0, x1, up_v, down_v, kv_v, sem):
    side = lax.rem(lax.axis_index("tm"), 2)
    mine = pl.ds(pl.multiple_of(side * HALF, HALF), HALF)
    own_at = side * 7
    copies = [
        pltpu.make_async_copy(up, up_v, sem.at[0]),
        pltpu.make_async_copy(down, down_v, sem.at[1]),
        pltpu.make_async_copy(w_kv, kv_v, sem.at[2]),
        pltpu.make_async_copy(hist.at[:, mine, :], x0.at[pl.ds(own_at, 4)], sem.at[3]),
        pltpu.make_async_copy(got, x0.at[pl.ds(4 - side, 4)], sem.at[4]),
        pltpu.make_async_copy(near, x0.at[pl.ds(8 - 8 * side, 3)], sem.at[5]),
    ]
    for i in (3, 4, 5, 0, 1, 2):
        copies[i].start()
    v = valid(0)
    one = 1.0
    for i in (3, 4, 5):
        copies[i].wait()
    rows0 = x0.reshape(11 * HALF, x0.shape[-1])
    copies[0].wait()
    copies[1].wait()
    for j in range(0, 9, 3):
        factors = [(v, v), (one, v), (one, one)] if j == 6 else [(one, one)] * 3
        x1[j * HALF : (j + 3) * HALF, :] = mix(
            rows0, j + 2, 3, 1, taps[0], gains[0:1, :], up_v[0], down_v[0], factors
        )
    tail[...] = x1[pl.ds(pl.multiple_of(side * (5 * HALF), HALF), 4 * HALF), :]
    x2 = jnp.concatenate([
        mix(x1, 4, 2, 2, taps[1], gains[1:2, :], up_v[1], down_v[1], [(one, one)] * 2),
        mix(x1, 6, 3, 2, taps[1], gains[1:2, :], up_v[1], down_v[1], [(v, v), (v, v), (one, v)]),
    ], 0)
    copies[2].wait()
    acc[...], top[...], total[...] = attend(x2, kv_v[...], queries[...])


def late_kernel(hist, far, tail, acc, top, total, taps, gains, up, down, w_kv, queries, out,
                x0, x1, up_v, down_v, kv_v, sem):
    side = lax.rem(lax.axis_index("tm"), 2)
    mine = pl.ds(pl.multiple_of(side * HALF, HALF), HALF)
    copies = [
        pltpu.make_async_copy(up, up_v, sem.at[0]),
        pltpu.make_async_copy(down, down_v, sem.at[1]),
        pltpu.make_async_copy(w_kv, kv_v, sem.at[2]),
        pltpu.make_async_copy(hist.at[pl.ds(2 * side, 2), mine, :], x0.at[pl.ds(3 - 3 * side, 2)], sem.at[3]),
        pltpu.make_async_copy(far, x0.at[pl.ds(2 * side, 3)], sem.at[4]),
    ]
    for i in (3, 4, 0, 1, 2):
        copies[i].start()
    x1[pl.ds(pl.multiple_of((3 - 3 * side) * HALF, HALF), 4 * HALF), :] = tail[...]
    v = valid(1)
    one = 1.0
    copies[3].wait()
    copies[4].wait()
    rows0 = x0.reshape(5 * HALF, x0.shape[-1])
    copies[0].wait()
    copies[1].wait()
    fresh = mix(rows0, 2, 3, 1, taps[0], gains[0:1, :], up_v[0], down_v[0], [(v, v), (one, v), (one, one)])
    x1[pl.ds(pl.multiple_of(side * (4 * HALF), HALF), 3 * HALF), :] = fresh
    x2 = mix(x1, 4, 3, 2, taps[1], gains[1:2, :], up_v[1], down_v[1], [(v, v), (v, v), (one, v)])
    copies[2].wait()
    acc2, top2, total2 = attend(x2, kv_v[...], queries[...])
    best = jnp.maximum(top[...], top2)
    a, b = jnp.exp(top[...] - best), jnp.exp(top2 - best)
    whole = total[...] * a + total2 * b
    out[...] = encode((acc[...] * a + acc2 * b) / whole, best + jnp.log(whole))


def pair_kernel(mine, theirs, out):
    shape = mine.shape
    flat = (shape[0] * shape[1], shape[2])
    context, lse = combine([decode(mine[...].reshape(flat)), decode(theirs[...].reshape(flat))])
    out[...] = encode(context, lse).reshape(shape)


def final_kernel(count, *refs):
    parts, readout, out = refs[:count], refs[count], refs[count + 1]
    context, _ = combine([decode(part[...]) for part in parts])
    out[...] = dot(context.astype(BF16), readout[...]).astype(BF16)


def on_device(history, taps, gains, up, down, w_kv, readout, queries):
    _, span, width = history.shape
    horizon, hidden = queries.shape[0], up.shape[-1]
    count = lax.axis_size("tm")
    here = lax.axis_index("tm")
    side, pair = lax.rem(here, 2), lax.div(here, 2)
    n_pairs = count // 2
    share = horizon // count

    hist = history.reshape(span // STEP, STEP, width)
    other = (1 - side) * HALF
    swap = [(i, i ^ 1) for i in range(count)]
    ahead = [(2 * p + 1, 2 * p + 2) for p in range(n_pairs - 1)]
    behind = [(2 * p, (2 * p - 2) % count) for p in range(n_pairs)]
    near_pairs = [(s, t + 1) for s, t in ahead] + behind
    far_pairs = ahead + [(s, t + 1) for s, t in behind]
    zero = jnp.zeros_like(side)
    out_swap = lax.dynamic_slice(hist, (zero, other, zero), (4, HALF, width))
    got = lax.ppermute(out_swap, "tm", swap)
    near = lax.ppermute(
        lax.dynamic_slice(hist, (side, side * HALF, zero), (3, HALF, width)), "tm", near_pairs
    )
    far_out = lax.dynamic_slice(hist, (side, other, zero), (3, HALF, width))
    far_out, got = lax.optimization_barrier((far_out, got))
    far = lax.ppermute(far_out, "tm", far_pairs)

    state = jax.ShapeDtypeStruct((horizon, width), F32)
    weights = [
        pltpu.VMEM(up.shape, BF16), pltpu.VMEM(down.shape, BF16), pltpu.VMEM(w_kv.shape, BF16),
        pltpu.SemaphoreType.DMA((6,)),
    ]
    per_row = 4 * width * hidden
    tail, acc, top, total = pl.pallas_call(
        early_kernel,
        out_shape=[jax.ShapeDtypeStruct((4 * HALF, width), BF16), state, state, state],
        in_specs=[ANY] * 3 + [VMEM] * 2 + [ANY] * 3 + [VMEM],
        out_specs=[VMEM] * 4,
        scratch_shapes=[pltpu.VMEM((11, HALF, width), BF16), pltpu.VMEM((9 * HALF, width), BF16)] + weights,
        compiler_params=pltpu.CompilerParams(vmem_limit_bytes=40 * 1024 * 1024),
        cost_estimate=pl.CostEstimate(
            flops=(14 * per_row + 5 * 2 * per_row) * HALF, bytes_accessed=8 << 20, transcendentals=2 << 20
        ),
        name="early",
    )(hist, got, near, taps, gains, up, down, w_kv, queries)
    payload = pl.pallas_call(
        late_kernel,
        out_shape=jax.ShapeDtypeStruct((horizon, width + 128), BF16),
        in_specs=[ANY] * 2 + [VMEM] * 6 + [ANY] * 3 + [VMEM],
        out_specs=VMEM,
        scratch_shapes=[pltpu.VMEM((5, HALF, width), BF16), pltpu.VMEM((7 * HALF, width), BF16)] + weights,
        compiler_params=pltpu.CompilerParams(vmem_limit_bytes=40 * 1024 * 1024),
        cost_estimate=pl.CostEstimate(
            flops=(6 * per_row + 3 * 2 * per_row) * HALF, bytes_accessed=8 << 20, transcendentals=1 << 20
        ),
        name="late",
    )(hist, far, tail, acc, top, total, taps, gains, up, down, w_kv, queries)

    lanes = payload.shape[-1]
    split = payload.reshape(n_pairs, 2, share, lanes)
    theirs = lax.ppermute(lax.dynamic_index_in_dim(split, 1 - side, 1, False), "tm", swap)
    merged = pl.pallas_call(
        pair_kernel,
        out_shape=jax.ShapeDtypeStruct((n_pairs, share, lanes), BF16),
        in_specs=[VMEM] * 2,
        out_specs=VMEM,
        name="pair",
    )(lax.dynamic_index_in_dim(split, side, 1, False), theirs)
    if n_pairs <= 4 and n_pairs & (n_pairs - 1) == 0:
        parts = [lax.dynamic_index_in_dim(merged, pair, 0, False)]
        for s in range(1, n_pairs):
            block = lax.dynamic_index_in_dim(merged, pair ^ s, 0, False)
            parts.append(lax.ppermute(block, "tm", [(i, i ^ (2 * s)) for i in range(count)]))
    else:
        groups = [[2 * p + s for p in range(n_pairs)] for s in range(2)]
        swapped = lax.all_to_all(merged, "tm", 0, 0, axis_index_groups=groups, tiled=True)
        parts = [swapped[p] for p in range(n_pairs)]
    result = pl.pallas_call(
        functools.partial(final_kernel, len(parts)),
        out_shape=jax.ShapeDtypeStruct((share, width), BF16),
        in_specs=[VMEM] * (len(parts) + 1),
        out_specs=VMEM,
        name="final",
    )(*parts, readout)
    return result[None]


def solution(mesh):
    placed = (P(("groups", "series"), "tm", None), P(), P(), P(), P(), P(), P(), P())
    return jax.shard_map(
        on_device,
        mesh=mesh,
        in_specs=placed,
        out_specs=P(("groups", "series"), "tm", None),
        check_vma=False,
    )
```

time: 161 us -> 60.8 us (0.38)
  blocking collectives: 64.1 us -> 0 us
  waiting for transfers between devices: 31.2 us -> 12 us
  Pallas kernels: 0 us -> 18.1 us
  matrix products: 16.4 us -> 0 us
  between operations: 13.5 us -> 0.16 us
  starting transfers between devices: 9.32 us -> 19.5 us
  other arithmetic: 8.57 us -> 0 us
  local copies, waits for them, and re-layouts: 16.3 us -> 10.6 us
    all_gather x2 -> x0, blocking collectives: 64.1 us -> none  [merged(): gathered = jax.tree.map(lambda a: lax.all_gather(a, axis), part)]
    ppermute x2 -> x7, waiting for transfers between devices: 31.2 us -> 12 us  [the longest x1 4.49 us: on_device(): got = lax.ppermute(out_swap, 'tm', swap)]
    pallas_call x0 -> x4, Pallas kernels: none -> 18.1 us  [the longest x1 8.57 us: on_device(): pl.pallas_call(early_kernel, out_shape=[jax.ShapeDtypeStruct((4 * HALF, w...]
    dot_general x6 -> x0, matrix products: 16.4 us -> none  [the longest x2 11.4 us: apply_block(): jnp.dot(inner, down_projection[index], preferred_element_type=jnp.float32)]
    ppermute x2 -> x7, starting transfers between devices: 9.32 us -> 19.5 us  [the longest x1 6.7 us: on_device(): far = lax.ppermute(far_out, 'tm', far_pairs)]
    reduce_sum x3 -> x0, other arithmetic: 4.04 us -> none  [the longest x1 2.9 us: on_device(): total = jnp.sum(expo, axis=-1)]
    convert_element_type x3 -> x0, other arithmetic: 3.6 us -> none  [the longest x2 3.46 us: apply_block(): values = extended.astype(jnp.float32)]
    dynamic_slice x14 -> x2, local copies, waits for them, and re-layouts: 7.72 us -> 4.14 us  [the longest x1 2.1 us: on_device(): lax.dynamic_slice(hist, (side, side * HALF, zero), (3, HALF, width))]
  transfers between devices with their start and end apart: 3 -> 7, of which waited for: 2 -> 4; matrix products, arithmetic and copies ran while one was open for 3% -> 3% of each run, Pallas kernels for 0% -> 14%
where the time goes in v1:
time: 60.8 us; the launch traced here: 60.4 us
  starting transfers between devices  19.5 us (32%)
  Pallas kernels  18.1 us (30%)
  waiting for transfers between devices  12 us (20%)
  local copies, waits for them, and re-layouts  10.6 us (17%)
    pallas_call x1, Pallas kernels, on_device(): pl.pallas_call(early_kernel, out_shape=[jax.ShapeDtypeStruct((4 * HALF, w...  8.57 us
    ppermute x1, starting transfers between devices, on_device(): far = lax.ppermute(far_out, 'tm', far_pairs)  6.7 us
    ppermute x1, starting transfers between devices, on_device(): lax.ppermute(lax.dynamic_slice(hist, (side, side * HALF, zero), (3, HALF,...  5.5 us
    pallas_call x1, Pallas kernels, on_device(): pl.pallas_call(late_kernel, out_shape=jax.ShapeDtypeStruct((horizon, widt...  5.46 us
    ppermute x1, waiting for transfers between devices, on_device(): got = lax.ppermute(out_swap, 'tm', swap)  4.49 us
    unnamed x27, local copies, waits for them, and re-layouts  4.44 us
    ppermute x1, waiting for transfers between devices, on_device(): lax.ppermute(lax.dynamic_index_in_dim(split, 1 - side, 1, False), 'tm', s...  4.44 us
    ppermute x3, starting transfers between devices, on_device(): lax.ppermute(block, 'tm', [(i, i ^ 2 * s) for i in range(count)])  4.39 us
  transfers between devices with their start and end apart: 7, of which 4 were waited for; matrix products, arithmetic and copies ran while one was open for 3% of the time, Pallas kernels for 14%

profile of v1, /device:TPU:0, one launch (start us, length us, event | category | flops | bytes accessed | tf_op | source)
XLA Modules:
  0.0 60.4 jit_solution(14661133249113970625)
XLA Ops:
  0.0 0.0 copy-start
  0.0 0.0 copy-start.12
  0.0 0.0 copy-start.7
  0.0 0.0 copy-start.5
  0.0 0.0 copy-start.6
  0.0 2.0 %constant_dynamic-slice_fusion.1 = bf16[4,128,512]{2,1,0:T(8,128)(2,1)} fusion(bf16[4,256,512]{2,1,0:T(8,128)(2,1)} %bitcast.19, s32[]{:T(128)S(6)} %select_n.32), kind=kLoop, calls=%fused_computation.7 | loop fusion | bytes 1048580 | tf_op jit(solution)/shard_map/dynamic_slice | solution.py:195
  2.1 3.0 %collective-permute-start = (bf16[4,128,512]{2,1,0:T(8,128)(2,1)}, bf16[4,128,512]{2,1,0:T(8,128)(2,1)S(1)}, u32[]{:S(2)}, u32[]{:S(2)}) collective-permute-start(bf16[4,128,512]{2,1,0:T(8,128)(2,1)} %constant_dynamic-slice_fusion.1), channel_id=1, source_target_pairs={{0,1},{1,0},{2,3},{3,2},{4,5},{5,4},{6,7},{7,6},{8,9},{9,8},{10,11... | collective-permute-start | bytes 1572872 | tf_op jit(solution)/shard_map/ppermute | solution.py:196
  5.0 2.1 %constant_dynamic-slice_fusion = (bf16[3,128,512]{2,1,0:T(8,128)(2,1)}, bf16[3,128,512]{2,1,0:T(8,128)(2,1)}) fusion(bf16[4,256,512]{2,1,0:T(8,128)(2,1)} %bitcast.20, s32[]{:T(128)S(6)} %select_n.31, s32[]{:T(128)S(6)} %select_n.33, s32[]{:T(128)S(6)} %select_n.32), kind=kLoop, calls=%fused_computation.6 | loop fusion | bytes 1572876 | tf_op jit(solution)/shard_map/dynamic_slice | solution.py:198
  7.1 5.5 %collective-permute-start.2 = (bf16[3,128,512]{2,1,0:T(8,128)(2,1)}, bf16[3,128,512]{2,1,0:T(8,128)(2,1)S(1)}, u32[]{:S(2)}, u32[]{:S(2)}) collective-permute-start(bf16[3,128,512]{2,1,0:T(8,128)(2,1)} %get-tuple-element.17), channel_id=1, source_target_pairs={{1,3},{3,5},{5,7},{0,6},{2,0},{4,2},{6,4},{9,11},{11,13},{13,15},{... | collective-permute-start | bytes 1179656 | tf_op jit(solution)/shard_map/ppermute | solution.py:197
  12.6 0.0 copy-done.12
  12.7 4.5 %collective-permute-done.got = bf16[4,128,512]{2,1,0:T(8,128)(2,1)S(1)} collective-permute-done((bf16[4,128,512]{2,1,0:T(8,128)(2,1)}, bf16[4,128,512]{2,1,0:T(8,128)(2,1)S(1)}, u32[]{:S(2)}, u32[]{:S(2)}) %collective-permute-start) | collective-permute-done | bytes 524320 | tf_op jit(solution)/shard_map/ppermute | solution.py:196
  17.1 6.7 %collective-permute-start.1 = (bf16[3,128,512]{2,1,0:T(8,128)(2,1)}, bf16[3,128,512]{2,1,0:T(8,128)(2,1)S(1)}, u32[]{:S(2)}, u32[]{:S(2)}) collective-permute-start(bf16[3,128,512]{2,1,0:T(8,128)(2,1)} %get-tuple-element.11), channel_id=1, source_target_pairs={{1,2},{3,4},{5,6},{0,7},{2,1},{4,3},{6,5},{9,10},{11,12},{13,14},{... | collective-permute-start | bytes 1179656 | tf_op jit(solution)/shard_map/ppermute | solution.py:202
  23.8 0.0 collective-permute-done.2.near
  23.9 0.0 copy-done
  23.9 0.0 copy-done.7
  23.9 0.0 copy-done.5
  23.9 0.0 copy-done.6
  23.9 0.0 copy-start.1
  23.9 1.6 %copy-done.1 = bf16[2,512,1024]{2,1,0:T(8,128)(2,1)S(1)} copy-done((bf16[2,512,1024]{2,1,0:T(8,128)(2,1)S(1)}, bf16[2,512,1024]{2,1,0:T(8,128)(2,1)}, u32[]{:S(2)}) %copy-start.1) | copy-done | bytes 2097176
  25.5 0.0 copy-start.3
  25.5 1.6 %copy-done.3 = bf16[2,1024,512]{2,1,0:T(8,128)(2,1)S(1)} copy-done((bf16[2,1024,512]{2,1,0:T(8,128)(2,1)S(1)}, bf16[2,1024,512]{2,1,0:T(8,128)(2,1)}, u32[]{:S(2)}) %copy-start.3) | copy-done | bytes 2097176
  27.1 0.0 copy-start.2
  27.1 0.0 copy-start.4
  27.1 8.6 %early.1 = (bf16[512,512]{1,0:T(8,128)(2,1)S(1)}, f32[128,512]{1,0:T(8,128)S(1)}, f32[128,512]{1,0:T(8,128)S(1)}, f32[128,512]{1,0:T(8,128)S(1)}) custom-call(bf16[4,256,512]{2,1,0:T(8,128)(2,1)S(1)} %bitcast.21, bf16[4,128,512]{2,1,0:T(8,128)(2,1)S(1)} %collective-permute-done.got, bf16[3,128,512]{2,1,0:T(8,128)(2,1)S(1)} %collective-permute-done.2.near, ...), custom_call_target="tpu_custom_call" | custom-call | flops 6442450944 | bytes 8388608 | tf_op jit(solution)/shard_map/early/pallas_call | solution.py:210
  35.7 0.0 collective-permute-done.1.far
  35.7 0.0 copy-done.2
  35.7 0.0 copy-done.4
  35.7 5.5 %late.1 = bf16[128,640]{1,0:T(8,128)(2,1)S(1)} custom-call(bf16[4,256,512]{2,1,0:T(8,128)(2,1)S(1)} %bitcast.22, bf16[3,128,512]{2,1,0:T(8,128)(2,1)S(1)} %collective-permute-done.1.far, bf16[512,512]{1,0:T(8,128)(2,1)S(1)} %get-tuple-element.13.tail, f32[128,512]{1,0:T(8,128)S(1)} %get-tuple-element.14.acc, f32[128,512]{1,0:T(8,128)S(1)} %get-tuple-element.15.top, ...), custom_call_target="tpu_custom_call" | custom-call | flops 3221225472 | bytes 8388608 | tf_op jit(solution)/shard_map/late/pallas_call | solution.py:222
  41.2 0.7 %dynamic-slice_bitcast_fusion = (bf16[4,16,640]{2,1,0:T(8,128)(2,1)S(1)}, bf16[4,16,640]{2,1,0:T(8,128)(2,1)}) fusion(bf16[4,2,16,640]{3,2,1,0:T(8,128)(2,1)S(1)} %bitcast.23, s32[]{:T(128)S(6)} %select_n.35, s32[]{:T(128)S(6)} %select_n.34), kind=kLoop, calls=%fused_computation | loop fusion | bytes 327688 | tf_op jit(solution)/shard_map/jit(dynamic_index_in_dim)/squeeze | solution.py:237
  41.8 0.0 collective-permute-start.3
  41.8 4.4 %collective-permute-done.3.theirs = bf16[4,16,640]{2,1,0:T(8,128)(2,1)S(1)} collective-permute-done((bf16[4,16,640]{2,1,0:T(8,128)(2,1)S(1)}, bf16[4,16,640]{2,1,0:T(8,128)(2,1)S(1)}, u32[]{:S(2)}, u32[]{:S(2)}) %collective-permute-start.3) | collective-permute-done | bytes 81952 | tf_op jit(solution)/shard_map/ppermute | solution.py:237
  46.3 0.0 copy-start.8
  46.3 0.6 %copy-done.8 = bf16[4,16,640]{2,1,0:T(8,128)(2,1)} copy-done((bf16[4,16,640]{2,1,0:T(8,128)(2,1)}, bf16[4,16,640]{2,1,0:T(8,128)(2,1)S(1)}, u32[]{:S(2)}) %copy-start.8) | copy-done | bytes 81944
  46.9 2.0 %pair.1 = bf16[4,16,640]{2,1,0:T(8,128)(2,1)} custom-call(bf16[4,16,640]{2,1,0:T(8,128)(2,1)} %get-tuple-element.20.mine, bf16[4,16,640]{2,1,0:T(8,128)(2,1)} %copy-done.8), custom_call_target="tpu_custom_call" | custom-call | tf_op jit(solution)/shard_map/pair/pallas_call | solution.py:238
  48.9 1.4 %dynamic-slice_bitcast_fusion.2 = (bf16[16,640]{1,0:T(8,128)(2,1)S(1)}, bf16[16,640]{1,0:T(8,128)(2,1)S(1)}, bf16[16,640]{1,0:T(8,128)(2,1)S(1)}, bf16[16,640]{1,0:T(8,128)(2,1)}) fusion(bf16[4,16,640]{2,1,0:T(8,128)(2,1)} %pair.1, s32[]{:T(128)S(6)} %select_n.39, s32[]{:T(128)S(6)} %select_n.38, s32[]{:T(128)S(6)} %select_n.37, s32[]{:T(128)S(6)} %select_n.36), kind=kLoop, calls=%fused_computation.2 | loop fusion | bytes 163856 | tf_op jit(solution)/shard_map/jit(dynamic_index_in_dim)/squeeze | solution.py:248
  50.3 0.0 collective-permute-start.4
  50.3 1.9 %collective-permute-start.5 = (bf16[16,640]{1,0:T(8,128)(2,1)S(1)}, bf16[16,640]{1,0:T(8,128)(2,1)S(1)}, u32[]{:S(2)}, u32[]{:S(2)}) collective-permute-start(bf16[16,640]{1,0:T(8,128)(2,1)S(1)} %get-tuple-element.22), channel_id=1, source_target_pairs={{0,4},{1,5},{2,6},{3,7},{4,0},{5,1},{6,2},{7,3},{8,12},{9,13},{10,... | collective-permute-start | bytes 61448 | tf_op jit(solution)/shard_map/ppermute | solution.py:249
  52.2 2.5 %collective-permute-start.6 = (bf16[16,640]{1,0:T(8,128)(2,1)S(1)}, bf16[16,640]{1,0:T(8,128)(2,1)S(1)}, u32[]{:S(2)}, u32[]{:S(2)}) collective-permute-start(bf16[16,640]{1,0:T(8,128)(2,1)S(1)} %get-tuple-element.21), channel_id=1, source_target_pairs={{0,6},{1,7},{2,4},{3,5},{4,2},{5,3},{6,0},{7,1},{8,14},{9,15},{10,... | collective-permute-start | bytes 61448 | tf_op jit(solution)/shard_map/ppermute | solution.py:249
  54.7 0.0 collective-permute-done.4.refs_1_
  54.7 0.0 copy-start.9
  54.7 0.3 collective-permute-done.5.refs_2_
  55.0 0.0 copy-start.10
  55.0 2.8 %collective-permute-done.6.refs_3_ = bf16[16,640]{1,0:T(8,128)(2,1)S(1)} collective-permute-done((bf16[16,640]{1,0:T(8,128)(2,1)S(1)}, bf16[16,640]{1,0:T(8,128)(2,1)S(1)}, u32[]{:S(2)}, u32[]{:S(2)}) %collective-permute-start.6) | collective-permute-done | bytes 20512 | tf_op jit(solution)/shard_map/ppermute | solution.py:249
  57.8 0.0 copy-start.11
  57.8 0.0 copy-done.9
  57.8 0.0 copy-done.10
  57.8 0.6 copy-done.11
  58.4 2.0 %final.1 = bf16[16,512]{1,0:T(8,128)(2,1)} custom-call(bf16[16,640]{1,0:T(8,128)(2,1)} %get-tuple-element.24.refs_0_, bf16[16,640]{1,0:T(8,128)(2,1)} %copy-done.9, bf16[16,640]{1,0:T(8,128)(2,1)} %copy-done.10, bf16[16,640]{1,0:T(8,128)(2,1)} %copy-done.11, bf16[512,512]{1,0:T(8,128)(2,1)} %refs_4_.1), custom_call_target="tpu_custom_call" | custom-call | tf_op jit(solution)/shard_map/final/pallas_call | solution.py:254
  (1 shorter events, 0.0 us)
Async XLA Ops:
  0.0 23.9 %copy-start = (bf16[1,1024,512]{2,1,0:T(8,128)(2,1)S(1)}, bf16[1,1024,512]{2,1,0:T(8,128)(2,1)}, u32[]{:S(2)}) copy-start(bf16[1,1024,512]{2,1,0:T(8,128)(2,1)} %param.8) | copy-start | bytes 3145732
  0.0 12.6 %copy-start.12 = (f32[2,3,512]{2,0,1:T(2,128)S(1)}, f32[2,3,512]{2,0,1:T(2,128)}, u32[]{:S(2)}) copy-start(f32[2,3,512]{2,0,1:T(2,128)} %param.9) | copy-start | bytes 36868
  0.0 23.9 %copy-start.7 = (f32[2,512]{1,0:T(2,128)S(1)}, f32[2,512]{1,0:T(2,128)}, u32[]{:S(2)}) copy-start(f32[2,512]{1,0:T(2,128)} %gains.3) | copy-start | bytes 12292
  0.0 23.9 %copy-start.5 = (bf16[512,1024]{1,0:T(8,128)(2,1)S(1)}, bf16[512,1024]{1,0:T(8,128)(2,1)}, u32[]{:S(2)}) copy-start(bf16[512,1024]{1,0:T(8,128)(2,1)} %w_kv.3) | copy-start | bytes 3145732
  0.0 23.9 %copy-start.6 = (bf16[128,512]{1,0:T(8,128)(2,1)S(1)}, bf16[128,512]{1,0:T(8,128)(2,1)}, u32[]{:S(2)}) copy-start(bf16[128,512]{1,0:T(8,128)(2,1)} %queries.3) | copy-start | bytes 393220
  2.1 15.1 %collective-permute-start = (bf16[4,128,512]{2,1,0:T(8,128)(2,1)}, bf16[4,128,512]{2,1,0:T(8,128)(2,1)S(1)}, u32[]{:S(2)}, u32[]{:S(2)}) collective-permute-start(bf16[4,128,512]{2,1,0:T(8,128)(2,1)} %constant_dynamic-slice_fusion.1), channel_id=1, source_target_pairs={{0,1},{1,0},{2,3},{3,2},{4,5},{5,4},{6,7},{7,6},{8,9},{9,8},{10,11... | collective-permute-start | bytes 1572872 | tf_op jit(solution)/shard_map/ppermute | solution.py:196
  7.1 16.7 %collective-permute-start.2 = (bf16[3,128,512]{2,1,0:T(8,128)(2,1)}, bf16[3,128,512]{2,1,0:T(8,128)(2,1)S(1)}, u32[]{:S(2)}, u32[]{:S(2)}) collective-permute-start(bf16[3,128,512]{2,1,0:T(8,128)(2,1)} %get-tuple-element.17), channel_id=1, source_target_pairs={{1,3},{3,5},{5,7},{0,6},{2,0},{4,2},{6,4},{9,11},{11,13},{13,15},{... | collective-permute-start | bytes 1179656 | tf_op jit(solution)/shard_map/ppermute | solution.py:197
  17.1 18.5 %collective-permute-start.1 = (bf16[3,128,512]{2,1,0:T(8,128)(2,1)}, bf16[3,128,512]{2,1,0:T(8,128)(2,1)S(1)}, u32[]{:S(2)}, u32[]{:S(2)}) collective-permute-start(bf16[3,128,512]{2,1,0:T(8,128)(2,1)} %get-tuple-element.11), channel_id=1, source_target_pairs={{1,2},{3,4},{5,6},{0,7},{2,1},{4,3},{6,5},{9,10},{11,12},{13,14},{... | collective-permute-start | bytes 1179656 | tf_op jit(solution)/shard_map/ppermute | solution.py:202
  23.9 1.6 %copy-start.1 = (bf16[2,512,1024]{2,1,0:T(8,128)(2,1)S(1)}, bf16[2,512,1024]{2,1,0:T(8,128)(2,1)}, u32[]{:S(2)}) copy-start(bf16[2,512,1024]{2,1,0:T(8,128)(2,1)} %up.3) | copy-start | bytes 6291460
  25.5 1.6 %copy-start.3 = (bf16[2,1024,512]{2,1,0:T(8,128)(2,1)S(1)}, bf16[2,1024,512]{2,1,0:T(8,128)(2,1)}, u32[]{:S(2)}) copy-start(bf16[2,1024,512]{2,1,0:T(8,128)(2,1)} %down.3) | copy-start | bytes 6291460
  27.1 8.6 %copy-start.2 = (bf16[2,512,1024]{2,1,0:T(8,128)(2,1)S(1)}, bf16[2,512,1024]{2,1,0:T(8,128)(2,1)}, u32[]{:S(2)}) copy-start(bf16[2,512,1024]{2,1,0:T(8,128)(2,1)} %up.3) | copy-start | bytes 6291460
  27.1 8.6 %copy-start.4 = (bf16[2,1024,512]{2,1,0:T(8,128)(2,1)S(1)}, bf16[2,1024,512]{2,1,0:T(8,128)(2,1)}, u32[]{:S(2)}) copy-start(bf16[2,1024,512]{2,1,0:T(8,128)(2,1)} %down.3) | copy-start | bytes 6291460
  41.8 4.4 %collective-permute-start.3 = (bf16[4,16,640]{2,1,0:T(8,128)(2,1)S(1)}, bf16[4,16,640]{2,1,0:T(8,128)(2,1)S(1)}, u32[]{:S(2)}, u32[]{:S(2)}) collective-permute-start(bf16[4,16,640]{2,1,0:T(8,128)(2,1)S(1)} %get-tuple-element.19), channel_id=1, source_target_pairs={{0,1},{1,0},{2,3},{3,2},{4,5},{5,4},{6,7},{7,6},{8,9},{9,8},{10,11... | collective-permute-start | bytes 245768 | tf_op jit(solution)/shard_map/ppermute | solution.py:237
  46.3 0.6 %copy-start.8 = (bf16[4,16,640]{2,1,0:T(8,128)(2,1)}, bf16[4,16,640]{2,1,0:T(8,128)(2,1)S(1)}, u32[]{:S(2)}) copy-start(bf16[4,16,640]{2,1,0:T(8,128)(2,1)S(1)} %collective-permute-done.3.theirs) | copy-start | bytes 245764
  50.3 4.4 %collective-permute-start.4 = (bf16[16,640]{1,0:T(8,128)(2,1)S(1)}, bf16[16,640]{1,0:T(8,128)(2,1)S(1)}, u32[]{:S(2)}, u32[]{:S(2)}) collective-permute-start(bf16[16,640]{1,0:T(8,128)(2,1)S(1)} %get-tuple-element.23), channel_id=1, source_target_pairs={{0,2},{1,3},{2,0},{3,1},{4,6},{5,7},{6,4},{7,5},{8,10},{9,11},{10,... | collective-permute-start | bytes 61448 | tf_op jit(solution)/shard_map/ppermute | solution.py:249
  50.3 4.7 %collective-permute-start.5 = (bf16[16,640]{1,0:T(8,128)(2,1)S(1)}, bf16[16,640]{1,0:T(8,128)(2,1)S(1)}, u32[]{:S(2)}, u32[]{:S(2)}) collective-permute-start(bf16[16,640]{1,0:T(8,128)(2,1)S(1)} %get-tuple-element.22), channel_id=1, source_target_pairs={{0,4},{1,5},{2,6},{3,7},{4,0},{5,1},{6,2},{7,3},{8,12},{9,13},{10,... | collective-permute-start | bytes 61448 | tf_op jit(solution)/shard_map/ppermute | solution.py:249
  52.2 5.6 %collective-permute-start.6 = (bf16[16,640]{1,0:T(8,128)(2,1)S(1)}, bf16[16,640]{1,0:T(8,128)(2,1)S(1)}, u32[]{:S(2)}, u32[]{:S(2)}) collective-permute-start(bf16[16,640]{1,0:T(8,128)(2,1)S(1)} %get-tuple-element.21), channel_id=1, source_target_pairs={{0,6},{1,7},{2,4},{3,5},{4,2},{5,3},{6,0},{7,1},{8,14},{9,15},{10,... | collective-permute-start | bytes 61448 | tf_op jit(solution)/shard_map/ppermute | solution.py:249
  54.7 3.1 %copy-start.9 = (bf16[16,640]{1,0:T(8,128)(2,1)}, bf16[16,640]{1,0:T(8,128)(2,1)S(1)}, u32[]{:S(2)}) copy-start(bf16[16,640]{1,0:T(8,128)(2,1)S(1)} %collective-permute-done.4.refs_1_) | copy-start | bytes 61444
  55.0 2.8 %copy-start.10 = (bf16[16,640]{1,0:T(8,128)(2,1)}, bf16[16,640]{1,0:T(8,128)(2,1)S(1)}, u32[]{:S(2)}) copy-start(bf16[16,640]{1,0:T(8,128)(2,1)S(1)} %collective-permute-done.5.refs_2_) | copy-start | bytes 61444
  57.8 0.6 %copy-start.11 = (bf16[16,640]{1,0:T(8,128)(2,1)}, bf16[16,640]{1,0:T(8,128)(2,1)S(1)}, u32[]{:S(2)}) copy-start(bf16[16,640]{1,0:T(8,128)(2,1)S(1)} %collective-permute-done.6.refs_3_) | copy-start | bytes 61444

commit v2 on v1

v2 whole, which is shorter than its diff:
```python
import functools

import jax
import jax.numpy as jnp
from jax import lax
from jax.experimental import pallas as pl
from jax.experimental.pallas import tpu as pltpu
from jax.sharding import PartitionSpec as P

HEADS = 8
STEP = 256
HALF = STEP // 2
BF16, F32 = jnp.bfloat16, jnp.float32
ANY = pl.BlockSpec(memory_space=pl.ANY)
VMEM = pl.BlockSpec(memory_space=pltpu.VMEM)
HBM = pl.BlockSpec(memory_space=pltpu.HBM)


def dot(a, b):
    return jnp.dot(a, b, preferred_element_type=F32)


def gelu(u):
    return 0.5 * u * (1.0 + jnp.tanh(0.7978845608028654 * (u + 0.044715 * (u * u * u))))


def mix(src, first, steps, dilation, taps, gain, up, down, factors):
    rows, kept = [], []
    for j in range(steps):
        w1, w2 = factors[j]
        at = [(first + j - k * dilation) * HALF for k in range(3)]
        now = src[at[0] : at[0] + HALF, :].astype(F32)
        conv = taps[0:1, :] * now
        conv = conv + (taps[1:2, :] * w1) * src[at[1] : at[1] + HALF, :].astype(F32)
        conv = conv + (taps[2:3, :] * w2) * src[at[2] : at[2] + HALF, :].astype(F32)
        scale = lax.rsqrt(jnp.mean(conv * conv, axis=-1, keepdims=True) + 1e-05)
        rows.append((conv * scale * gain).astype(BF16))
        kept.append(now)
    inner = gelu(dot(jnp.concatenate(rows, 0), up)).astype(BF16)
    return (jnp.concatenate(kept, 0) + dot(inner, down)).astype(BF16)


def attend(x2, w_kv, queries):
    pairs = dot(x2, w_kv).astype(BF16)
    horizon, width = queries.shape
    low = lax.broadcasted_iota(jnp.int32, (horizon, 128), 1) < 64
    zero = jnp.zeros((horizon, 128), BF16)
    acc, top, total = [], [], []
    for p in range(width // 128):
        lanes = slice(128 * p, 128 * p + 128)
        q = queries[:, lanes] * jnp.asarray(0.125, BF16)
        q2 = jnp.concatenate([jnp.where(low, q, zero), jnp.where(low, zero, q)], 0)
        scores = lax.dot_general(q2, pairs[:, lanes], (((1,), (1,)), ((), ())), preferred_element_type=F32)
        m = jnp.max(scores, axis=-1, keepdims=True)
        e = jnp.exp(scores - m)
        s = jnp.sum(e, axis=-1, keepdims=True)
        c = dot(e.astype(BF16), pairs[:, width + 128 * p : width + 128 * p + 128])
        acc.append(jnp.where(low, c[:horizon], c[horizon:]))
        top.append(jnp.where(low, m[:horizon], m[horizon:]))
        total.append(jnp.where(low, s[:horizon], s[horizon:]))
    return jnp.concatenate(acc, 1), jnp.concatenate(top, 1), jnp.concatenate(total, 1)


def encode(context, lse):
    lane = lax.broadcasted_iota(jnp.int32, (lse.shape[0], 128), 1) & 63
    stats = jnp.zeros((lse.shape[0], 128), F32)
    for p in range(lse.shape[1] // 128):
        rest = lse[:, 128 * p : 128 * p + 128]
        for piece in range(3):
            part = rest.astype(BF16).astype(F32)
            stats = jnp.where(lane == 3 * p + piece, part, stats)
            rest = rest - part
    return jnp.concatenate([context.astype(BF16), stats.astype(BF16)], 1)


def spread_matrix(width):
    row = lax.broadcasted_iota(jnp.int32, (128, width), 0)
    col = lax.broadcasted_iota(jnp.int32, (128, width), 1)
    piece = (row & 63) - 3 * (col >> 7)
    return jnp.where((piece >= 0) & (piece < 3) & ((row >> 6) == ((col >> 6) & 1)), 1.0, 0.0).astype(BF16)


def decode(rows, spread):
    width = rows.shape[1] - 128
    return rows[:, :width].astype(F32), dot(rows[:, width:], spread)


def combine(parts):
    top = functools.reduce(jnp.maximum, [l for _, l in parts])
    weights = [jnp.exp(l - top) for _, l in parts]
    total = functools.reduce(jnp.add, weights)
    context = functools.reduce(jnp.add, [w * c for w, (c, _) in zip(weights, parts)])
    return context / total, top + jnp.log(total)


def valid(side):
    here, count = lax.axis_index("tm"), lax.axis_size("tm")
    return jnp.where(here == count - 2 + side, 0.0, 1.0).astype(F32)


def early_kernel(own, got, near, taps, gains, up_v, down_v, kv_v, queries, tail, acc, top, total,
                 x0, x1, sem):
    side = lax.rem(lax.axis_index("tm"), 2)
    copies = [
        pltpu.make_async_copy(own, x0.at[pl.ds(side * 7, 4)], sem.at[0]),
        pltpu.make_async_copy(got, x0.at[pl.ds(4 - side, 4)], sem.at[1]),
        pltpu.make_async_copy(near, x0.at[pl.ds(8 - 8 * side, 3)], sem.at[2]),
    ]
    for copy in copies:
        copy.start()
    v = valid(0)
    one = 1.0
    for copy in copies:
        copy.wait()
    rows0 = x0.reshape(11 * HALF, x0.shape[-1])
    for j in range(0, 9, 3):
        factors = [(v, v), (one, v), (one, one)] if j == 6 else [(one, one)] * 3
        x1[j * HALF : (j + 3) * HALF, :] = mix(
            rows0, j + 2, 3, 1, taps[0], gains[0:1, :], up_v[0], down_v[0], factors
        )
    tail[...] = x1[pl.ds(pl.multiple_of(side * (5 * HALF), HALF), 4 * HALF), :]
    x2 = jnp.concatenate([
        mix(x1, 4, 2, 2, taps[1], gains[1:2, :], up_v[1], down_v[1], [(one, one)] * 2),
        mix(x1, 6, 3, 2, taps[1], gains[1:2, :], up_v[1], down_v[1], [(v, v), (v, v), (one, v)]),
    ], 0)
    acc[...], top[...], total[...] = attend(x2, kv_v[...], queries[...])


def late_kernel(own, far, tail, acc, top, total, taps, gains, up_v, down_v, kv_v, queries, *refs):
    outs, (x0, x1, sem) = refs[:-3], refs[-3:]
    side = lax.rem(lax.axis_index("tm"), 2)
    copies = [
        pltpu.make_async_copy(own.at[pl.ds(2 * side, 2)], x0.at[pl.ds(3 - 3 * side, 2)], sem.at[0]),
        pltpu.make_async_copy(far, x0.at[pl.ds(2 * side, 3)], sem.at[1]),
    ]
    for copy in copies:
        copy.start()
    x1[pl.ds(pl.multiple_of((3 - 3 * side) * HALF, HALF), 4 * HALF), :] = tail[...]
    v = valid(1)
    one = 1.0
    for copy in copies:
        copy.wait()
    rows0 = x0.reshape(5 * HALF, x0.shape[-1])
    fresh = mix(rows0, 2, 3, 1, taps[0], gains[0:1, :], up_v[0], down_v[0], [(v, v), (one, v), (one, one)])
    x1[pl.ds(pl.multiple_of(side * (4 * HALF), HALF), 3 * HALF), :] = fresh
    x2 = mix(x1, 4, 3, 2, taps[1], gains[1:2, :], up_v[1], down_v[1], [(v, v), (v, v), (one, v)])
    acc2, top2, total2 = attend(x2, kv_v[...], queries[...])
    best = jnp.maximum(top[...], top2)
    a, b = jnp.exp(top[...] - best), jnp.exp(top2 - best)
    whole = total[...] * a + total2 * b
    rows = encode((acc[...] * a + acc2 * b) / whole, best + jnp.log(whole))
    if len(outs) == 1:
        outs[0][...] = rows
        return
    n_pairs, share, lanes = outs[0].shape
    split = rows.reshape(n_pairs, 2, share, lanes)
    outs[0][...] = jnp.where(side == 0, split[:, 0], split[:, 1])
    outs[1][...] = jnp.where(side == 0, split[:, 1], split[:, 0])


def pack_kernel(n, hist, *refs):
    side = lax.rem(lax.axis_index("tm"), 2)
    mine = pl.ds(pl.multiple_of(side * HALF, HALF), HALF)
    other = pl.ds(pl.multiple_of((1 - side) * HALF, HALF), HALF)
    three = pl.ds(side, 3)
    if n == 0:
        swap_out, sem = refs
        copies = [pltpu.make_async_copy(hist.at[:, other, :], swap_out, sem.at[0])]
    elif n == 2:
        whole, (own_out, *outs, sem) = refs[:4], refs[4:]
        copies = [
            pltpu.make_async_copy(a, b, sem.at[i]) for i, (a, b) in enumerate(zip(whole, outs))
        ] + [pltpu.make_async_copy(hist.at[:, mine, :], own_out, sem.at[4])]
    else:
        near_out, far_out, sem = refs
        copies = [
            pltpu.make_async_copy(hist.at[three, mine, :], near_out, sem.at[0]),
            pltpu.make_async_copy(hist.at[three, other, :], far_out, sem.at[1]),
        ]
    for copy in copies:
        copy.start()
    for copy in copies:
        copy.wait()


def pair_kernel(mine, theirs, *refs):
    shape = mine.shape
    flat = (shape[0] * shape[1], shape[2])
    spread = spread_matrix(shape[2] - 128)
    context, lse = combine([
        decode(mine[...].reshape(flat), spread), decode(theirs[...].reshape(flat), spread)
    ])
    merged = encode(context, lse).reshape(shape)
    if len(refs) == 1:
        refs[0][...] = merged
        return
    held = refs[-1]
    held[...] = merged
    pair = lax.div(lax.axis_index("tm"), 2)
    for s, out in enumerate(refs[:-1]):
        out[...] = held[pair ^ s]


def final_kernel(count, *refs):
    parts, readout, out = refs[:count], refs[count], refs[count + 1]
    spread = spread_matrix(out.shape[1])
    context, _ = combine([decode(part[...], spread) for part in parts])
    out[...] = dot(context.astype(BF16), readout[...]).astype(BF16)


def small(limit=8):
    return pltpu.CompilerParams(vmem_limit_bytes=limit * 1024 * 1024)


def on_device(history, taps, gains, up, down, w_kv, readout, queries):
    _, span, width = history.shape
    horizon, hidden = queries.shape[0], up.shape[-1]
    count = lax.axis_size("tm")
    here = lax.axis_index("tm")
    side, pair = lax.rem(here, 2), lax.div(here, 2)
    n_pairs = count // 2
    share = horizon // count

    hist = history.reshape(span // STEP, STEP, width)
    swap = [(i, i ^ 1) for i in range(count)]
    ahead = [(2 * p + 1, 2 * p + 2) for p in range(n_pairs - 1)]
    behind = [(2 * p, (2 * p - 2) % count) for p in range(n_pairs)]
    near_pairs = [(s, t + 1) for s, t in ahead] + behind
    far_pairs = ahead + [(s, t + 1) for s, t in behind]
    three = jax.ShapeDtypeStruct((3, HALF, width), BF16)
    swap_out = pl.pallas_call(
        functools.partial(pack_kernel, 0),
        out_shape=jax.ShapeDtypeStruct((4, HALF, width), BF16),
        in_specs=[HBM],
        out_specs=VMEM,
        scratch_shapes=[pltpu.SemaphoreType.DMA((1,))],
        compiler_params=small(),
        name="pack_swap",
    )(hist)
    got = lax.ppermute(swap_out, "tm", swap)
    near_out, far_out = pl.pallas_call(
        functools.partial(pack_kernel, 1),
        out_shape=[three, three],
        in_specs=[HBM],
        out_specs=[VMEM, VMEM],
        scratch_shapes=[pltpu.SemaphoreType.DMA((2,))],
        compiler_params=small(),
        name="pack_halo",
    )(hist)
    near = lax.ppermute(near_out, "tm", near_pairs)
    far = lax.ppermute(far_out, "tm", far_pairs)

    own, up_v, down_v, kv_v, readout_v = pl.pallas_call(
        functools.partial(pack_kernel, 2),
        out_shape=[jax.ShapeDtypeStruct((4, HALF, width), BF16)]
        + [jax.ShapeDtypeStruct(w.shape, w.dtype) for w in (up, down, w_kv, readout)],
        in_specs=[HBM] * 5,
        out_specs=[VMEM] * 5,
        scratch_shapes=[pltpu.SemaphoreType.DMA((5,))],
        compiler_params=small(16),
        name="stage",
    )(hist, up, down, w_kv, readout)
    state = jax.ShapeDtypeStruct((horizon, width), F32)
    per_row = 4 * width * hidden
    tail, acc, top, total = pl.pallas_call(
        early_kernel,
        out_shape=[jax.ShapeDtypeStruct((4 * HALF, width), BF16), state, state, state],
        in_specs=[ANY] * 3 + [VMEM] * 6,
        out_specs=[VMEM] * 4,
        scratch_shapes=[
            pltpu.VMEM((11, HALF, width), BF16), pltpu.VMEM((9 * HALF, width), BF16), pltpu.SemaphoreType.DMA((3,))
        ],
        compiler_params=pltpu.CompilerParams(vmem_limit_bytes=32 * 1024 * 1024),
        cost_estimate=pl.CostEstimate(
            flops=(14 * per_row + 5 * 2 * per_row) * HALF, bytes_accessed=8 << 20, transcendentals=2 << 20
        ),
        name="early",
    )(own, got, near, taps, gains, up_v, down_v, kv_v, queries)
    lanes = width + 128
    fused = share % 16 == 0 and n_pairs <= 4 and n_pairs & (n_pairs - 1) == 0
    one = jax.ShapeDtypeStruct((share, lanes), BF16)
    quarter = jax.ShapeDtypeStruct((n_pairs, share, lanes), BF16)
    payload = pl.pallas_call(
        late_kernel,
        out_shape=[quarter, quarter] if fused else [jax.ShapeDtypeStruct((horizon, lanes), BF16)],
        in_specs=[ANY] * 2 + [VMEM] * 10,
        out_specs=[VMEM] * (2 if fused else 1),
        scratch_shapes=[
            pltpu.VMEM((5, HALF, width), BF16), pltpu.VMEM((7 * HALF, width), BF16), pltpu.SemaphoreType.DMA((2,))
        ],
        compiler_params=pltpu.CompilerParams(vmem_limit_bytes=32 * 1024 * 1024),
        cost_estimate=pl.CostEstimate(
            flops=(6 * per_row + 3 * 2 * per_row) * HALF, bytes_accessed=8 << 20, transcendentals=1 << 20
        ),
        name="late",
    )(own, far, tail, acc, top, total, taps, gains, up_v, down_v, kv_v, queries)
    if fused:
        mine, send = payload
    else:
        split = payload[0].reshape(n_pairs, 2, share, lanes)
        mine, send = (lax.dynamic_index_in_dim(split, s, 1, False) for s in (side, 1 - side))
    theirs = lax.ppermute(send, "tm", swap)
    merged = pl.pallas_call(
        pair_kernel,
        out_shape=[one] * n_pairs if fused else [quarter],
        in_specs=[VMEM] * 2,
        out_specs=[VMEM] * (n_pairs if fused else 1),
        scratch_shapes=[pltpu.VMEM(quarter.shape, BF16)] if fused else [],
        compiler_params=small(),
        name="pair",
    )(mine, theirs)
    if fused:
        parts = [merged[0]] + [
            lax.ppermute(merged[s], "tm", [(i, i ^ (2 * s)) for i in range(count)]) for s in range(1, n_pairs)
        ]
    else:
        groups = [[2 * p + s for p in range(n_pairs)] for s in range(2)]
        swapped = lax.all_to_all(merged[0], "tm", 0, 0, axis_index_groups=groups, tiled=True)
        parts = [swapped[p] for p in range(n_pairs)]
    result = pl.pallas_call(
        functools.partial(final_kernel, len(parts)),
        out_shape=jax.ShapeDtypeStruct((share, width), BF16),
        in_specs=[VMEM] * (len(parts) + 1),
        out_specs=VMEM,
        compiler_params=small(),
        name="final",
    )(*parts, readout_v)
    return result[None]


def solution(mesh):
    placed = (P(("groups", "series"), "tm", None), P(), P(), P(), P(), P(), P(), P())
    return jax.shard_map(
        on_device,
        mesh=mesh,
        in_specs=placed,
        out_specs=P(("groups", "series"), "tm", None),
        check_vma=False,
    )
```

time: 60.8 us -> 48.8 us (0.80)
  local copies, waits for them, and re-layouts: 10.6 us -> 5.13 us
  starting transfers between devices: 19.5 us -> 14.8 us
  Pallas kernels: 18.1 us -> 14.6 us
  waiting for transfers between devices: 12 us -> 13.8 us
    ppermute x1, starting transfers between devices: 6.7 us -> 1.31 us  [on_device(): far = lax.ppermute(far_out, 'tm', far_pairs)]
    dynamic_slice x2 -> x0, local copies, waits for them, and re-layouts: 4.14 us -> none  [the longest x1 2.1 us: on_device(): lax.dynamic_slice(hist, (side, side * HALF, zero), (3, HALF, width))]
    squeeze x2 -> x0, local copies, waits for them, and re-layouts: 2.05 us -> none  [the longest x1 1.39 us: on_device(): block = lax.dynamic_index_in_dim(merged, pair ^ s, 0, False)]
    pallas_call x2 -> x5, Pallas kernels: 7.48 us -> 5.58 us  [the longest x1 4.56 us: on_device(): pl.pallas_call(late_kernel, out_shape=[quarter, quarter] if fused else [j...]
    ppermute x6, waiting for transfers between devices: 12 us -> 13.8 us  [the longest x3 5.58 us: on_device(): lax.ppermute(merged[s], 'tm', [(i, i ^ 2 * s) for i in range(count)])]
    pallas_call x1, Pallas kernels: 2.04 us -> 1.03 us  [on_device(): pl.pallas_call(functools.partial(final_kernel, len(parts)), out_shape=jax...]
    unnamed x27 -> x17, local copies, waits for them, and re-layouts: 4.44 us -> 5.13 us
    ppermute x6, starting transfers between devices: 12.8 us -> 13.5 us  [the longest x1 5.51 us: on_device(): near = lax.ppermute(near_out, 'tm', near_pairs)]
  transfers between devices with their start and end apart: 7 -> 7, of which waited for: 4 -> 4; matrix products, arithmetic and copies ran while one was open for 3% -> 1% of each run, Pallas kernels for 14% -> 18%
where the time goes in v2:
time: 48.8 us; the launch traced here: 48.5 us
  starting transfers between devices  14.8 us (30%)
  Pallas kernels  14.6 us (30%)
  waiting for transfers between devices  13.8 us (28%)
  local copies, waits for them, and re-layouts  5.13 us (11%)
    pallas_call x1, Pallas kernels, on_device(): pl.pallas_call(early_kernel, out_shape=[jax.ShapeDtypeStruct((4 * HALF, w...  7.99 us
    ppermute x3, waiting for transfers between devices, on_device(): lax.ppermute(merged[s], 'tm', [(i, i ^ 2 * s) for i in range(count)])  5.58 us
    ppermute x1, starting transfers between devices, on_device(): near = lax.ppermute(near_out, 'tm', near_pairs)  5.51 us
    unnamed x17, local copies, waits for them, and re-layouts  5.13 us
    ppermute x3, starting transfers between devices, on_device(): lax.ppermute(merged[s], 'tm', [(i, i ^ 2 * s) for i in range(count)])  4.92 us
    pallas_call x1, Pallas kernels, on_device(): pl.pallas_call(late_kernel, out_shape=[quarter, quarter] if fused else [j...  4.56 us
    ppermute x1, waiting for transfers between devices, on_device(): theirs = lax.ppermute(send, 'tm', swap)  4.43 us
    ppermute x1, waiting for transfers between devices, on_device(): near = lax.ppermute(near_out, 'tm', near_pairs)  3.81 us
  transfers between devices with their start and end apart: 7, of which 4 were waited for; matrix products, arithmetic and copies ran while one was open for 1% of the time, Pallas kernels for 18%

profile of v2, /device:TPU:0, one launch (start us, length us, event | category | flops | bytes accessed | tf_op | source)
XLA Modules:
  0.0 48.5 jit_solution(12381966722783503600)
XLA Ops:
  0.0 0.0 copy-start
  0.0 1.2 %copy-done = bf16[1,1024,512]{2,1,0:T(8,128)(2,1)S(1)} copy-done((bf16[1,1024,512]{2,1,0:T(8,128)(2,1)S(1)}, bf16[1,1024,512]{2,1,0:T(8,128)(2,1)}, u32[]{:S(2)}) %copy-start) | copy-done | bytes 1048600
  1.2 0.0 copy-start.1
  1.2 0.0 copy-start.4
  1.2 0.0 copy-start.5
  1.3 3.0 %collective-permute-start.1 = (bf16[4,128,512]{2,1,0:T(8,128)(2,1)S(1)}, bf16[4,128,512]{2,1,0:T(8,128)(2,1)S(1)}, u32[]{:S(2)}, u32[]{:S(2)}) collective-permute-start(bf16[4,128,512]{2,1,0:T(8,128)(2,1)S(1)} %pack_swap.1), channel_id=1, source_target_pairs={{0,1},{1,0},{2,3},{3,2},{4,5},{5,4},{6,7},{7,6},{8,9},{9,8},{10,11... | collective-permute-start | bytes 1572872 | tf_op jit(solution)/shard_map/ppermute | solution.py:240
  4.3 0.1 pack_halo.1
  4.4 5.5 %collective-permute-start.2 = (bf16[3,128,512]{2,1,0:T(8,128)(2,1)S(1)}, bf16[3,128,512]{2,1,0:T(8,128)(2,1)S(1)}, u32[]{:S(2)}, u32[]{:S(2)}) collective-permute-start(bf16[3,128,512]{2,1,0:T(8,128)(2,1)S(1)} %get-tuple-element.24), channel_id=1, source_target_pairs={{1,3},{3,5},{5,7},{0,6},{2,0},{4,2},{6,4},{9,11},{11,13},{13,15},{... | collective-permute-start | bytes 1179656 | tf_op jit(solution)/shard_map/ppermute | solution.py:250
  10.0 1.3 %collective-permute-start = (bf16[3,128,512]{2,1,0:T(8,128)(2,1)S(1)}, bf16[3,128,512]{2,1,0:T(8,128)(2,1)S(1)}, u32[]{:S(2)}, u32[]{:S(2)}) collective-permute-start(bf16[3,128,512]{2,1,0:T(8,128)(2,1)S(1)} %get-tuple-element.23), channel_id=1, source_target_pairs={{1,2},{3,4},{5,6},{0,7},{2,1},{4,3},{6,5},{9,10},{11,12},{13,14},{... | collective-permute-start | bytes 1179656 | tf_op jit(solution)/shard_map/ppermute | solution.py:251
  11.3 0.7 %copy.9.taps = f32[2,3,512]{2,1,0:T(4,128)S(1)} copy(f32[2,3,512]{2,0,1:T(2,128)} %param.9) | data formatting | bytes 24576 | tf_op args[1]
  12.0 0.0 copy-done.1
  12.0 0.0 copy-done.4
  12.0 0.0 copy-done.5
  12.0 0.0 copy-start.2
  12.0 1.6 %copy-done.2 = bf16[2,512,1024]{2,1,0:T(8,128)(2,1)S(1)} copy-done((bf16[2,512,1024]{2,1,0:T(8,128)(2,1)S(1)}, bf16[2,512,1024]{2,1,0:T(8,128)(2,1)}, u32[]{:S(2)}) %copy-start.2) | copy-done | bytes 2097176
  13.6 0.0 copy-start.3
  13.6 1.6 %copy-done.3 = bf16[2,1024,512]{2,1,0:T(8,128)(2,1)S(1)} copy-done((bf16[2,1024,512]{2,1,0:T(8,128)(2,1)S(1)}, bf16[2,1024,512]{2,1,0:T(8,128)(2,1)}, u32[]{:S(2)}) %copy-start.3) | copy-done | bytes 2097176
  15.2 0.0 copy-start.6
  15.2 0.0 copy-start.7
  15.2 0.5 stage.1
  15.7 3.8 %collective-permute-done.2.near = bf16[3,128,512]{2,1,0:T(8,128)(2,1)S(1)} collective-permute-done((bf16[3,128,512]{2,1,0:T(8,128)(2,1)S(1)}, bf16[3,128,512]{2,1,0:T(8,128)(2,1)S(1)}, u32[]{:S(2)}, u32[]{:S(2)}) %collective-permute-start.2) | collective-permute-done | bytes 393248 | tf_op jit(solution)/shard_map/ppermute | solution.py:250
  19.5 0.0 collective-permute-done.1.got
  19.5 0.0 copy-done.6
  19.5 0.0 copy-done.7
  19.5 8.0 %early.1 = (bf16[512,512]{1,0:T(8,128)(2,1)S(1)}, f32[128,512]{1,0:T(8,128)S(1)}, f32[128,512]{1,0:T(8,128)S(1)}, f32[128,512]{1,0:T(8,128)S(1)}) custom-call(bf16[4,128,512]{2,1,0:T(8,128)(2,1)S(1)} %get-tuple-element.22.own, bf16[4,128,512]{2,1,0:T(8,128)(2,1)S(1)} %collective-permute-done.1.got, bf16[3,128,512]{2,1,0:T(8,128)(2,1)S(1)} %collective-permute-done.2.near, ...), custom_call_target="tpu_custom_call" | custom-call | flops 6442450944 | bytes 8388608 | tf_op jit(solution)/shard_map/early/pallas_call | solution.py:265
  27.5 0.0 collective-permute-done.far
  27.5 4.6 %late.1 = (bf16[4,16,640]{2,1,0:T(8,128)(2,1)S(1)}, bf16[4,16,640]{2,1,0:T(8,128)(2,1)S(1)}) custom-call(bf16[4,128,512]{2,1,0:T(8,128)(2,1)S(1)} %get-tuple-element.22.own, bf16[3,128,512]{2,1,0:T(8,128)(2,1)S(1)} %collective-permute-done.far, bf16[512,512]{1,0:T(8,128)(2,1)S(1)} %get-tuple-element.28.tail, f32[128,512]{1,0:T(8,128)S(1)} %get-tuple-element.29.acc, ...), custom_call_target="tpu_custom_call" | custom-call | flops 3221225472 | bytes 8388608 | tf_op jit(solution)/shard_map/late/pallas_call | solution.py:283
  32.1 0.1 collective-permute-start.3
  32.2 4.4 %collective-permute-done.3.theirs = bf16[4,16,640]{2,1,0:T(8,128)(2,1)S(1)} collective-permute-done((bf16[4,16,640]{2,1,0:T(8,128)(2,1)S(1)}, bf16[4,16,640]{2,1,0:T(8,128)(2,1)S(1)}, u32[]{:S(2)}, u32[]{:S(2)}) %collective-permute-start.3) | collective-permute-done | bytes 81952 | tf_op jit(solution)/shard_map/ppermute | solution.py:302
  36.6 0.4 pair.1
  37.0 0.5 %collective-permute-start.4 = (bf16[16,640]{1,0:T(8,128)(2,1)S(1)}, bf16[16,640]{1,0:T(8,128)(2,1)S(1)}, u32[]{:S(2)}, u32[]{:S(2)}) collective-permute-start(bf16[16,640]{1,0:T(8,128)(2,1)S(1)} %get-tuple-element.35), channel_id=1, source_target_pairs={{0,2},{1,3},{2,0},{3,1},{4,6},{5,7},{6,4},{7,5},{8,10},{9,11},{10,... | collective-permute-start | bytes 61448 | tf_op jit(solution)/shard_map/ppermute | solution.py:314
  37.5 4.4 %collective-permute-start.5 = (bf16[16,640]{1,0:T(8,128)(2,1)S(1)}, bf16[16,640]{1,0:T(8,128)(2,1)S(1)}, u32[]{:S(2)}, u32[]{:S(2)}) collective-permute-start(bf16[16,640]{1,0:T(8,128)(2,1)S(1)} %get-tuple-element.36), channel_id=1, source_target_pairs={{0,4},{1,5},{2,6},{3,7},{4,0},{5,1},{6,2},{7,3},{8,12},{9,13},{10,... | collective-permute-start | bytes 61448 | tf_op jit(solution)/shard_map/ppermute | solution.py:314
  41.9 0.0 collective-permute-start.6
  41.9 0.0 collective-permute-done.4.refs_1_
  41.9 1.8 %collective-permute-done.5.refs_2_ = bf16[16,640]{1,0:T(8,128)(2,1)S(1)} collective-permute-done((bf16[16,640]{1,0:T(8,128)(2,1)S(1)}, bf16[16,640]{1,0:T(8,128)(2,1)S(1)}, u32[]{:S(2)}, u32[]{:S(2)}) %collective-permute-start.5) | collective-permute-done | bytes 20512 | tf_op jit(solution)/shard_map/ppermute | solution.py:314
  43.6 3.8 %collective-permute-done.6.refs_3_ = bf16[16,640]{1,0:T(8,128)(2,1)S(1)} collective-permute-done((bf16[16,640]{1,0:T(8,128)(2,1)S(1)}, bf16[16,640]{1,0:T(8,128)(2,1)S(1)}, u32[]{:S(2)}, u32[]{:S(2)}) %collective-permute-start.6) | collective-permute-done | bytes 20512 | tf_op jit(solution)/shard_map/ppermute | solution.py:314
  47.5 1.0 %final.1 = bf16[16,512]{1,0:T(8,128)(2,1)} custom-call(bf16[16,640]{1,0:T(8,128)(2,1)S(1)} %get-tuple-element.34.refs_0_, bf16[16,640]{1,0:T(8,128)(2,1)S(1)} %collective-permute-done.4.refs_1_, bf16[16,640]{1,0:T(8,128)(2,1)S(1)} %collective-permute-done.5.refs_2_, bf16[16,640]{1,0:T(8,128)(2,1)S(1)} %collective-permute-done.6.refs_3_, ...), custom_call_target="tpu_custom_call" | custom-call | tf_op jit(solution)/shard_map/final/pallas_call | solution.py:320
  (1 shorter events, 0.0 us)
Async XLA Ops:
  0.0 1.2 %copy-start = (bf16[1,1024,512]{2,1,0:T(8,128)(2,1)S(1)}, bf16[1,1024,512]{2,1,0:T(8,128)(2,1)}, u32[]{:S(2)}) copy-start(bf16[1,1024,512]{2,1,0:T(8,128)(2,1)} %param.8) | copy-start | bytes 3145732
  1.2 10.8 %copy-start.1 = (bf16[1,1024,512]{2,1,0:T(8,128)(2,1)S(1)}, bf16[1,1024,512]{2,1,0:T(8,128)(2,1)}, u32[]{:S(2)}) copy-start(bf16[1,1024,512]{2,1,0:T(8,128)(2,1)} %param.8) | copy-start | bytes 3145732
  1.2 10.8 %copy-start.4 = (bf16[512,1024]{1,0:T(8,128)(2,1)S(1)}, bf16[512,1024]{1,0:T(8,128)(2,1)}, u32[]{:S(2)}) copy-start(bf16[512,1024]{1,0:T(8,128)(2,1)} %refs_2_.1) | copy-start | bytes 3145732
  1.2 10.8 %copy-start.5 = (bf16[512,512]{1,0:T(8,128)(2,1)S(1)}, bf16[512,512]{1,0:T(8,128)(2,1)}, u32[]{:S(2)}) copy-start(bf16[512,512]{1,0:T(8,128)(2,1)} %refs_3_.1) | copy-start | bytes 1572868
  1.3 18.2 %collective-permute-start.1 = (bf16[4,128,512]{2,1,0:T(8,128)(2,1)S(1)}, bf16[4,128,512]{2,1,0:T(8,128)(2,1)S(1)}, u32[]{:S(2)}, u32[]{:S(2)}) collective-permute-start(bf16[4,128,512]{2,1,0:T(8,128)(2,1)S(1)} %pack_swap.1), channel_id=1, source_target_pairs={{0,1},{1,0},{2,3},{3,2},{4,5},{5,4},{6,7},{7,6},{8,9},{9,8},{10,11... | collective-permute-start | bytes 1572872 | tf_op jit(solution)/shard_map/ppermute | solution.py:240
  4.4 15.1 %collective-permute-start.2 = (bf16[3,128,512]{2,1,0:T(8,128)(2,1)S(1)}, bf16[3,128,512]{2,1,0:T(8,128)(2,1)S(1)}, u32[]{:S(2)}, u32[]{:S(2)}) collective-permute-start(bf16[3,128,512]{2,1,0:T(8,128)(2,1)S(1)} %get-tuple-element.24), channel_id=1, source_target_pairs={{1,3},{3,5},{5,7},{0,6},{2,0},{4,2},{6,4},{9,11},{11,13},{13,15},{... | collective-permute-start | bytes 1179656 | tf_op jit(solution)/shard_map/ppermute | solution.py:250
  10.0 17.6 %collective-permute-start = (bf16[3,128,512]{2,1,0:T(8,128)(2,1)S(1)}, bf16[3,128,512]{2,1,0:T(8,128)(2,1)S(1)}, u32[]{:S(2)}, u32[]{:S(2)}) collective-permute-start(bf16[3,128,512]{2,1,0:T(8,128)(2,1)S(1)} %get-tuple-element.23), channel_id=1, source_target_pairs={{1,2},{3,4},{5,6},{0,7},{2,1},{4,3},{6,5},{9,10},{11,12},{13,14},{... | collective-permute-start | bytes 1179656 | tf_op jit(solution)/shard_map/ppermute | solution.py:251
  12.0 1.6 %copy-start.2 = (bf16[2,512,1024]{2,1,0:T(8,128)(2,1)S(1)}, bf16[2,512,1024]{2,1,0:T(8,128)(2,1)}, u32[]{:S(2)}) copy-start(bf16[2,512,1024]{2,1,0:T(8,128)(2,1)} %refs_0_.1) | copy-start | bytes 6291460
  13.6 1.6 %copy-start.3 = (bf16[2,1024,512]{2,1,0:T(8,128)(2,1)S(1)}, bf16[2,1024,512]{2,1,0:T(8,128)(2,1)}, u32[]{:S(2)}) copy-start(bf16[2,1024,512]{2,1,0:T(8,128)(2,1)} %refs_1_.1) | copy-start | bytes 6291460
  15.2 4.3 %copy-start.6 = (bf16[128,512]{1,0:T(8,128)(2,1)S(1)}, bf16[128,512]{1,0:T(8,128)(2,1)}, u32[]{:S(2)}) copy-start(bf16[128,512]{1,0:T(8,128)(2,1)} %queries.3) | copy-start | bytes 393220
  15.2 4.3 %copy-start.7 = (f32[2,512]{1,0:T(2,128)S(1)}, f32[2,512]{1,0:T(2,128)}, u32[]{:S(2)}) copy-start(f32[2,512]{1,0:T(2,128)} %gains.3) | copy-start | bytes 12292
  32.1 4.5 %collective-permute-start.3 = (bf16[4,16,640]{2,1,0:T(8,128)(2,1)S(1)}, bf16[4,16,640]{2,1,0:T(8,128)(2,1)S(1)}, u32[]{:S(2)}, u32[]{:S(2)}) collective-permute-start(bf16[4,16,640]{2,1,0:T(8,128)(2,1)S(1)} %get-tuple-element.33), channel_id=1, source_target_pairs={{0,1},{1,0},{2,3},{3,2},{4,5},{5,4},{6,7},{7,6},{8,9},{9,8},{10,11... | collective-permute-start | bytes 245768 | tf_op jit(solution)/shard_map/ppermute | solution.py:302
  37.0 4.9 %collective-permute-start.4 = (bf16[16,640]{1,0:T(8,128)(2,1)S(1)}, bf16[16,640]{1,0:T(8,128)(2,1)S(1)}, u32[]{:S(2)}, u32[]{:S(2)}) collective-permute-start(bf16[16,640]{1,0:T(8,128)(2,1)S(1)} %get-tuple-element.35), channel_id=1, source_target_pairs={{0,2},{1,3},{2,0},{3,1},{4,6},{5,7},{6,4},{7,5},{8,10},{9,11},{10,... | collective-permute-start | bytes 61448 | tf_op jit(solution)/shard_map/ppermute | solution.py:314
  37.5 6.1 %collective-permute-start.5 = (bf16[16,640]{1,0:T(8,128)(2,1)S(1)}, bf16[16,640]{1,0:T(8,128)(2,1)S(1)}, u32[]{:S(2)}, u32[]{:S(2)}) collective-permute-start(bf16[16,640]{1,0:T(8,128)(2,1)S(1)} %get-tuple-element.36), channel_id=1, source_target_pairs={{0,4},{1,5},{2,6},{3,7},{4,0},{5,1},{6,2},{7,3},{8,12},{9,13},{10,... | collective-permute-start | bytes 61448 | tf_op jit(solution)/shard_map/ppermute | solution.py:314
  41.9 5.6 %collective-permute-start.6 = (bf16[16,640]{1,0:T(8,128)(2,1)S(1)}, bf16[16,640]{1,0:T(8,128)(2,1)S(1)}, u32[]{:S(2)}, u32[]{:S(2)}) collective-permute-start(bf16[16,640]{1,0:T(8,128)(2,1)S(1)} %get-tuple-element.37), channel_id=1, source_target_pairs={{0,6},{1,7},{2,4},{3,5},{4,2},{5,3},{6,0},{7,1},{8,14},{9,15},{10,... | collective-permute-start | bytes 61448 | tf_op jit(solution)/shard_map/ppermute | solution.py:314

commit v3 on v2

v3 whole, which is shorter than its diff:
```python
import functools

import jax
import jax.numpy as jnp
from jax import lax
from jax.experimental import pallas as pl
from jax.experimental.pallas import tpu as pltpu
from jax.sharding import PartitionSpec as P

HEADS = 8
STEP = 256
HALF = STEP // 2
BF16, F32 = jnp.bfloat16, jnp.float32
ANY = pl.BlockSpec(memory_space=pl.ANY)
VMEM = pl.BlockSpec(memory_space=pltpu.VMEM)
HBM = pl.BlockSpec(memory_space=pltpu.HBM)


def dot(a, b):
    return jnp.dot(a, b, preferred_element_type=F32)


def gelu(u):
    half = 0.5 * u
    return half + half * jnp.tanh(u * (0.7978845608028654 + (0.7978845608028654 * 0.044715) * (u * u)))


def mix(src, first, steps, dilation, taps, gain, up, down, factors):
    rows, kept = [], []
    for j in range(steps):
        w1, w2 = factors[j]
        at = [(first + j - k * dilation) * HALF for k in range(3)]
        now = src[at[0] : at[0] + HALF, :].astype(F32)
        conv = taps[0:1, :] * now
        conv = conv + (taps[1:2, :] * w1) * src[at[1] : at[1] + HALF, :].astype(F32)
        conv = conv + (taps[2:3, :] * w2) * src[at[2] : at[2] + HALF, :].astype(F32)
        scale = lax.rsqrt(jnp.mean(conv * conv, axis=-1, keepdims=True) + 1e-05)
        rows.append((conv * scale * gain).astype(BF16))
        kept.append(now)
    inner = gelu(dot(jnp.concatenate(rows, 0), up)).astype(BF16)
    return (jnp.concatenate(kept, 0) + dot(inner, down)).astype(BF16)


def attend(x2, w_kv, queries):
    pairs = dot(x2, w_kv).astype(BF16)
    horizon, width = queries.shape
    low = lax.broadcasted_iota(jnp.int32, (horizon, 128), 1) < 64
    zero = jnp.zeros((horizon, 128), BF16)
    acc, top, total, scores = [], [], [], []
    for p in range(width // 128):
        lanes = slice(128 * p, 128 * p + 128)
        q = queries[:, lanes] * jnp.asarray(0.125, BF16)
        q2 = jnp.concatenate([jnp.where(low, q, zero), jnp.where(low, zero, q)], 0)
        scores.append(
            lax.dot_general(q2, pairs[:, lanes], (((1,), (1,)), ((), ())), preferred_element_type=F32)
        )
    for p in range(width // 128):
        m = jnp.max(scores[p], axis=-1, keepdims=True)
        e = jnp.exp(scores[p] - m)
        s = jnp.sum(e, axis=-1, keepdims=True)
        c = dot(e.astype(BF16), pairs[:, width + 128 * p : width + 128 * p + 128])
        acc.append(jnp.where(low, c[:horizon], c[horizon:]))
        top.append(jnp.where(low, m[:horizon], m[horizon:]))
        total.append(jnp.where(low, s[:horizon], s[horizon:]))
    return jnp.concatenate(acc, 1), jnp.concatenate(top, 1), jnp.concatenate(total, 1)


def encode(context, lse):
    lane = lax.broadcasted_iota(jnp.int32, (lse.shape[0], 128), 1) & 63
    stats = jnp.zeros((lse.shape[0], 128), F32)
    for p in range(lse.shape[1] // 128):
        rest = lse[:, 128 * p : 128 * p + 128]
        for piece in range(3):
            part = rest.astype(BF16).astype(F32)
            stats = jnp.where(lane == 3 * p + piece, part, stats)
            rest = rest - part
    return jnp.concatenate([context.astype(BF16), stats.astype(BF16)], 1)


def spread_matrix(width):
    row = lax.broadcasted_iota(jnp.int32, (128, width), 0)
    col = lax.broadcasted_iota(jnp.int32, (128, width), 1)
    piece = (row & 63) - 3 * (col >> 7)
    return jnp.where((piece >= 0) & (piece < 3) & ((row >> 6) == ((col >> 6) & 1)), 1.0, 0.0).astype(BF16)


def decode(rows, spread):
    width = rows.shape[1] - 128
    return rows[:, :width].astype(F32), dot(rows[:, width:], spread)


def combine(parts):
    top = functools.reduce(jnp.maximum, [l for _, l in parts])
    weights = [jnp.exp(l - top) for _, l in parts]
    total = functools.reduce(jnp.add, weights)
    context = functools.reduce(jnp.add, [w * c for w, (c, _) in zip(weights, parts)])
    return context / total, top + jnp.log(total)


def valid(side):
    here, count = lax.axis_index("tm"), lax.axis_size("tm")
    return jnp.where(here == count - 2 + side, 0.0, 1.0).astype(F32)


def early_kernel(own, got0, got1, near0, near1, taps, gains, up_v, down_v, kv_v, queries, tail, acc, top, total,
                 x0, x1, sem):
    side, series = lax.rem(lax.axis_index("tm"), 2), lax.rem(lax.axis_index("series"), 2)
    pltpu.make_async_copy(own, x0.at[pl.ds(side * 7, 4)], sem.at[0]).start()
    got_at, near_at = pl.ds(4 - side, 4), pl.ds(8 - 8 * side, 3)
    for which, got, near in ((0, got0, near0), (1, got1, near1)):
        @pl.when(series == which)
        def _():
            pltpu.make_async_copy(got, x0.at[got_at], sem.at[1]).start()
            pltpu.make_async_copy(near, x0.at[near_at], sem.at[2]).start()
    v = valid(0)
    one = 1.0
    pltpu.make_async_copy(own, x0.at[pl.ds(side * 7, 4)], sem.at[0]).wait()
    pltpu.make_async_copy(got0, x0.at[got_at], sem.at[1]).wait()
    pltpu.make_async_copy(near0, x0.at[near_at], sem.at[2]).wait()
    rows0 = x0.reshape(11 * HALF, x0.shape[-1])
    for j in range(0, 9, 3):
        factors = [(v, v), (one, v), (one, one)] if j == 6 else [(one, one)] * 3
        x1[j * HALF : (j + 3) * HALF, :] = mix(
            rows0, j + 2, 3, 1, taps[0], gains[0:1, :], up_v[0], down_v[0], factors
        )
    tail[...] = x1[pl.ds(pl.multiple_of(side * (5 * HALF), HALF), 4 * HALF), :]
    x2 = jnp.concatenate([
        mix(x1, 4, 2, 2, taps[1], gains[1:2, :], up_v[1], down_v[1], [(one, one)] * 2),
        mix(x1, 6, 3, 2, taps[1], gains[1:2, :], up_v[1], down_v[1], [(v, v), (v, v), (one, v)]),
    ], 0)
    acc[...], top[...], total[...] = attend(x2, kv_v[...], queries[...])


def late_kernel(own, far0, far1, tail, acc, top, total, taps, gains, up_v, down_v, kv_v, queries, out, x0, x1, sem):
    side, series = lax.rem(lax.axis_index("tm"), 2), lax.rem(lax.axis_index("series"), 2)
    own_copy = pltpu.make_async_copy(own.at[pl.ds(2 * side, 2)], x0.at[pl.ds(3 - 3 * side, 2)], sem.at[0])
    own_copy.start()
    for which, far in ((0, far0), (1, far1)):
        @pl.when(series == which)
        def _():
            pltpu.make_async_copy(far, x0.at[pl.ds(2 * side, 3)], sem.at[1]).start()
    x1[pl.ds(pl.multiple_of((3 - 3 * side) * HALF, HALF), 4 * HALF), :] = tail[...]
    v = valid(1)
    one = 1.0
    own_copy.wait()
    pltpu.make_async_copy(far0, x0.at[pl.ds(2 * side, 3)], sem.at[1]).wait()
    rows0 = x0.reshape(5 * HALF, x0.shape[-1])
    fresh = mix(rows0, 2, 3, 1, taps[0], gains[0:1, :], up_v[0], down_v[0], [(v, v), (one, v), (one, one)])
    x1[pl.ds(pl.multiple_of(side * (4 * HALF), HALF), 3 * HALF), :] = fresh
    x2 = mix(x1, 4, 3, 2, taps[1], gains[1:2, :], up_v[1], down_v[1], [(v, v), (v, v), (one, v)])
    acc2, top2, total2 = attend(x2, kv_v[...], queries[...])
    best = jnp.maximum(top[...], top2)
    a, b = jnp.exp(top[...] - best), jnp.exp(top2 - best)
    whole = total[...] * a + total2 * b
    rows = encode((acc[...] * a + acc2 * b) / whole, best + jnp.log(whole))
    out[...] = rows


def start_all(copies):
    for copy in copies:
        copy.start()
    for copy in copies:
        copy.wait()


def pack_kernel(n, hist, *refs):
    side = lax.rem(lax.axis_index("tm"), 2)
    mine = pl.ds(pl.multiple_of(side * HALF, HALF), HALF)
    other = pl.ds(pl.multiple_of((1 - side) * HALF, HALF), HALF)
    three = pl.ds(side, 3)
    if n == 0:
        out, sem = refs
        start_all([pltpu.make_async_copy(hist.at[:, other, :], out, sem.at[0])])
    elif n == 1:
        near, far, sem = refs
        start_all([
            pltpu.make_async_copy(hist.at[three, mine, :], near, sem.at[0]),
            pltpu.make_async_copy(hist.at[three, other, :], far, sem.at[1]),
        ])
    else:
        whole, (own, *outs, sem) = refs[:4], refs[4:]
        start_all(
            [pltpu.make_async_copy(a, b, sem.at[i]) for i, (a, b) in enumerate(zip(whole, outs))]
            + [pltpu.make_async_copy(hist.at[:, mine, :], own, sem.at[4])]
        )


def final_kernel(parts, readout, out):
    share, width = out.shape
    rows = parts[...]
    context, lse = decode(rows, spread_matrix(width))
    count = rows.shape[0] // share
    cut = [slice(i * share, (i + 1) * share) for i in range(count)]
    context, _ = combine([(context[c], lse[c]) for c in cut])
    out[...] = dot(context.astype(BF16), readout[...]).astype(BF16)


def small(limit=8):
    return pltpu.CompilerParams(vmem_limit_bytes=limit * 1024 * 1024)


def on_device(history, taps, gains, up, down, w_kv, readout, queries):
    _, span, width = history.shape
    horizon, hidden = queries.shape[0], up.shape[-1]
    count = lax.axis_size("tm")
    here = lax.axis_index("tm")
    side, pair = lax.rem(here, 2), lax.div(here, 2)
    n_pairs = count // 2
    share = horizon // count

    hist = history.reshape(span // STEP, STEP, width)
    swap = [(i, i ^ 1) for i in range(count)]
    ahead = [(2 * p + 1, 2 * p + 2) for p in range(n_pairs - 1)]
    behind = [(2 * p, (2 * p - 2) % count) for p in range(n_pairs)]
    near_pairs = [(s, t + 1) for s, t in ahead] + behind
    far_pairs = ahead + [(s, t + 1) for s, t in behind]

    def send(value, *by_series):
        pairs = [
            (r * count + s, r * count + t)
            for r in range(lax.axis_size("series")) for s, t in by_series[r % 2]
        ]
        return lax.ppermute(value, ("series", "tm"), pairs)

    four, three = (jax.ShapeDtypeStruct((k, HALF, width), BF16) for k in (4, 3))
    swap_out = pl.pallas_call(
        functools.partial(pack_kernel, 0),
        out_shape=four,
        in_specs=[HBM],
        out_specs=VMEM,
        scratch_shapes=[pltpu.SemaphoreType.DMA((1,))],
        compiler_params=small(),
        name="pack_swap",
    )(hist)
    got0 = send(swap_out, swap, [])
    near_out, far_out = pl.pallas_call(
        functools.partial(pack_kernel, 1),
        out_shape=[three, three],
        in_specs=[HBM],
        out_specs=[VMEM, VMEM],
        scratch_shapes=[pltpu.SemaphoreType.DMA((2,))],
        compiler_params=small(),
        name="pack_halo",
    )(hist)
    near0 = send(near_out, near_pairs, [])
    own, up_v, down_v, kv_v, readout_v = pl.pallas_call(
        functools.partial(pack_kernel, 2),
        out_shape=[jax.ShapeDtypeStruct((4, HALF, width), BF16)]
        + [jax.ShapeDtypeStruct(w.shape, w.dtype) for w in (up, down, w_kv, readout)],
        in_specs=[HBM] * 5,
        out_specs=[VMEM] * 5,
        scratch_shapes=[pltpu.SemaphoreType.DMA((5,))],
        compiler_params=small(16),
        name="stage",
    )(hist, up, down, w_kv, readout)
    own, swap_out, near_out, far_out = lax.optimization_barrier((own, swap_out, near_out, far_out))
    far0 = send(far_out, far_pairs, [])
    got1 = send(swap_out, [], swap)
    near1 = send(near_out, [], near_pairs)
    far1 = send(far_out, [], far_pairs)
    state = jax.ShapeDtypeStruct((horizon, width), F32)
    per_row = 4 * width * hidden
    tail, acc, top, total = pl.pallas_call(
        early_kernel,
        out_shape=[jax.ShapeDtypeStruct((4 * HALF, width), BF16), state, state, state],
        in_specs=[ANY] * 5 + [VMEM] * 6,
        out_specs=[VMEM] * 4,
        scratch_shapes=[
            pltpu.VMEM((11, HALF, width), BF16), pltpu.VMEM((9 * HALF, width), BF16), pltpu.SemaphoreType.DMA((3,))
        ],
        compiler_params=pltpu.CompilerParams(vmem_limit_bytes=32 * 1024 * 1024),
        cost_estimate=pl.CostEstimate(
            flops=(14 * per_row + 5 * 2 * per_row) * HALF, bytes_accessed=8 << 20, transcendentals=2 << 20
        ),
        name="early",
    )(own, got0, got1, near0, near1, taps, gains, up_v, down_v, kv_v, queries)
    lanes = width + 128
    payload = pl.pallas_call(
        late_kernel,
        out_shape=jax.ShapeDtypeStruct((horizon, lanes), BF16),
        in_specs=[ANY] * 3 + [VMEM] * 10,
        out_specs=VMEM,
        scratch_shapes=[
            pltpu.VMEM((5, HALF, width), BF16), pltpu.VMEM((7 * HALF, width), BF16), pltpu.SemaphoreType.DMA((2,))
        ],
        compiler_params=pltpu.CompilerParams(vmem_limit_bytes=32 * 1024 * 1024),
        cost_estimate=pl.CostEstimate(
            flops=(6 * per_row + 3 * 2 * per_row) * HALF, bytes_accessed=8 << 20, transcendentals=1 << 20
        ),
        name="late",
    )(own, far0, far1, tail, acc, top, total, taps, gains, up_v, down_v, kv_v, queries)
    parts = lax.all_to_all(payload, "tm", 0, 0, tiled=True)
    result = pl.pallas_call(
        final_kernel,
        out_shape=jax.ShapeDtypeStruct((share, width), BF16),
        in_specs=[VMEM] * 2,
        out_specs=VMEM,
        compiler_params=small(),
        name="final",
    )(parts, readout_v)
    return result[None]


def solution(mesh):
    placed = (P(("groups", "series"), "tm", None), P(), P(), P(), P(), P(), P(), P())
    return jax.shard_map(
        on_device,
        mesh=mesh,
        in_specs=placed,
        out_specs=P(("groups", "series"), "tm", None),
        check_vma=False,
    )
```

time: 48.8 us -> 52.5 us (1.076)
  blocking collectives: 0 us -> 13.7 us
  waiting for transfers between devices: 13.8 us -> 5.34 us
  Pallas kernels: 14.6 us -> 13.3 us
  starting transfers between devices: 14.8 us -> 13.7 us
  local copies, waits for them, and re-layouts: 5.13 us -> 5.87 us
    all_to_all x0 -> x1, blocking collectives: none -> 13.7 us  [on_device(): parts = lax.all_to_all(payload, 'tm', 0, 0, tiled=True)]
    ppermute x7 -> x6, waiting for transfers between devices: 13.8 us -> 5.34 us  [send(): return lax.ppermute(value, ('series', 'tm'), pairs)]
    ppermute x7 -> x6, starting transfers between devices: 14.8 us -> 13.7 us  [send(): return lax.ppermute(value, ('series', 'tm'), pairs)]
    pallas_call x4 -> x3, Pallas kernels: 5.99 us -> 5.2 us  [the longest x1 4.1 us: on_device(): pl.pallas_call(late_kernel, out_shape=jax.ShapeDtypeStruct((horizon, lane...]
    unnamed x17 -> x19, local copies, waits for them, and re-layouts: 5.13 us -> 5.87 us
  transfers between devices with their start and end apart: 7 -> 6, of which waited for: 4 -> 1; matrix products, arithmetic and copies ran while one was open for 1% -> 0% of each run, Pallas kernels for 18% -> 14%
where the time goes in v3:
time: 52.5 us; the launch traced here: 52.1 us
  starting transfers between devices  13.7 us (26%)
  blocking collectives  13.7 us (26%)
  Pallas kernels  13.3 us (25%)
  local copies, waits for them, and re-layouts  5.87 us (11%)
  waiting for transfers between devices  5.34 us (10%)
    ppermute x6, starting transfers between devices, send(): return lax.ppermute(value, ('series', 'tm'), pairs)  13.7 us
    all_to_all x1, blocking collectives, on_device(): parts = lax.all_to_all(payload, 'tm', 0, 0, tiled=True)  13.7 us
    pallas_call x1, Pallas kernels, on_device(): pl.pallas_call(early_kernel, out_shape=[jax.ShapeDtypeStruct((4 * HALF, w...  7.49 us
    unnamed x19, local copies, waits for them, and re-layouts  5.87 us
    ppermute x6, waiting for transfers between devices, send(): return lax.ppermute(value, ('series', 'tm'), pairs)  5.34 us
    pallas_call x1, Pallas kernels, on_device(): pl.pallas_call(late_kernel, out_shape=jax.ShapeDtypeStruct((horizon, lane...  4.1 us
  transfers between devices with their start and end apart: 6, of which 1 were waited for; matrix products, arithmetic and copies ran while one was open for 0% of the time, Pallas kernels for 14%

profile of v3, /device:TPU:0, one launch (start us, length us, event | category | flops | bytes accessed | tf_op | source)
XLA Modules:
  0.0 52.1 jit_solution(11729376256713762547)
XLA Ops:
  0.0 0.0 copy-start
  0.0 1.2 %copy-done = bf16[1,1024,512]{2,1,0:T(8,128)(2,1)S(1)} copy-done((bf16[1,1024,512]{2,1,0:T(8,128)(2,1)S(1)}, bf16[1,1024,512]{2,1,0:T(8,128)(2,1)}, u32[]{:S(2)}) %copy-start) | copy-done | bytes 1048600
  1.2 0.0 copy-start.1
  1.2 0.0 copy-start.4
  1.2 0.0 copy-start.5
  1.2 0.1 pack_halo.1
  1.4 0.1 pack_swap.1
  1.4 1.0 %copy-done.1 = bf16[1,1024,512]{2,1,0:T(8,128)(2,1)S(1)} copy-done((bf16[1,1024,512]{2,1,0:T(8,128)(2,1)S(1)}, bf16[1,1024,512]{2,1,0:T(8,128)(2,1)}, u32[]{:S(2)}) %copy-start.1) | copy-done | bytes 1048600
  2.5 0.3 copy-done.4
  2.8 0.1 copy-done.5
  2.9 0.0 copy-start.2
  2.9 1.6 %copy-done.2 = bf16[2,512,1024]{2,1,0:T(8,128)(2,1)S(1)} copy-done((bf16[2,512,1024]{2,1,0:T(8,128)(2,1)S(1)}, bf16[2,512,1024]{2,1,0:T(8,128)(2,1)}, u32[]{:S(2)}) %copy-start.2) | copy-done | bytes 2097176
  4.5 0.0 copy-start.3
  4.5 1.6 %copy-done.3 = bf16[2,1024,512]{2,1,0:T(8,128)(2,1)S(1)} copy-done((bf16[2,1024,512]{2,1,0:T(8,128)(2,1)S(1)}, bf16[2,1024,512]{2,1,0:T(8,128)(2,1)}, u32[]{:S(2)}) %copy-start.3) | copy-done | bytes 2097176
  6.1 0.0 copy-start.8
  6.1 0.0 copy-start.6
  6.1 0.0 copy-start.7
  6.1 0.5 stage.1
  6.6 0.7 %collective-permute-start.3 = (bf16[4,128,512]{2,1,0:T(8,128)(2,1)S(1)}, bf16[4,128,512]{2,1,0:T(8,128)(2,1)S(1)}, u32[]{:S(2)}, u32[]{:S(2)}) collective-permute-start(bf16[4,128,512]{2,1,0:T(8,128)(2,1)S(1)} %pack_swap.1), channel_id=1, source_target_pairs={{8,9},{9,8},{10,11},{11,10},{12,13},{13,12},{14,15},{15,14},{24,25... | collective-permute-start | bytes 1572872 | tf_op jit(solution)/shard_map/ppermute | solution.py:223
  7.3 4.8 %collective-permute-start.2 = (bf16[4,128,512]{2,1,0:T(8,128)(2,1)S(1)}, bf16[4,128,512]{2,1,0:T(8,128)(2,1)S(1)}, u32[]{:S(2)}, u32[]{:S(2)}) collective-permute-start(bf16[4,128,512]{2,1,0:T(8,128)(2,1)S(1)} %pack_swap.1), channel_id=1, source_target_pairs={{0,1},{1,0},{2,3},{3,2},{4,5},{5,4},{6,7},{7,6},{16,17},{17,16},{1... | collective-permute-start | bytes 1572872 | tf_op jit(solution)/shard_map/ppermute | solution.py:223
  12.1 0.7 %collective-permute-start.5 = (bf16[3,128,512]{2,1,0:T(8,128)(2,1)S(1)}, bf16[3,128,512]{2,1,0:T(8,128)(2,1)S(1)}, u32[]{:S(2)}, u32[]{:S(2)}) collective-permute-start(bf16[3,128,512]{2,1,0:T(8,128)(2,1)S(1)} %get-tuple-element.26), channel_id=1, source_target_pairs={{9,11},{11,13},{13,15},{8,14},{10,8},{12,10},{14,12},{25,27},{27,2... | collective-permute-start | bytes 1179656 | tf_op jit(solution)/shard_map/ppermute | solution.py:223
  12.8 5.5 %collective-permute-start.4 = (bf16[3,128,512]{2,1,0:T(8,128)(2,1)S(1)}, bf16[3,128,512]{2,1,0:T(8,128)(2,1)S(1)}, u32[]{:S(2)}, u32[]{:S(2)}) collective-permute-start(bf16[3,128,512]{2,1,0:T(8,128)(2,1)S(1)} %get-tuple-element.26), channel_id=1, source_target_pairs={{1,3},{3,5},{5,7},{0,6},{2,0},{4,2},{6,4},{17,19},{19,21},{21,23},... | collective-permute-start | bytes 1179656 | tf_op jit(solution)/shard_map/ppermute | solution.py:223
  18.3 1.3 %collective-permute-start = (bf16[3,128,512]{2,1,0:T(8,128)(2,1)S(1)}, bf16[3,128,512]{2,1,0:T(8,128)(2,1)S(1)}, u32[]{:S(2)}, u32[]{:S(2)}) collective-permute-start(bf16[3,128,512]{2,1,0:T(8,128)(2,1)S(1)} %get-tuple-element.24), channel_id=1, source_target_pairs={{1,2},{3,4},{5,6},{0,7},{2,1},{4,3},{6,5},{17,18},{19,20},{21,22},... | collective-permute-start | bytes 1179656 | tf_op jit(solution)/shard_map/ppermute | solution.py:223
  19.7 0.0 copy-done.8
  19.7 0.0 collective-permute-done.5.near1
  19.7 0.7 %collective-permute-start.1 = (bf16[3,128,512]{2,1,0:T(8,128)(2,1)S(1)}, bf16[3,128,512]{2,1,0:T(8,128)(2,1)S(1)}, u32[]{:S(2)}, u32[]{:S(2)}) collective-permute-start(bf16[3,128,512]{2,1,0:T(8,128)(2,1)S(1)} %get-tuple-element.24), channel_id=1, source_target_pairs={{9,10},{11,12},{13,14},{8,15},{10,9},{12,11},{14,13},{25,26},{27,2... | collective-permute-start | bytes 1179656 | tf_op jit(solution)/shard_map/ppermute | solution.py:223
  20.4 5.3 %collective-permute-done.4.near0 = bf16[3,128,512]{2,1,0:T(8,128)(2,1)S(1)} collective-permute-done((bf16[3,128,512]{2,1,0:T(8,128)(2,1)S(1)}, bf16[3,128,512]{2,1,0:T(8,128)(2,1)S(1)}, u32[]{:S(2)}, u32[]{:S(2)}) %collective-permute-start.4) | collective-permute-done | bytes 393248 | tf_op jit(solution)/shard_map/ppermute | solution.py:223
  25.7 0.0 collective-permute-done.3.got1
  25.7 0.0 collective-permute-done.2.got0
  25.7 0.0 copy-done.6
  25.7 0.0 copy-done.7
  25.7 7.5 %early.1 = (bf16[512,512]{1,0:T(8,128)(2,1)S(1)}, f32[128,512]{1,0:T(8,128)S(1)}, f32[128,512]{1,0:T(8,128)S(1)}, f32[128,512]{1,0:T(8,128)S(1)}) custom-call(bf16[4,128,512]{2,1,0:T(8,128)(2,1)S(1)} %get-tuple-element.23.own, bf16[4,128,512]{2,1,0:T(8,128)(2,1)S(1)} %collective-permute-done.2.got0, bf16[4,128,512]{2,1,0:T(8,128)(2,1)S(1)} %collective-permute-done.3.got1, ...), custom_call_target="tpu_custom_call" | custom-call | flops 6442450944 | bytes 8388608 | tf_op jit(solution)/shard_map/early/pallas_call | solution.py:263
  33.2 0.0 collective-permute-done.far0
  33.2 0.0 collective-permute-done.1.far1
  33.3 4.1 %late.1 = bf16[128,640]{1,0:T(8,128)(2,1)S(1)} custom-call(bf16[4,128,512]{2,1,0:T(8,128)(2,1)S(1)} %get-tuple-element.23.own, bf16[3,128,512]{2,1,0:T(8,128)(2,1)S(1)} %collective-permute-done.far0, bf16[3,128,512]{2,1,0:T(8,128)(2,1)S(1)} %collective-permute-done.1.far1, bf16[512,512]{1,0:T(8,128)(2,1)S(1)} %get-tuple-element.30.tail, ...), custom_call_target="tpu_custom_call" | custom-call | flops 3221225472 | bytes 8388608 | tf_op jit(solution)/shard_map/late/pallas_call | solution.py:278
  37.4 13.7 %all_to_all.11 = bf16[8,16,640]{2,1,0:T(8,128)(2,1)S(1)} all-to-all(bf16[8,16,640]{2,1,0:T(8,128)(2,1)S(1)} %bitcast.8), channel_id=1, replica_groups=mesh['groups'=2,'series'=2,'tm'=8] {'tm'}, dimensions={0} | all-to-all | bytes 327680 | tf_op jit(solution)/shard_map/all_to_all | solution.py:292
  51.1 1.0 %final.1 = bf16[16,512]{1,0:T(8,128)(2,1)} custom-call(bf16[128,640]{1,0:T(8,128)(2,1)S(1)} %bitcast.7, bf16[512,512]{1,0:T(8,128)(2,1)S(1)} %get-tuple-element.34.readout), custom_call_target="tpu_custom_call" | custom-call | tf_op jit(solution)/shard_map/final/pallas_call | solution.py:293
  (1 shorter events, 0.0 us)
Async XLA Ops:
  0.0 1.2 %copy-start = (bf16[1,1024,512]{2,1,0:T(8,128)(2,1)S(1)}, bf16[1,1024,512]{2,1,0:T(8,128)(2,1)}, u32[]{:S(2)}) copy-start(bf16[1,1024,512]{2,1,0:T(8,128)(2,1)} %param.8) | copy-start | bytes 3145732
  1.2 1.2 %copy-start.1 = (bf16[1,1024,512]{2,1,0:T(8,128)(2,1)S(1)}, bf16[1,1024,512]{2,1,0:T(8,128)(2,1)}, u32[]{:S(2)}) copy-start(bf16[1,1024,512]{2,1,0:T(8,128)(2,1)} %param.8) | copy-start | bytes 3145732
  1.2 1.5 %copy-start.4 = (bf16[512,1024]{1,0:T(8,128)(2,1)S(1)}, bf16[512,1024]{1,0:T(8,128)(2,1)}, u32[]{:S(2)}) copy-start(bf16[512,1024]{1,0:T(8,128)(2,1)} %refs_2_.1) | copy-start | bytes 3145732
  1.2 1.7 %copy-start.5 = (bf16[512,512]{1,0:T(8,128)(2,1)S(1)}, bf16[512,512]{1,0:T(8,128)(2,1)}, u32[]{:S(2)}) copy-start(bf16[512,512]{1,0:T(8,128)(2,1)} %refs_3_.1) | copy-start | bytes 1572868
  2.9 1.6 %copy-start.2 = (bf16[2,512,1024]{2,1,0:T(8,128)(2,1)S(1)}, bf16[2,512,1024]{2,1,0:T(8,128)(2,1)}, u32[]{:S(2)}) copy-start(bf16[2,512,1024]{2,1,0:T(8,128)(2,1)} %refs_0_.1) | copy-start | bytes 6291460
  4.5 1.6 %copy-start.3 = (bf16[2,1024,512]{2,1,0:T(8,128)(2,1)S(1)}, bf16[2,1024,512]{2,1,0:T(8,128)(2,1)}, u32[]{:S(2)}) copy-start(bf16[2,1024,512]{2,1,0:T(8,128)(2,1)} %refs_1_.1) | copy-start | bytes 6291460
  6.1 13.6 %copy-start.8 = (f32[2,3,512]{2,0,1:T(2,128)S(1)}, f32[2,3,512]{2,0,1:T(2,128)}, u32[]{:S(2)}) copy-start(f32[2,3,512]{2,0,1:T(2,128)} %param.9) | copy-start | bytes 36868
  6.1 19.6 %copy-start.6 = (bf16[128,512]{1,0:T(8,128)(2,1)S(1)}, bf16[128,512]{1,0:T(8,128)(2,1)}, u32[]{:S(2)}) copy-start(bf16[128,512]{1,0:T(8,128)(2,1)} %queries.3) | copy-start | bytes 393220
  6.1 19.6 %copy-start.7 = (f32[2,512]{1,0:T(2,128)S(1)}, f32[2,512]{1,0:T(2,128)}, u32[]{:S(2)}) copy-start(f32[2,512]{1,0:T(2,128)} %gains.3) | copy-start | bytes 12292
  6.6 19.1 %collective-permute-start.3 = (bf16[4,128,512]{2,1,0:T(8,128)(2,1)S(1)}, bf16[4,128,512]{2,1,0:T(8,128)(2,1)S(1)}, u32[]{:S(2)}, u32[]{:S(2)}) collective-permute-start(bf16[4,128,512]{2,1,0:T(8,128)(2,1)S(1)} %pack_swap.1), channel_id=1, source_target_pairs={{8,9},{9,8},{10,11},{11,10},{12,13},{13,12},{14,15},{15,14},{24,25... | collective-permute-start | bytes 1572872 | tf_op jit(solution)/shard_map/ppermute | solution.py:223
  7.3 18.4 %collective-permute-start.2 = (bf16[4,128,512]{2,1,0:T(8,128)(2,1)S(1)}, bf16[4,128,512]{2,1,0:T(8,128)(2,1)S(1)}, u32[]{:S(2)}, u32[]{:S(2)}) collective-permute-start(bf16[4,128,512]{2,1,0:T(8,128)(2,1)S(1)} %pack_swap.1), channel_id=1, source_target_pairs={{0,1},{1,0},{2,3},{3,2},{4,5},{5,4},{6,7},{7,6},{16,17},{17,16},{1... | collective-permute-start | bytes 1572872 | tf_op jit(solution)/shard_map/ppermute | solution.py:223
  12.1 7.6 %collective-permute-start.5 = (bf16[3,128,512]{2,1,0:T(8,128)(2,1)S(1)}, bf16[3,128,512]{2,1,0:T(8,128)(2,1)S(1)}, u32[]{:S(2)}, u32[]{:S(2)}) collective-permute-start(bf16[3,128,512]{2,1,0:T(8,128)(2,1)S(1)} %get-tuple-element.26), channel_id=1, source_target_pairs={{9,11},{11,13},{13,15},{8,14},{10,8},{12,10},{14,12},{25,27},{27,2... | collective-permute-start | bytes 1179656 | tf_op jit(solution)/shard_map/ppermute | solution.py:223
  12.8 12.9 %collective-permute-start.4 = (bf16[3,128,512]{2,1,0:T(8,128)(2,1)S(1)}, bf16[3,128,512]{2,1,0:T(8,128)(2,1)S(1)}, u32[]{:S(2)}, u32[]{:S(2)}) collective-permute-start(bf16[3,128,512]{2,1,0:T(8,128)(2,1)S(1)} %get-tuple-element.26), channel_id=1, source_target_pairs={{1,3},{3,5},{5,7},{0,6},{2,0},{4,2},{6,4},{17,19},{19,21},{21,23},... | collective-permute-start | bytes 1179656 | tf_op jit(solution)/shard_map/ppermute | solution.py:223
  18.3 14.9 %collective-permute-start = (bf16[3,128,512]{2,1,0:T(8,128)(2,1)S(1)}, bf16[3,128,512]{2,1,0:T(8,128)(2,1)S(1)}, u32[]{:S(2)}, u32[]{:S(2)}) collective-permute-start(bf16[3,128,512]{2,1,0:T(8,128)(2,1)S(1)} %get-tuple-element.24), channel_id=1, source_target_pairs={{1,2},{3,4},{5,6},{0,7},{2,1},{4,3},{6,5},{17,18},{19,20},{21,22},... | collective-permute-start | bytes 1179656 | tf_op jit(solution)/shard_map/ppermute | solution.py:223
  19.7 13.6 %collective-permute-start.1 = (bf16[3,128,512]{2,1,0:T(8,128)(2,1)S(1)}, bf16[3,128,512]{2,1,0:T(8,128)(2,1)S(1)}, u32[]{:S(2)}, u32[]{:S(2)}) collective-permute-start(bf16[3,128,512]{2,1,0:T(8,128)(2,1)S(1)} %get-tuple-element.24), channel_id=1, source_target_pairs={{9,10},{11,12},{13,14},{8,15},{10,9},{12,11},{14,13},{25,26},{27,2... | collective-permute-start | bytes 1179656 | tf_op jit(solution)/shard_map/ppermute | solution.py:223

commit v4 on v2

--- a/solution.py
+++ b/solution.py
@@ -21,7 +21,8 @@
 
 
 def gelu(u):
-    return 0.5 * u * (1.0 + jnp.tanh(0.7978845608028654 * (u + 0.044715 * (u * u * u))))
+    half = 0.5 * u
+    return half + half * jnp.tanh(u * (0.7978845608028654 + (0.7978845608028654 * 0.044715) * (u * u)))
 
 
 def mix(src, first, steps, dilation, taps, gain, up, down, factors):
@@ -45,14 +46,17 @@
     horizon, width = queries.shape
     low = lax.broadcasted_iota(jnp.int32, (horizon, 128), 1) < 64
     zero = jnp.zeros((horizon, 128), BF16)
-    acc, top, total = [], [], []
+    acc, top, total, scores = [], [], [], []
     for p in range(width // 128):
         lanes = slice(128 * p, 128 * p + 128)
         q = queries[:, lanes] * jnp.asarray(0.125, BF16)
         q2 = jnp.concatenate([jnp.where(low, q, zero), jnp.where(low, zero, q)], 0)
-        scores = lax.dot_general(q2, pairs[:, lanes], (((1,), (1,)), ((), ())), preferred_element_type=F32)
-        m = jnp.max(scores, axis=-1, keepdims=True)
-        e = jnp.exp(scores - m)
+        scores.append(
+            lax.dot_general(q2, pairs[:, lanes], (((1,), (1,)), ((), ())), preferred_element_type=F32)
+        )
+    for p in range(width // 128):
+        m = jnp.max(scores[p], axis=-1, keepdims=True)
+        e = jnp.exp(scores[p] - m)
         s = jnp.sum(e, axis=-1, keepdims=True)
         c = dot(e.astype(BF16), pairs[:, width + 128 * p : width + 128 * p + 128])
         acc.append(jnp.where(low, c[:horizon], c[horizon:]))
@@ -126,8 +130,7 @@
     acc[...], top[...], total[...] = attend(x2, kv_v[...], queries[...])
 
 
-def late_kernel(own, far, tail, acc, top, total, taps, gains, up_v, down_v, kv_v, queries, *refs):
-    outs, (x0, x1, sem) = refs[:-3], refs[-3:]
+def late_kernel(own, far, tail, acc, top, total, taps, gains, up_v, down_v, kv_v, queries, out, x0, x1, sem):
     side = lax.rem(lax.axis_index("tm"), 2)
     copies = [
         pltpu.make_async_copy(own.at[pl.ds(2 * side, 2)], x0.at[pl.ds(3 - 3 * side, 2)], sem.at[0]),
@@ -149,13 +152,7 @@
     a, b = jnp.exp(top[...] - best), jnp.exp(top2 - best)
     whole = total[...] * a + total2 * b
     rows = encode((acc[...] * a + acc2 * b) / whole, best + jnp.log(whole))
-    if len(outs) == 1:
-        outs[0][...] = rows
-        return
-    n_pairs, share, lanes = outs[0].shape
-    split = rows.reshape(n_pairs, 2, share, lanes)
-    outs[0][...] = jnp.where(side == 0, split[:, 0], split[:, 1])
-    outs[1][...] = jnp.where(side == 0, split[:, 1], split[:, 0])
+    out[...] = rows
 
 
 def pack_kernel(n, hist, *refs):
@@ -183,28 +180,13 @@
         copy.wait()
 
 
-def pair_kernel(mine, theirs, *refs):
-    shape = mine.shape
-    flat = (shape[0] * shape[1], shape[2])
-    spread = spread_matrix(shape[2] - 128)
-    context, lse = combine([
-        decode(mine[...].reshape(flat), spread), decode(theirs[...].reshape(flat), spread)
-    ])
-    merged = encode(context, lse).reshape(shape)
-    if len(refs) == 1:
-        refs[0][...] = merged
-        return
-    held = refs[-1]
-    held[...] = merged
-    pair = lax.div(lax.axis_index("tm"), 2)
-    for s, out in enumerate(refs[:-1]):
-        out[...] = held[pair ^ s]
-
-
-def final_kernel(count, *refs):
-    parts, readout, out = refs[:count], refs[count], refs[count + 1]
-    spread = spread_matrix(out.shape[1])
-    context, _ = combine([decode(part[...], spread) for part in parts])
+def final_kernel(parts, readout, out):
+    share, width = out.shape
+    rows = parts[...]
+    context, lse = decode(rows, spread_matrix(width))
+    count = rows.shape[0] // share
+    cut = [slice(i * share, (i + 1) * share) for i in range(count)]
+    context, _ = combine([(context[c], lse[c]) for c in cut])
     out[...] = dot(context.astype(BF16), readout[...]).astype(BF16)
 
 
@@ -216,8 +198,6 @@
     _, span, width = history.shape
     horizon, hidden = queries.shape[0], up.shape[-1]
     count = lax.axis_size("tm")
-    here = lax.axis_index("tm")
-    side, pair = lax.rem(here, 2), lax.div(here, 2)
     n_pairs = count // 2
     share = horizon // count
 
@@ -277,14 +257,11 @@
         name="early",
     )(own, got, near, taps, gains, up_v, down_v, kv_v, queries)
     lanes = width + 128
-    fused = share % 16 == 0 and n_pairs <= 4 and n_pairs & (n_pairs - 1) == 0
-    one = jax.ShapeDtypeStruct((share, lanes), BF16)
-    quarter = jax.ShapeDtypeStruct((n_pairs, share, lanes), BF16)
     payload = pl.pallas_call(
         late_kernel,
-        out_shape=[quarter, quarter] if fused else [jax.ShapeDtypeStruct((horizon, lanes), BF16)],
+        out_shape=jax.ShapeDtypeStruct((horizon, lanes), BF16),
         in_specs=[ANY] * 2 + [VMEM] * 10,
-        out_specs=[VMEM] * (2 if fused else 1),
+        out_specs=VMEM,
         scratch_shapes=[
             pltpu.VMEM((5, HALF, width), BF16), pltpu.VMEM((7 * HALF, width), BF16), pltpu.SemaphoreType.DMA((2,))
         ],
@@ -294,37 +271,15 @@
         ),
         name="late",
     )(own, far, tail, acc, top, total, taps, gains, up_v, down_v, kv_v, queries)
-    if fused:
-        mine, send = payload
-    else:
-        split = payload[0].reshape(n_pairs, 2, share, lanes)
-        mine, send = (lax.dynamic_index_in_dim(split, s, 1, False) for s in (side, 1 - side))
-    theirs = lax.ppermute(send, "tm", swap)
-    merged = pl.pallas_call(
-        pair_kernel,
-        out_shape=[one] * n_pairs if fused else [quarter],
+    parts = lax.all_to_all(payload, "tm", 0, 0, tiled=True)
+    result = pl.pallas_call(
+        final_kernel,
+        out_shape=jax.ShapeDtypeStruct((share, width), BF16),
         in_specs=[VMEM] * 2,
-        out_specs=[VMEM] * (n_pairs if fused else 1),
-        scratch_shapes=[pltpu.VMEM(quarter.shape, BF16)] if fused else [],
-        compiler_params=small(),
-        name="pair",
-    )(mine, theirs)
-    if fused:
-        parts = [merged[0]] + [
-            lax.ppermute(merged[s], "tm", [(i, i ^ (2 * s)) for i in range(count)]) for s in range(1, n_pairs)
-        ]
-    else:
-        groups = [[2 * p + s for p in range(n_pairs)] for s in range(2)]
-        swapped = lax.all_to_all(merged[0], "tm", 0, 0, axis_index_groups=groups, tiled=True)
-        parts = [swapped[p] for p in range(n_pairs)]
-    result = pl.pallas_call(
-        functools.partial(final_kernel, len(parts)),
-        out_shape=jax.ShapeDtypeStruct((share, width), BF16),
-        in_specs=[VMEM] * (len(parts) + 1),
         out_specs=VMEM,
         compiler_params=small(),
         name="final",
-    )(*parts, readout_v)
+    )(parts, readout_v)
     return result[None]
 
 

time: 48.8 us -> 45.7 us (0.936)
  blocking collectives: 0 us -> 13.3 us
  waiting for transfers between devices: 13.8 us -> 3.82 us
  starting transfers between devices: 14.8 us -> 9.83 us
  Pallas kernels: 14.6 us -> 13.3 us
    all_to_all x0 -> x1, blocking collectives: none -> 13.3 us  [on_device(): parts = lax.all_to_all(payload, 'tm', 0, 0, tiled=True)]
    ppermute x4 -> x0, waiting for transfers between devices: 10 us -> none  [the longest x3 5.58 us: on_device(): lax.ppermute(merged[s], 'tm', [(i, i ^ 2 * s) for i in range(count)])]
    ppermute x4 -> x0, starting transfers between devices: 4.99 us -> none  [the longest x3 4.92 us: on_device(): lax.ppermute(merged[s], 'tm', [(i, i ^ 2 * s) for i in range(count)])]
    pallas_call x3 -> x2, Pallas kernels: 5.95 us -> 5.15 us  [the longest x1 4.11 us: on_device(): pl.pallas_call(late_kernel, out_shape=jax.ShapeDtypeStruct((horizon, lane...]
    pallas_call x1, Pallas kernels: 7.99 us -> 7.47 us  [on_device(): pl.pallas_call(early_kernel, out_shape=[jax.ShapeDtypeStruct((4 * HALF, w...]
  transfers between devices with their start and end apart: 7 -> 3, of which waited for: 4 -> 1; matrix products, arithmetic and copies ran while one was open for 1% -> 2% of each run, Pallas kernels for 18% -> 18%
where the time goes in v4:
time: 45.7 us; the launch traced here: 45.4 us
  Pallas kernels  13.3 us (29%)
  blocking collectives  13.3 us (29%)
  starting transfers between devices  9.83 us (22%)
  local copies, waits for them, and re-layouts  5.13 us (11%)
  waiting for transfers between devices  3.82 us (8%)
    all_to_all x1, blocking collectives, on_device(): parts = lax.all_to_all(payload, 'tm', 0, 0, tiled=True)  13.3 us
    pallas_call x1, Pallas kernels, on_device(): pl.pallas_call(early_kernel, out_shape=[jax.ShapeDtypeStruct((4 * HALF, w...  7.47 us
    ppermute x1, starting transfers between devices, on_device(): near = lax.ppermute(near_out, 'tm', near_pairs)  5.51 us
    unnamed x17, local copies, waits for them, and re-layouts  5.13 us
    pallas_call x1, Pallas kernels, on_device(): pl.pallas_call(late_kernel, out_shape=jax.ShapeDtypeStruct((horizon, lane...  4.11 us
    ppermute x1, waiting for transfers between devices, on_device(): near = lax.ppermute(near_out, 'tm', near_pairs)  3.81 us
    ppermute x1, starting transfers between devices, on_device(): got = lax.ppermute(swap_out, 'tm', swap)  3 us
    ppermute x1, starting transfers between devices, on_device(): far = lax.ppermute(far_out, 'tm', far_pairs)  1.31 us
  transfers between devices with their start and end apart: 3, of which 1 were waited for; matrix products, arithmetic and copies ran while one was open for 2% of the time, Pallas kernels for 18%

profile of v4, /device:TPU:0, one launch (start us, length us, event | category | flops | bytes accessed | tf_op | source)
XLA Modules:
  0.0 45.4 jit_solution(13516267248690892030)
XLA Ops:
  0.0 0.0 copy-start
  0.0 1.2 %copy-done = bf16[1,1024,512]{2,1,0:T(8,128)(2,1)S(1)} copy-done((bf16[1,1024,512]{2,1,0:T(8,128)(2,1)S(1)}, bf16[1,1024,512]{2,1,0:T(8,128)(2,1)}, u32[]{:S(2)}) %copy-start) | copy-done | bytes 1048600
  1.2 0.0 copy-start.1
  1.2 0.0 copy-start.4
  1.2 0.0 copy-start.5
  1.3 3.0 %collective-permute-start.1 = (bf16[4,128,512]{2,1,0:T(8,128)(2,1)S(1)}, bf16[4,128,512]{2,1,0:T(8,128)(2,1)S(1)}, u32[]{:S(2)}, u32[]{:S(2)}) collective-permute-start(bf16[4,128,512]{2,1,0:T(8,128)(2,1)S(1)} %pack_swap.1), channel_id=1, source_target_pairs={{0,1},{1,0},{2,3},{3,2},{4,5},{5,4},{6,7},{7,6},{8,9},{9,8},{10,11... | collective-permute-start | bytes 1572872 | tf_op jit(solution)/shard_map/ppermute | solution.py:220
  4.3 0.1 pack_halo.1
  4.4 5.5 %collective-permute-start.2 = (bf16[3,128,512]{2,1,0:T(8,128)(2,1)S(1)}, bf16[3,128,512]{2,1,0:T(8,128)(2,1)S(1)}, u32[]{:S(2)}, u32[]{:S(2)}) collective-permute-start(bf16[3,128,512]{2,1,0:T(8,128)(2,1)S(1)} %get-tuple-element.18), channel_id=1, source_target_pairs={{1,3},{3,5},{5,7},{0,6},{2,0},{4,2},{6,4},{9,11},{11,13},{13,15},{... | collective-permute-start | bytes 1179656 | tf_op jit(solution)/shard_map/ppermute | solution.py:230
  10.0 1.3 %collective-permute-start = (bf16[3,128,512]{2,1,0:T(8,128)(2,1)S(1)}, bf16[3,128,512]{2,1,0:T(8,128)(2,1)S(1)}, u32[]{:S(2)}, u32[]{:S(2)}) collective-permute-start(bf16[3,128,512]{2,1,0:T(8,128)(2,1)S(1)} %get-tuple-element.17), channel_id=1, source_target_pairs={{1,2},{3,4},{5,6},{0,7},{2,1},{4,3},{6,5},{9,10},{11,12},{13,14},{... | collective-permute-start | bytes 1179656 | tf_op jit(solution)/shard_map/ppermute | solution.py:231
  11.3 0.7 %copy.9.taps = f32[2,3,512]{2,1,0:T(4,128)S(1)} copy(f32[2,3,512]{2,0,1:T(2,128)} %param.9) | data formatting | bytes 24576 | tf_op args[1]
  12.0 0.0 copy-done.1
  12.0 0.0 copy-done.4
  12.0 0.0 copy-done.5
  12.0 0.0 copy-start.2
  12.0 1.6 %copy-done.2 = bf16[2,512,1024]{2,1,0:T(8,128)(2,1)S(1)} copy-done((bf16[2,512,1024]{2,1,0:T(8,128)(2,1)S(1)}, bf16[2,512,1024]{2,1,0:T(8,128)(2,1)}, u32[]{:S(2)}) %copy-start.2) | copy-done | bytes 2097176
  13.6 0.0 copy-start.3
  13.6 1.6 %copy-done.3 = bf16[2,1024,512]{2,1,0:T(8,128)(2,1)S(1)} copy-done((bf16[2,1024,512]{2,1,0:T(8,128)(2,1)S(1)}, bf16[2,1024,512]{2,1,0:T(8,128)(2,1)}, u32[]{:S(2)}) %copy-start.3) | copy-done | bytes 2097176
  15.2 0.0 copy-start.6
  15.2 0.0 copy-start.7
  15.2 0.5 %stage.1 = (bf16[4,128,512]{2,1,0:T(8,128)(2,1)S(1)}, bf16[2,512,1024]{2,1,0:T(8,128)(2,1)S(1)}, bf16[2,1024,512]{2,1,0:T(8,128)(2,1)S(1)}, bf16[512,1024]{1,0:T(8,128)(2,1)S(1)}, bf16[512,512]{1,0:T(8,128)(2,1)S(1)}) custom-call(bf16[4,256,512]{2,1,0:T(8,128)(2,1)S(1)} %bitcast.6, bf16[2,512,1024]{2,1,0:T(8,128)(2,1)S(1)} %copy-done.2, ...), custom_call_target="tpu_custom_call" | custom-call | tf_op jit(solution)/shard_map/stage/pallas_call | solution.py:233
  15.7 3.8 %collective-permute-done.2.near = bf16[3,128,512]{2,1,0:T(8,128)(2,1)S(1)} collective-permute-done((bf16[3,128,512]{2,1,0:T(8,128)(2,1)S(1)}, bf16[3,128,512]{2,1,0:T(8,128)(2,1)S(1)}, u32[]{:S(2)}, u32[]{:S(2)}) %collective-permute-start.2) | collective-permute-done | bytes 393248 | tf_op jit(solution)/shard_map/ppermute | solution.py:230
  19.5 0.0 collective-permute-done.1.got
  19.5 0.0 copy-done.6
  19.5 0.0 copy-done.7
  19.5 7.5 %early.1 = (bf16[512,512]{1,0:T(8,128)(2,1)S(1)}, f32[128,512]{1,0:T(8,128)S(1)}, f32[128,512]{1,0:T(8,128)S(1)}, f32[128,512]{1,0:T(8,128)S(1)}) custom-call(bf16[4,128,512]{2,1,0:T(8,128)(2,1)S(1)} %get-tuple-element.16.own, bf16[4,128,512]{2,1,0:T(8,128)(2,1)S(1)} %collective-permute-done.1.got, bf16[3,128,512]{2,1,0:T(8,128)(2,1)S(1)} %collective-permute-done.2.near, ...), custom_call_target="tpu_custom_call" | custom-call | flops 6442450944 | bytes 8388608 | tf_op jit(solution)/shard_map/early/pallas_call | solution.py:245
  27.0 0.0 collective-permute-done.far
  27.0 4.1 %late.1 = bf16[128,640]{1,0:T(8,128)(2,1)S(1)} custom-call(bf16[4,128,512]{2,1,0:T(8,128)(2,1)S(1)} %get-tuple-element.16.own, bf16[3,128,512]{2,1,0:T(8,128)(2,1)S(1)} %collective-permute-done.far, bf16[512,512]{1,0:T(8,128)(2,1)S(1)} %get-tuple-element.22.tail, f32[128,512]{1,0:T(8,128)S(1)} %get-tuple-element.23.acc, ...), custom_call_target="tpu_custom_call" | custom-call | flops 3221225472 | bytes 8388608 | tf_op jit(solution)/shard_map/late/pallas_call | solution.py:260
  31.1 13.3 %all_to_all.11 = bf16[8,16,640]{2,1,0:T(8,128)(2,1)S(1)} all-to-all(bf16[8,16,640]{2,1,0:T(8,128)(2,1)S(1)} %bitcast.8), channel_id=1, replica_groups=mesh['groups'=2,'series'=2,'tm'=8] {'tm'}, dimensions={0} | all-to-all | bytes 327680 | tf_op jit(solution)/shard_map/all_to_all | solution.py:274
  44.4 1.0 %final.1 = bf16[16,512]{1,0:T(8,128)(2,1)} custom-call(bf16[128,640]{1,0:T(8,128)(2,1)S(1)} %bitcast.7, bf16[512,512]{1,0:T(8,128)(2,1)S(1)} %get-tuple-element.26.readout), custom_call_target="tpu_custom_call" | custom-call | tf_op jit(solution)/shard_map/final/pallas_call | solution.py:275
  (1 shorter events, 0.0 us)
Async XLA Ops:
  0.0 1.2 %copy-start = (bf16[1,1024,512]{2,1,0:T(8,128)(2,1)S(1)}, bf16[1,1024,512]{2,1,0:T(8,128)(2,1)}, u32[]{:S(2)}) copy-start(bf16[1,1024,512]{2,1,0:T(8,128)(2,1)} %param.8) | copy-start | bytes 3145732
  1.2 10.8 %copy-start.1 = (bf16[1,1024,512]{2,1,0:T(8,128)(2,1)S(1)}, bf16[1,1024,512]{2,1,0:T(8,128)(2,1)}, u32[]{:S(2)}) copy-start(bf16[1,1024,512]{2,1,0:T(8,128)(2,1)} %param.8) | copy-start | bytes 3145732
  1.2 10.8 %copy-start.4 = (bf16[512,1024]{1,0:T(8,128)(2,1)S(1)}, bf16[512,1024]{1,0:T(8,128)(2,1)}, u32[]{:S(2)}) copy-start(bf16[512,1024]{1,0:T(8,128)(2,1)} %refs_2_.1) | copy-start | bytes 3145732
  1.2 10.8 %copy-start.5 = (bf16[512,512]{1,0:T(8,128)(2,1)S(1)}, bf16[512,512]{1,0:T(8,128)(2,1)}, u32[]{:S(2)}) copy-start(bf16[512,512]{1,0:T(8,128)(2,1)} %refs_3_.1) | copy-start | bytes 1572868
  1.3 18.2 %collective-permute-start.1 = (bf16[4,128,512]{2,1,0:T(8,128)(2,1)S(1)}, bf16[4,128,512]{2,1,0:T(8,128)(2,1)S(1)}, u32[]{:S(2)}, u32[]{:S(2)}) collective-permute-start(bf16[4,128,512]{2,1,0:T(8,128)(2,1)S(1)} %pack_swap.1), channel_id=1, source_target_pairs={{0,1},{1,0},{2,3},{3,2},{4,5},{5,4},{6,7},{7,6},{8,9},{9,8},{10,11... | collective-permute-start | bytes 1572872 | tf_op jit(solution)/shard_map/ppermute | solution.py:220
  4.4 15.1 %collective-permute-start.2 = (bf16[3,128,512]{2,1,0:T(8,128)(2,1)S(1)}, bf16[3,128,512]{2,1,0:T(8,128)(2,1)S(1)}, u32[]{:S(2)}, u32[]{:S(2)}) collective-permute-start(bf16[3,128,512]{2,1,0:T(8,128)(2,1)S(1)} %get-tuple-element.18), channel_id=1, source_target_pairs={{1,3},{3,5},{5,7},{0,6},{2,0},{4,2},{6,4},{9,11},{11,13},{13,15},{... | collective-permute-start | bytes 1179656 | tf_op jit(solution)/shard_map/ppermute | solution.py:230
  10.0 17.0 %collective-permute-start = (bf16[3,128,512]{2,1,0:T(8,128)(2,1)S(1)}, bf16[3,128,512]{2,1,0:T(8,128)(2,1)S(1)}, u32[]{:S(2)}, u32[]{:S(2)}) collective-permute-start(bf16[3,128,512]{2,1,0:T(8,128)(2,1)S(1)} %get-tuple-element.17), channel_id=1, source_target_pairs={{1,2},{3,4},{5,6},{0,7},{2,1},{4,3},{6,5},{9,10},{11,12},{13,14},{... | collective-permute-start | bytes 1179656 | tf_op jit(solution)/shard_map/ppermute | solution.py:231
  12.0 1.6 %copy-start.2 = (bf16[2,512,1024]{2,1,0:T(8,128)(2,1)S(1)}, bf16[2,512,1024]{2,1,0:T(8,128)(2,1)}, u32[]{:S(2)}) copy-start(bf16[2,512,1024]{2,1,0:T(8,128)(2,1)} %refs_0_.1) | copy-start | bytes 6291460
  13.6 1.6 %copy-start.3 = (bf16[2,1024,512]{2,1,0:T(8,128)(2,1)S(1)}, bf16[2,1024,512]{2,1,0:T(8,128)(2,1)}, u32[]{:S(2)}) copy-start(bf16[2,1024,512]{2,1,0:T(8,128)(2,1)} %refs_1_.1) | copy-start | bytes 6291460
  15.2 4.3 %copy-start.6 = (bf16[128,512]{1,0:T(8,128)(2,1)S(1)}, bf16[128,512]{1,0:T(8,128)(2,1)}, u32[]{:S(2)}) copy-start(bf16[128,512]{1,0:T(8,128)(2,1)} %queries.3) | copy-start | bytes 393220
  15.2 4.3 %copy-start.7 = (f32[2,512]{1,0:T(2,128)S(1)}, f32[2,512]{1,0:T(2,128)}, u32[]{:S(2)}) copy-start(f32[2,512]{1,0:T(2,128)} %gains.3) | copy-start | bytes 12292

commit v5 on v4

--- a/solution.py
+++ b/solution.py
@@ -25,23 +25,23 @@
     return half + half * jnp.tanh(u * (0.7978845608028654 + (0.7978845608028654 * 0.044715) * (u * u)))
 
 
-def mix(src, first, steps, dilation, taps, gain, up, down, factors):
+def mix(src, first, steps, dilation, taps, gain, up, down, reach=None):
     rows, kept = [], []
     for j in range(steps):
-        w1, w2 = factors[j]
-        at = [(first + j - k * dilation) * HALF for k in range(3)]
-        now = src[at[0] : at[0] + HALF, :].astype(F32)
-        conv = taps[0:1, :] * now
-        conv = conv + (taps[1:2, :] * w1) * src[at[1] : at[1] + HALF, :].astype(F32)
-        conv = conv + (taps[2:3, :] * w2) * src[at[2] : at[2] + HALF, :].astype(F32)
+        conv = None
+        for k in range(reach[j] if reach else 3):
+            at = (first + j - k * dilation) * HALF
+            value = src[at : at + HALF, :].astype(F32)
+            if k == 0:
+                kept.append(value)
+            conv = taps[k : k + 1, :] * value if k == 0 else conv + taps[k : k + 1, :] * value
         scale = lax.rsqrt(jnp.mean(conv * conv, axis=-1, keepdims=True) + 1e-05)
         rows.append((conv * scale * gain).astype(BF16))
-        kept.append(now)
     inner = gelu(dot(jnp.concatenate(rows, 0), up)).astype(BF16)
     return (jnp.concatenate(kept, 0) + dot(inner, down)).astype(BF16)
 
 
-def attend(x2, w_kv, queries):
+def attend(x2, w_kv, queries, absent=None):
     pairs = dot(x2, w_kv).astype(BF16)
     horizon, width = queries.shape
     low = lax.broadcasted_iota(jnp.int32, (horizon, 128), 1) < 64
@@ -54,6 +54,10 @@
         scores.append(
             lax.dot_general(q2, pairs[:, lanes], (((1,), (1,)), ((), ())), preferred_element_type=F32)
         )
+    if absent is not None:
+        row = lax.broadcasted_iota(jnp.int32, (1, x2.shape[0]), 1)
+        bias = jnp.where(row < absent, 0.0, -1e30).astype(F32)
+        scores = [s + bias for s in scores]
     for p in range(width // 128):
         m = jnp.max(scores[p], axis=-1, keepdims=True)
         e = jnp.exp(scores[p] - m)
@@ -97,9 +101,17 @@
     return context / total, top + jnp.log(total)
 
 
-def valid(side):
-    here, count = lax.axis_index("tm"), lax.axis_size("tm")
-    return jnp.where(here == count - 2 + side, 0.0, 1.0).astype(F32)
+def join(a, b):
+    best = jnp.maximum(a[1], b[1])
+    wa, wb = jnp.exp(a[1] - best), jnp.exp(b[1] - best)
+    return a[0] * wa + b[0] * wb, best, a[2] * wa + b[2] * wb
+
+
+def first_steps(x1, taps, gains, up_v, down_v, kv_v, queries, state):
+    x2 = mix(x1, 1, 3, 2, taps[1], gains[1:2, :], up_v[1], down_v[1], (1, 1, 2))
+    added = join([ref[...] for ref in state], attend(x2, kv_v[...], queries[...]))
+    for ref, value in zip(state, added):
+        ref[...] = value
 
 
 def early_kernel(own, got, near, taps, gains, up_v, down_v, kv_v, queries, tail, acc, top, total,
@@ -112,25 +124,26 @@
     ]
     for copy in copies:
         copy.start()
-    v = valid(0)
-    one = 1.0
     for copy in copies:
         copy.wait()
     rows0 = x0.reshape(11 * HALF, x0.shape[-1])
     for j in range(0, 9, 3):
-        factors = [(v, v), (one, v), (one, one)] if j == 6 else [(one, one)] * 3
-        x1[j * HALF : (j + 3) * HALF, :] = mix(
-            rows0, j + 2, 3, 1, taps[0], gains[0:1, :], up_v[0], down_v[0], factors
-        )
+        x1[j * HALF : (j + 3) * HALF, :] = mix(rows0, j + 2, 3, 1, taps[0], gains[0:1, :], up_v[0], down_v[0])
     tail[...] = x1[pl.ds(pl.multiple_of(side * (5 * HALF), HALF), 4 * HALF), :]
     x2 = jnp.concatenate([
-        mix(x1, 4, 2, 2, taps[1], gains[1:2, :], up_v[1], down_v[1], [(one, one)] * 2),
-        mix(x1, 6, 3, 2, taps[1], gains[1:2, :], up_v[1], down_v[1], [(v, v), (v, v), (one, v)]),
+        mix(x1, 4, 2, 2, taps[1], gains[1:2, :], up_v[1], down_v[1]),
+        mix(x1, 6, 3, 2, taps[1], gains[1:2, :], up_v[1], down_v[1]),
     ], 0)
-    acc[...], top[...], total[...] = attend(x2, kv_v[...], queries[...])
-
-
-def late_kernel(own, far, tail, acc, top, total, taps, gains, up_v, down_v, kv_v, queries, out, x0, x1, sem):
+    here, count = lax.axis_index("tm"), lax.axis_size("tm")
+    absent = jnp.where(here == count - 2, 2 * HALF, 5 * HALF)
+    acc[...], top[...], total[...] = attend(x2, kv_v[...], queries[...], absent)
+
+    @pl.when(here == 1)
+    def _():
+        first_steps(x1, taps, gains, up_v, down_v, kv_v, queries, (acc, top, total))
+
+
+def late_kernel(own, far, tail, acc, top, total, taps, gains, up_v, down_v, kv_v, queries, out, x0, x1, acc2, top2, total2, sem):
     side = lax.rem(lax.axis_index("tm"), 2)
     copies = [
         pltpu.make_async_copy(own.at[pl.ds(2 * side, 2)], x0.at[pl.ds(3 - 3 * side, 2)], sem.at[0]),
@@ -139,20 +152,23 @@
     for copy in copies:
         copy.start()
     x1[pl.ds(pl.multiple_of((3 - 3 * side) * HALF, HALF), 4 * HALF), :] = tail[...]
-    v = valid(1)
-    one = 1.0
     for copy in copies:
         copy.wait()
     rows0 = x0.reshape(5 * HALF, x0.shape[-1])
-    fresh = mix(rows0, 2, 3, 1, taps[0], gains[0:1, :], up_v[0], down_v[0], [(v, v), (one, v), (one, one)])
+    fresh = mix(rows0, 2, 3, 1, taps[0], gains[0:1, :], up_v[0], down_v[0])
     x1[pl.ds(pl.multiple_of(side * (4 * HALF), HALF), 3 * HALF), :] = fresh
-    x2 = mix(x1, 4, 3, 2, taps[1], gains[1:2, :], up_v[1], down_v[1], [(v, v), (v, v), (one, v)])
-    acc2, top2, total2 = attend(x2, kv_v[...], queries[...])
-    best = jnp.maximum(top[...], top2)
-    a, b = jnp.exp(top[...] - best), jnp.exp(top2 - best)
-    whole = total[...] * a + total2 * b
-    rows = encode((acc[...] * a + acc2 * b) / whole, best + jnp.log(whole))
-    out[...] = rows
+    x2 = mix(x1, 4, 3, 2, taps[1], gains[1:2, :], up_v[1], down_v[1])
+    here, count = lax.axis_index("tm"), lax.axis_size("tm")
+    absent = jnp.where(here == count - 1, 0, 3 * HALF)
+    acc2[...], top2[...], total2[...] = join(
+        (acc[...], top[...], total[...]), attend(x2, kv_v[...], queries[...], absent)
+    )
+
+    @pl.when(here == 0)
+    def _():
+        first_steps(x1, taps, gains, up_v, down_v, kv_v, queries, (acc2, top2, total2))
+
+    out[...] = encode(acc2[...] / total2[...], top2[...] + jnp.log(total2[...]))
 
 
 def pack_kernel(n, hist, *refs):
@@ -204,7 +220,7 @@
     hist = history.reshape(span // STEP, STEP, width)
     swap = [(i, i ^ 1) for i in range(count)]
     ahead = [(2 * p + 1, 2 * p + 2) for p in range(n_pairs - 1)]
-    behind = [(2 * p, (2 * p - 2) % count) for p in range(n_pairs)]
+    behind = [(2 * p, 2 * p - 2) for p in range(1, n_pairs)]
     near_pairs = [(s, t + 1) for s, t in ahead] + behind
     far_pairs = ahead + [(s, t + 1) for s, t in behind]
     three = jax.ShapeDtypeStruct((3, HALF, width), BF16)
@@ -263,7 +279,8 @@
         in_specs=[ANY] * 2 + [VMEM] * 10,
         out_specs=VMEM,
         scratch_shapes=[
-            pltpu.VMEM((5, HALF, width), BF16), pltpu.VMEM((7 * HALF, width), BF16), pltpu.SemaphoreType.DMA((2,))
+            pltpu.VMEM((5, HALF, width), BF16), pltpu.VMEM((7 * HALF, width), BF16),
+            *[pltpu.VMEM(state.shape, F32)] * 3, pltpu.SemaphoreType.DMA((2,))
         ],
         compiler_params=pltpu.CompilerParams(vmem_limit_bytes=32 * 1024 * 1024),
         cost_estimate=pl.CostEstimate(

time: 45.7 us -> 44 us (0.963)
  starting transfers between devices: 9.83 us -> 4.98 us
  waiting for transfers between devices: 3.82 us -> 7.54 us
  blocking collectives: 13.3 us -> 9.96 us
  Pallas kernels: 13.3 us -> 16 us
    ppermute x1, starting transfers between devices: 5.51 us -> 1.29 us  [on_device(): near = lax.ppermute(near_out, 'tm', near_pairs)]
    ppermute x1, waiting for transfers between devices: 3.81 us -> 7.54 us  [on_device(): near = lax.ppermute(near_out, 'tm', near_pairs)]
    all_to_all x1, blocking collectives: 13.3 us -> 9.96 us  [on_device(): parts = lax.all_to_all(payload, 'tm', 0, 0, tiled=True)]
    pallas_call x1, Pallas kernels: 4.11 us -> 6.46 us  [on_device(): pl.pallas_call(late_kernel, out_shape=jax.ShapeDtypeStruct((horizon, lane...]
    ppermute x1, starting transfers between devices: 1.31 us -> 0.69 us  [on_device(): far = lax.ppermute(far_out, 'tm', far_pairs)]
  transfers between devices with their start and end apart: 3 -> 3, of which waited for: 1 -> 1; matrix products, arithmetic and copies ran while one was open for 2% -> 2% of each run, Pallas kernels for 18% -> 19%
where the time goes in v5:
time: 44 us; the launch traced here: 43.7 us
  Pallas kernels  16 us (36%)
  blocking collectives  9.96 us (23%)
  waiting for transfers between devices  7.54 us (17%)
  local copies, waits for them, and re-layouts  5.13 us (12%)
  starting transfers between devices  4.98 us (11%)
    all_to_all x1, blocking collectives, on_device(): parts = lax.all_to_all(payload, 'tm', 0, 0, tiled=True)  9.96 us
    pallas_call x1, Pallas kernels, on_device(): pl.pallas_call(early_kernel, out_shape=[jax.ShapeDtypeStruct((4 * HALF, w...  7.79 us
    ppermute x1, waiting for transfers between devices, on_device(): near = lax.ppermute(near_out, 'tm', near_pairs)  7.54 us
    pallas_call x1, Pallas kernels, on_device(): pl.pallas_call(late_kernel, out_shape=jax.ShapeDtypeStruct((horizon, lane...  6.46 us
    unnamed x17, local copies, waits for them, and re-layouts  5.13 us
    ppermute x1, starting transfers between devices, on_device(): got = lax.ppermute(swap_out, 'tm', swap)  3 us
    ppermute x1, starting transfers between devices, on_device(): near = lax.ppermute(near_out, 'tm', near_pairs)  1.29 us
    pallas_call x1, Pallas kernels, on_device(): pl.pallas_call(final_kernel, out_shape=jax.ShapeDtypeStruct((share, width...  1.04 us
  transfers between devices with their start and end apart: 3, of which 1 were waited for; matrix products, arithmetic and copies ran while one was open for 2% of the time, Pallas kernels for 19%

profile of v5, /device:TPU:0, one launch (start us, length us, event | category | flops | bytes accessed | tf_op | source)
XLA Modules:
  0.0 43.7 jit_solution(12086062771713164520)
XLA Ops:
  0.0 0.0 copy-start
  0.0 1.2 %copy-done = bf16[1,1024,512]{2,1,0:T(8,128)(2,1)S(1)} copy-done((bf16[1,1024,512]{2,1,0:T(8,128)(2,1)S(1)}, bf16[1,1024,512]{2,1,0:T(8,128)(2,1)}, u32[]{:S(2)}) %copy-start) | copy-done | bytes 1048600
  1.2 0.0 copy-start.1
  1.2 0.0 copy-start.4
  1.2 0.0 copy-start.5
  1.3 3.0 %collective-permute-start.1 = (bf16[4,128,512]{2,1,0:T(8,128)(2,1)S(1)}, bf16[4,128,512]{2,1,0:T(8,128)(2,1)S(1)}, u32[]{:S(2)}, u32[]{:S(2)}) collective-permute-start(bf16[4,128,512]{2,1,0:T(8,128)(2,1)S(1)} %pack_swap.1), channel_id=1, source_target_pairs={{0,1},{1,0},{2,3},{3,2},{4,5},{5,4},{6,7},{7,6},{8,9},{9,8},{10,11... | collective-permute-start | bytes 1572872 | tf_op jit(solution)/shard_map/ppermute | solution.py:236
  4.3 0.1 pack_halo.1
  4.4 1.3 %collective-permute-start.2 = (bf16[3,128,512]{2,1,0:T(8,128)(2,1)S(1)}, bf16[3,128,512]{2,1,0:T(8,128)(2,1)S(1)}, u32[]{:S(2)}, u32[]{:S(2)}) collective-permute-start(bf16[3,128,512]{2,1,0:T(8,128)(2,1)S(1)} %get-tuple-element.18), channel_id=1, source_target_pairs={{1,3},{3,5},{5,7},{2,0},{4,2},{6,4},{9,11},{11,13},{13,15},{10,8},... | collective-permute-start | bytes 1179656 | tf_op jit(solution)/shard_map/ppermute | solution.py:246
  5.7 0.7 %collective-permute-start = (bf16[3,128,512]{2,1,0:T(8,128)(2,1)S(1)}, bf16[3,128,512]{2,1,0:T(8,128)(2,1)S(1)}, u32[]{:S(2)}, u32[]{:S(2)}) collective-permute-start(bf16[3,128,512]{2,1,0:T(8,128)(2,1)S(1)} %get-tuple-element.17), channel_id=1, source_target_pairs={{1,2},{3,4},{5,6},{2,1},{4,3},{6,5},{9,10},{11,12},{13,14},{10,9},... | collective-permute-start | bytes 1179656 | tf_op jit(solution)/shard_map/ppermute | solution.py:247
  6.4 0.7 %copy.9.taps = f32[2,3,512]{2,1,0:T(4,128)S(1)} copy(f32[2,3,512]{2,0,1:T(2,128)} %param.9) | data formatting | bytes 24576 | tf_op args[1]
  7.1 0.0 copy-done.1
  7.2 0.0 copy-done.4
  7.2 0.0 copy-done.5
  7.2 0.0 copy-start.2
  7.2 1.6 %copy-done.2 = bf16[2,512,1024]{2,1,0:T(8,128)(2,1)S(1)} copy-done((bf16[2,512,1024]{2,1,0:T(8,128)(2,1)S(1)}, bf16[2,512,1024]{2,1,0:T(8,128)(2,1)}, u32[]{:S(2)}) %copy-start.2) | copy-done | bytes 2097176
  8.8 0.0 copy-start.3
  8.8 1.6 %copy-done.3 = bf16[2,1024,512]{2,1,0:T(8,128)(2,1)S(1)} copy-done((bf16[2,1024,512]{2,1,0:T(8,128)(2,1)S(1)}, bf16[2,1024,512]{2,1,0:T(8,128)(2,1)}, u32[]{:S(2)}) %copy-start.3) | copy-done | bytes 2097176
  10.4 0.0 copy-start.6
  10.4 0.0 copy-start.7
  10.4 0.5 %stage.1 = (bf16[4,128,512]{2,1,0:T(8,128)(2,1)S(1)}, bf16[2,512,1024]{2,1,0:T(8,128)(2,1)S(1)}, bf16[2,1024,512]{2,1,0:T(8,128)(2,1)S(1)}, bf16[512,1024]{1,0:T(8,128)(2,1)S(1)}, bf16[512,512]{1,0:T(8,128)(2,1)S(1)}) custom-call(bf16[4,256,512]{2,1,0:T(8,128)(2,1)S(1)} %bitcast.6, bf16[2,512,1024]{2,1,0:T(8,128)(2,1)S(1)} %copy-done.2, ...), custom_call_target="tpu_custom_call" | custom-call | tf_op jit(solution)/shard_map/stage/pallas_call | solution.py:249
  10.8 7.5 %collective-permute-done.2.near = bf16[3,128,512]{2,1,0:T(8,128)(2,1)S(1)} collective-permute-done((bf16[3,128,512]{2,1,0:T(8,128)(2,1)S(1)}, bf16[3,128,512]{2,1,0:T(8,128)(2,1)S(1)}, u32[]{:S(2)}, u32[]{:S(2)}) %collective-permute-start.2) | collective-permute-done | bytes 393248 | tf_op jit(solution)/shard_map/ppermute | solution.py:246
  18.4 0.0 collective-permute-done.1.got
  18.4 0.0 copy-done.6
  18.4 0.0 copy-done.7
  18.4 7.8 %early.1 = (bf16[512,512]{1,0:T(8,128)(2,1)S(1)}, f32[128,512]{1,0:T(8,128)S(1)}, f32[128,512]{1,0:T(8,128)S(1)}, f32[128,512]{1,0:T(8,128)S(1)}) custom-call(bf16[4,128,512]{2,1,0:T(8,128)(2,1)S(1)} %get-tuple-element.16.own, bf16[4,128,512]{2,1,0:T(8,128)(2,1)S(1)} %collective-permute-done.1.got, bf16[3,128,512]{2,1,0:T(8,128)(2,1)S(1)} %collective-permute-done.2.near, ...), custom_call_target="tpu_custom_call" | custom-call | flops 6442450944 | bytes 8388608 | tf_op jit(solution)/shard_map/early/pallas_call | solution.py:261
  26.2 0.0 collective-permute-done.far
  26.2 6.5 %late.1 = bf16[128,640]{1,0:T(8,128)(2,1)S(1)} custom-call(bf16[4,128,512]{2,1,0:T(8,128)(2,1)S(1)} %get-tuple-element.16.own, bf16[3,128,512]{2,1,0:T(8,128)(2,1)S(1)} %collective-permute-done.far, bf16[512,512]{1,0:T(8,128)(2,1)S(1)} %get-tuple-element.22.tail, f32[128,512]{1,0:T(8,128)S(1)} %get-tuple-element.23.acc, ...), custom_call_target="tpu_custom_call" | custom-call | flops 3221225472 | bytes 8388608 | tf_op jit(solution)/shard_map/late/pallas_call | solution.py:276
  32.7 10.0 %all_to_all.11 = bf16[8,16,640]{2,1,0:T(8,128)(2,1)S(1)} all-to-all(bf16[8,16,640]{2,1,0:T(8,128)(2,1)S(1)} %bitcast.8), channel_id=1, replica_groups=mesh['groups'=2,'series'=2,'tm'=8] {'tm'}, dimensions={0} | all-to-all | bytes 327680 | tf_op jit(solution)/shard_map/all_to_all | solution.py:291
  42.6 1.0 %final.1 = bf16[16,512]{1,0:T(8,128)(2,1)} custom-call(bf16[128,640]{1,0:T(8,128)(2,1)S(1)} %bitcast.7, bf16[512,512]{1,0:T(8,128)(2,1)S(1)} %get-tuple-element.26.readout), custom_call_target="tpu_custom_call" | custom-call | tf_op jit(solution)/shard_map/final/pallas_call | solution.py:292
  (1 shorter events, 0.0 us)
Async XLA Ops:
  0.0 1.2 %copy-start = (bf16[1,1024,512]{2,1,0:T(8,128)(2,1)S(1)}, bf16[1,1024,512]{2,1,0:T(8,128)(2,1)}, u32[]{:S(2)}) copy-start(bf16[1,1024,512]{2,1,0:T(8,128)(2,1)} %param.8) | copy-start | bytes 3145732
  1.2 5.9 %copy-start.1 = (bf16[1,1024,512]{2,1,0:T(8,128)(2,1)S(1)}, bf16[1,1024,512]{2,1,0:T(8,128)(2,1)}, u32[]{:S(2)}) copy-start(bf16[1,1024,512]{2,1,0:T(8,128)(2,1)} %param.8) | copy-start | bytes 3145732
  1.2 5.9 %copy-start.4 = (bf16[512,1024]{1,0:T(8,128)(2,1)S(1)}, bf16[512,1024]{1,0:T(8,128)(2,1)}, u32[]{:S(2)}) copy-start(bf16[512,1024]{1,0:T(8,128)(2,1)} %refs_2_.1) | copy-start | bytes 3145732
  1.2 5.9 %copy-start.5 = (bf16[512,512]{1,0:T(8,128)(2,1)S(1)}, bf16[512,512]{1,0:T(8,128)(2,1)}, u32[]{:S(2)}) copy-start(bf16[512,512]{1,0:T(8,128)(2,1)} %refs_3_.1) | copy-start | bytes 1572868
  1.3 17.1 %collective-permute-start.1 = (bf16[4,128,512]{2,1,0:T(8,128)(2,1)S(1)}, bf16[4,128,512]{2,1,0:T(8,128)(2,1)S(1)}, u32[]{:S(2)}, u32[]{:S(2)}) collective-permute-start(bf16[4,128,512]{2,1,0:T(8,128)(2,1)S(1)} %pack_swap.1), channel_id=1, source_target_pairs={{0,1},{1,0},{2,3},{3,2},{4,5},{5,4},{6,7},{7,6},{8,9},{9,8},{10,11... | collective-permute-start | bytes 1572872 | tf_op jit(solution)/shard_map/ppermute | solution.py:236
  4.4 13.9 %collective-permute-start.2 = (bf16[3,128,512]{2,1,0:T(8,128)(2,1)S(1)}, bf16[3,128,512]{2,1,0:T(8,128)(2,1)S(1)}, u32[]{:S(2)}, u32[]{:S(2)}) collective-permute-start(bf16[3,128,512]{2,1,0:T(8,128)(2,1)S(1)} %get-tuple-element.18), channel_id=1, source_target_pairs={{1,3},{3,5},{5,7},{2,0},{4,2},{6,4},{9,11},{11,13},{13,15},{10,8},... | collective-permute-start | bytes 1179656 | tf_op jit(solution)/shard_map/ppermute | solution.py:246
  5.7 20.4 %collective-permute-start = (bf16[3,128,512]{2,1,0:T(8,128)(2,1)S(1)}, bf16[3,128,512]{2,1,0:T(8,128)(2,1)S(1)}, u32[]{:S(2)}, u32[]{:S(2)}) collective-permute-start(bf16[3,128,512]{2,1,0:T(8,128)(2,1)S(1)} %get-tuple-element.17), channel_id=1, source_target_pairs={{1,2},{3,4},{5,6},{2,1},{4,3},{6,5},{9,10},{11,12},{13,14},{10,9},... | collective-permute-start | bytes 1179656 | tf_op jit(solution)/shard_map/ppermute | solution.py:247
  7.2 1.6 %copy-start.2 = (bf16[2,512,1024]{2,1,0:T(8,128)(2,1)S(1)}, bf16[2,512,1024]{2,1,0:T(8,128)(2,1)}, u32[]{:S(2)}) copy-start(bf16[2,512,1024]{2,1,0:T(8,128)(2,1)} %refs_0_.1) | copy-start | bytes 6291460
  8.8 1.6 %copy-start.3 = (bf16[2,1024,512]{2,1,0:T(8,128)(2,1)S(1)}, bf16[2,1024,512]{2,1,0:T(8,128)(2,1)}, u32[]{:S(2)}) copy-start(bf16[2,1024,512]{2,1,0:T(8,128)(2,1)} %refs_1_.1) | copy-start | bytes 6291460
  10.4 8.0 %copy-start.6 = (bf16[128,512]{1,0:T(8,128)(2,1)S(1)}, bf16[128,512]{1,0:T(8,128)(2,1)}, u32[]{:S(2)}) copy-start(bf16[128,512]{1,0:T(8,128)(2,1)} %queries.3) | copy-start | bytes 393220
  10.4 8.0 %copy-start.7 = (f32[2,512]{1,0:T(2,128)S(1)}, f32[2,512]{1,0:T(2,128)}, u32[]{:S(2)}) copy-start(f32[2,512]{1,0:T(2,128)} %gains.3) | copy-start | bytes 12292

commit v6 on v5

--- a/solution.py
+++ b/solution.py
@@ -11,7 +11,6 @@
 STEP = 256
 HALF = STEP // 2
 BF16, F32 = jnp.bfloat16, jnp.float32
-ANY = pl.BlockSpec(memory_space=pl.ANY)
 VMEM = pl.BlockSpec(memory_space=pltpu.VMEM)
 HBM = pl.BlockSpec(memory_space=pltpu.HBM)
 
@@ -25,13 +24,21 @@
     return half + half * jnp.tanh(u * (0.7978845608028654 + (0.7978845608028654 * 0.044715) * (u * u)))
 
 
-def mix(src, first, steps, dilation, taps, gain, up, down, reach=None):
+def groups(ref):
+    return lambda g: ref[g * HALF : (g + 1) * HALF, :]
+
+
+def chain(*refs):
+    at = [(ref, g) for ref in refs for g in range(ref.shape[0])]
+    return lambda g: at[g][0][at[g][1]]
+
+
+def mix(get, first, steps, dilation, taps, gain, up, down, reach=None):
     rows, kept = [], []
     for j in range(steps):
         conv = None
         for k in range(reach[j] if reach else 3):
-            at = (first + j - k * dilation) * HALF
-            value = src[at : at + HALF, :].astype(F32)
+            value = get(first + j - k * dilation).astype(F32)
             if k == 0:
                 kept.append(value)
             conv = taps[k : k + 1, :] * value if k == 0 else conv + taps[k : k + 1, :] * value
@@ -108,33 +115,39 @@
 
 
 def first_steps(x1, taps, gains, up_v, down_v, kv_v, queries, state):
-    x2 = mix(x1, 1, 3, 2, taps[1], gains[1:2, :], up_v[1], down_v[1], (1, 1, 2))
+    x2 = mix(groups(x1), 1, 3, 2, taps[1], gains[1:2, :], up_v[1], down_v[1], (1, 1, 2))
     added = join([ref[...] for ref in state], attend(x2, kv_v[...], queries[...]))
     for ref, value in zip(state, added):
         ref[...] = value
 
 
-def early_kernel(own, got, near, taps, gains, up_v, down_v, kv_v, queries, tail, acc, top, total,
-                 x0, x1, sem):
-    side = lax.rem(lax.axis_index("tm"), 2)
-    copies = [
-        pltpu.make_async_copy(own, x0.at[pl.ds(side * 7, 4)], sem.at[0]),
-        pltpu.make_async_copy(got, x0.at[pl.ds(4 - side, 4)], sem.at[1]),
-        pltpu.make_async_copy(near, x0.at[pl.ds(8 - 8 * side, 3)], sem.at[2]),
-    ]
-    for copy in copies:
-        copy.start()
-    for copy in copies:
-        copy.wait()
-    rows0 = x0.reshape(11 * HALF, x0.shape[-1])
-    for j in range(0, 9, 3):
-        x1[j * HALF : (j + 3) * HALF, :] = mix(rows0, j + 2, 3, 1, taps[0], gains[0:1, :], up_v[0], down_v[0])
-    tail[...] = x1[pl.ds(pl.multiple_of(side * (5 * HALF), HALF), 4 * HALF), :]
+def own_kernel(own, taps, gains, up_v, down_v, out):
+    out[...] = mix(chain(own), 2, 2, 1, taps[0], gains[0:1, :], up_v[0], down_v[0])
+
+
+def early_kernel(own, got, near, done, taps, gains, up_v, down_v, kv_v, queries, tail, acc, top, total, x1):
+    here, count = lax.axis_index("tm"), lax.axis_size("tm")
+
+    def block_one(refs, first, done_at, tail_at):
+        x1[done_at * HALF : (done_at + 2) * HALF, :] = done[...]
+        for j, steps in ((first, 4), (first + 4, 3)):
+            x1[j * HALF : (j + steps) * HALF, :] = mix(
+                chain(*refs), j + 2, steps, 1, taps[0], gains[0:1, :], up_v[0], down_v[0]
+            )
+        tail[...] = x1[tail_at * HALF : (tail_at + 4) * HALF, :]
+
+    @pl.when(lax.rem(here, 2) == 0)
+    def _():
+        block_one((own, got, near), 2, 0, 0)
+
+    @pl.when(lax.rem(here, 2) == 1)
+    def _():
+        block_one((near, got, own), 0, 7, 5)
+
     x2 = jnp.concatenate([
-        mix(x1, 4, 2, 2, taps[1], gains[1:2, :], up_v[1], down_v[1]),
-        mix(x1, 6, 3, 2, taps[1], gains[1:2, :], up_v[1], down_v[1]),
+        mix(groups(x1), 4, 2, 2, taps[1], gains[1:2, :], up_v[1], down_v[1]),
+        mix(groups(x1), 6, 3, 2, taps[1], gains[1:2, :], up_v[1], down_v[1]),
     ], 0)
-    here, count = lax.axis_index("tm"), lax.axis_size("tm")
     absent = jnp.where(here == count - 2, 2 * HALF, 5 * HALF)
     acc[...], top[...], total[...] = attend(x2, kv_v[...], queries[...], absent)
 
@@ -143,22 +156,24 @@
         first_steps(x1, taps, gains, up_v, down_v, kv_v, queries, (acc, top, total))
 
 
-def late_kernel(own, far, tail, acc, top, total, taps, gains, up_v, down_v, kv_v, queries, out, x0, x1, acc2, top2, total2, sem):
-    side = lax.rem(lax.axis_index("tm"), 2)
-    copies = [
-        pltpu.make_async_copy(own.at[pl.ds(2 * side, 2)], x0.at[pl.ds(3 - 3 * side, 2)], sem.at[0]),
-        pltpu.make_async_copy(far, x0.at[pl.ds(2 * side, 3)], sem.at[1]),
-    ]
-    for copy in copies:
-        copy.start()
-    x1[pl.ds(pl.multiple_of((3 - 3 * side) * HALF, HALF), 4 * HALF), :] = tail[...]
-    for copy in copies:
-        copy.wait()
-    rows0 = x0.reshape(5 * HALF, x0.shape[-1])
-    fresh = mix(rows0, 2, 3, 1, taps[0], gains[0:1, :], up_v[0], down_v[0])
-    x1[pl.ds(pl.multiple_of(side * (4 * HALF), HALF), 3 * HALF), :] = fresh
-    x2 = mix(x1, 4, 3, 2, taps[1], gains[1:2, :], up_v[1], down_v[1])
+def late_kernel(own, far, tail, acc, top, total, taps, gains, up_v, down_v, kv_v, queries, out, x1, acc2, top2, total2):
     here, count = lax.axis_index("tm"), lax.axis_size("tm")
+
+    def block_one(refs, new_at, tail_at):
+        x1[tail_at * HALF : (tail_at + 4) * HALF, :] = tail[...]
+        x1[new_at * HALF : (new_at + 3) * HALF, :] = mix(
+            chain(*refs), 2, 3, 1, taps[0], gains[0:1, :], up_v[0], down_v[0]
+        )
+
+    @pl.when(lax.rem(here, 2) == 0)
+    def _():
+        block_one((far, own.at[0:2]), 0, 3)
+
+    @pl.when(lax.rem(here, 2) == 1)
+    def _():
+        block_one((own.at[2:4], far), 4, 0)
+
+    x2 = mix(groups(x1), 4, 3, 2, taps[1], gains[1:2, :], up_v[1], down_v[1])
     absent = jnp.where(here == count - 1, 0, 3 * HALF)
     acc2[...], top2[...], total2[...] = join(
         (acc[...], top[...], total[...]), attend(x2, kv_v[...], queries[...], absent)
@@ -258,29 +273,37 @@
     )(hist, up, down, w_kv, readout)
     state = jax.ShapeDtypeStruct((horizon, width), F32)
     per_row = 4 * width * hidden
+    done = pl.pallas_call(
+        own_kernel,
+        out_shape=jax.ShapeDtypeStruct((2 * HALF, width), BF16),
+        in_specs=[VMEM] * 5,
+        out_specs=VMEM,
+        compiler_params=small(16),
+        cost_estimate=pl.CostEstimate(flops=2 * per_row * HALF, bytes_accessed=4 << 20, transcendentals=2 * HALF * hidden),
+        name="own",
+    )(own, taps, gains, up_v, down_v)
     tail, acc, top, total = pl.pallas_call(
         early_kernel,
         out_shape=[jax.ShapeDtypeStruct((4 * HALF, width), BF16), state, state, state],
-        in_specs=[ANY] * 3 + [VMEM] * 6,
+        in_specs=[VMEM] * 10,
         out_specs=[VMEM] * 4,
         scratch_shapes=[
-            pltpu.VMEM((11, HALF, width), BF16), pltpu.VMEM((9 * HALF, width), BF16), pltpu.SemaphoreType.DMA((3,))
+            pltpu.VMEM((9 * HALF, width), BF16)
         ],
         compiler_params=pltpu.CompilerParams(vmem_limit_bytes=32 * 1024 * 1024),
         cost_estimate=pl.CostEstimate(
             flops=(14 * per_row + 5 * 2 * per_row) * HALF, bytes_accessed=8 << 20, transcendentals=2 << 20
         ),
         name="early",
-    )(own, got, near, taps, gains, up_v, down_v, kv_v, queries)
+    )(own, got, near, done, taps, gains, up_v, down_v, kv_v, queries)
     lanes = width + 128
     payload = pl.pallas_call(
         late_kernel,
         out_shape=jax.ShapeDtypeStruct((horizon, lanes), BF16),
-        in_specs=[ANY] * 2 + [VMEM] * 10,
+        in_specs=[VMEM] * 12,
         out_specs=VMEM,
         scratch_shapes=[
-            pltpu.VMEM((5, HALF, width), BF16), pltpu.VMEM((7 * HALF, width), BF16),
-            *[pltpu.VMEM(state.shape, F32)] * 3, pltpu.SemaphoreType.DMA((2,))
+            pltpu.VMEM((7 * HALF, width), BF16), *[pltpu.VMEM(state.shape, F32)] * 3
         ],
         compiler_params=pltpu.CompilerParams(vmem_limit_bytes=32 * 1024 * 1024),
         cost_estimate=pl.CostEstimate(

time: 44 us -> 43.1 us (0.980)
  waiting for transfers between devices: 7.54 us -> 6.31 us
    ppermute x1, waiting for transfers between devices: 7.54 us -> 6.3 us  [on_device(): near = lax.ppermute(near_out, 'tm', near_pairs)]
    pallas_call x0 -> x1, Pallas kernels: none -> 1.02 us  [on_device(): pl.pallas_call(own_kernel, out_shape=jax.ShapeDtypeStruct((2 * HALF, widt...]
    pallas_call x1, Pallas kernels: 7.79 us -> 6.85 us  [on_device(): pl.pallas_call(early_kernel, out_shape=[jax.ShapeDtypeStruct((4 * HALF, w...]
  transfers between devices with their start and end apart: 3 -> 3, of which waited for: 1 -> 1; matrix products, arithmetic and copies ran while one was open for 2% -> 2% of each run, Pallas kernels for 19% -> 20%
where the time goes in v6:
time: 43.1 us; the launch traced here: 42.7 us
  Pallas kernels  15.8 us (37%)
  blocking collectives  10.2 us (24%)
  waiting for transfers between devices  6.31 us (15%)
  local copies, waits for them, and re-layouts  5.34 us (12%)
  starting transfers between devices  4.98 us (12%)
    all_to_all x1, blocking collectives, on_device(): parts = lax.all_to_all(payload, 'tm', 0, 0, tiled=True)  10.2 us
    pallas_call x1, Pallas kernels, on_device(): pl.pallas_call(early_kernel, out_shape=[jax.ShapeDtypeStruct((4 * HALF, w...  6.85 us
    ppermute x1, waiting for transfers between devices, on_device(): near = lax.ppermute(near_out, 'tm', near_pairs)  6.3 us
    pallas_call x1, Pallas kernels, on_device(): pl.pallas_call(late_kernel, out_shape=jax.ShapeDtypeStruct((horizon, lane...  6.26 us
    unnamed x17, local copies, waits for them, and re-layouts  5.34 us
    ppermute x1, starting transfers between devices, on_device(): got = lax.ppermute(swap_out, 'tm', swap)  3 us
    ppermute x1, starting transfers between devices, on_device(): near = lax.ppermute(near_out, 'tm', near_pairs)  1.29 us
    pallas_call x1, Pallas kernels, on_device(): pl.pallas_call(final_kernel, out_shape=jax.ShapeDtypeStruct((share, width...  1.04 us
  transfers between devices with their start and end apart: 3, of which 1 were waited for; matrix products, arithmetic and copies ran while one was open for 2% of the time, Pallas kernels for 20%

profile of v6, /device:TPU:0, one launch (start us, length us, event | category | flops | bytes accessed | tf_op | source)
XLA Modules:
  0.0 42.7 jit_solution(10935699142409892926)
XLA Ops:
  0.0 0.0 copy-start
  0.0 1.2 %copy-done = bf16[1,1024,512]{2,1,0:T(8,128)(2,1)S(1)} copy-done((bf16[1,1024,512]{2,1,0:T(8,128)(2,1)S(1)}, bf16[1,1024,512]{2,1,0:T(8,128)(2,1)}, u32[]{:S(2)}) %copy-start) | copy-done | bytes 1048600
  1.2 0.0 copy-start.1
  1.2 0.0 copy-start.4
  1.2 0.0 copy-start.5
  1.3 3.0 %collective-permute-start.1 = (bf16[4,128,512]{2,1,0:T(8,128)(2,1)S(1)}, bf16[4,128,512]{2,1,0:T(8,128)(2,1)S(1)}, u32[]{:S(2)}, u32[]{:S(2)}) collective-permute-start(bf16[4,128,512]{2,1,0:T(8,128)(2,1)S(1)} %pack_swap.1), channel_id=1, source_target_pairs={{0,1},{1,0},{2,3},{3,2},{4,5},{5,4},{6,7},{7,6},{8,9},{9,8},{10,11... | collective-permute-start | bytes 1572872 | tf_op jit(solution)/shard_map/ppermute | solution.py:251
  4.3 0.1 pack_halo.1
  4.4 1.3 %collective-permute-start.2 = (bf16[3,128,512]{2,1,0:T(8,128)(2,1)S(1)}, bf16[3,128,512]{2,1,0:T(8,128)(2,1)S(1)}, u32[]{:S(2)}, u32[]{:S(2)}) collective-permute-start(bf16[3,128,512]{2,1,0:T(8,128)(2,1)S(1)} %get-tuple-element.18), channel_id=1, source_target_pairs={{1,3},{3,5},{5,7},{2,0},{4,2},{6,4},{9,11},{11,13},{13,15},{10,8},... | collective-permute-start | bytes 1179656 | tf_op jit(solution)/shard_map/ppermute | solution.py:261
  5.7 0.7 %collective-permute-start = (bf16[3,128,512]{2,1,0:T(8,128)(2,1)S(1)}, bf16[3,128,512]{2,1,0:T(8,128)(2,1)S(1)}, u32[]{:S(2)}, u32[]{:S(2)}) collective-permute-start(bf16[3,128,512]{2,1,0:T(8,128)(2,1)S(1)} %get-tuple-element.17), channel_id=1, source_target_pairs={{1,2},{3,4},{5,6},{2,1},{4,3},{6,5},{9,10},{11,12},{13,14},{10,9},... | collective-permute-start | bytes 1179656 | tf_op jit(solution)/shard_map/ppermute | solution.py:262
  6.4 0.7 %copy.9.taps = f32[2,3,512]{2,1,0:T(4,128)S(1)} copy(f32[2,3,512]{2,0,1:T(2,128)} %param.9) | data formatting | bytes 24576 | tf_op args[1]
  7.1 0.0 copy-done.1
  7.2 0.0 copy-done.4
  7.2 0.0 copy-done.5
  7.2 0.0 copy-start.2
  7.2 1.6 %copy-done.2 = bf16[2,512,1024]{2,1,0:T(8,128)(2,1)S(1)} copy-done((bf16[2,512,1024]{2,1,0:T(8,128)(2,1)S(1)}, bf16[2,512,1024]{2,1,0:T(8,128)(2,1)}, u32[]{:S(2)}) %copy-start.2) | copy-done | bytes 2097176
  8.8 0.0 copy-start.3
  8.8 1.6 %copy-done.3 = bf16[2,1024,512]{2,1,0:T(8,128)(2,1)S(1)} copy-done((bf16[2,1024,512]{2,1,0:T(8,128)(2,1)S(1)}, bf16[2,1024,512]{2,1,0:T(8,128)(2,1)}, u32[]{:S(2)}) %copy-start.3) | copy-done | bytes 2097176
  10.4 0.0 copy-start.6
  10.4 0.5 %stage.1 = (bf16[4,128,512]{2,1,0:T(8,128)(2,1)S(1)}, bf16[2,512,1024]{2,1,0:T(8,128)(2,1)S(1)}, bf16[2,1024,512]{2,1,0:T(8,128)(2,1)S(1)}, bf16[512,1024]{1,0:T(8,128)(2,1)S(1)}, bf16[512,512]{1,0:T(8,128)(2,1)S(1)}) custom-call(bf16[4,256,512]{2,1,0:T(8,128)(2,1)S(1)} %bitcast.6, bf16[2,512,1024]{2,1,0:T(8,128)(2,1)S(1)} %copy-done.2, ...), custom_call_target="tpu_custom_call" | custom-call | tf_op jit(solution)/shard_map/stage/pallas_call | solution.py:264
  10.8 0.2 copy-done.6
  11.0 0.0 copy-start.7
  11.0 1.0 %own.1.done = bf16[256,512]{1,0:T(8,128)(2,1)S(1)} custom-call(bf16[4,128,512]{2,1,0:T(8,128)(2,1)S(1)} %get-tuple-element.16.own, f32[2,3,512]{2,1,0:T(4,128)S(1)} %copy.9.taps, f32[2,512]{1,0:T(2,128)S(1)} %copy-done.6, bf16[2,512,1024]{2,1,0:T(8,128)(2,1)S(1)} %get-tuple-element.19.up_v, bf16[2,1024,512]{2,1,0:T(8,128)(2,1)S(1)} %get-tuple-element.20.down_v), custom_call_target="tpu_custom_call" | custom-call | flops 536870912 | bytes 4194304 | tf_op jit(solution)/shard_map/own/pallas_call | solution.py:276
  12.1 6.3 %collective-permute-done.2.near = bf16[3,128,512]{2,1,0:T(8,128)(2,1)S(1)} collective-permute-done((bf16[3,128,512]{2,1,0:T(8,128)(2,1)S(1)}, bf16[3,128,512]{2,1,0:T(8,128)(2,1)S(1)}, u32[]{:S(2)}, u32[]{:S(2)}) %collective-permute-start.2) | collective-permute-done | bytes 393248 | tf_op jit(solution)/shard_map/ppermute | solution.py:261
  18.4 0.0 collective-permute-done.1.got
  18.4 0.0 copy-done.7
  18.4 6.8 %early.1 = (bf16[512,512]{1,0:T(8,128)(2,1)S(1)}, f32[128,512]{1,0:T(8,128)S(1)}, f32[128,512]{1,0:T(8,128)S(1)}, f32[128,512]{1,0:T(8,128)S(1)}) custom-call(bf16[4,128,512]{2,1,0:T(8,128)(2,1)S(1)} %get-tuple-element.16.own, bf16[4,128,512]{2,1,0:T(8,128)(2,1)S(1)} %collective-permute-done.1.got, bf16[3,128,512]{2,1,0:T(8,128)(2,1)S(1)} %collective-permute-done.2.near, ...), custom_call_target="tpu_custom_call" | custom-call | flops 6442450944 | bytes 8388608 | tf_op jit(solution)/shard_map/early/pallas_call | solution.py:285
  25.2 0.0 collective-permute-done.far
  25.2 6.3 %late.1 = bf16[128,640]{1,0:T(8,128)(2,1)S(1)} custom-call(bf16[4,128,512]{2,1,0:T(8,128)(2,1)S(1)} %get-tuple-element.16.own, bf16[3,128,512]{2,1,0:T(8,128)(2,1)S(1)} %collective-permute-done.far, bf16[512,512]{1,0:T(8,128)(2,1)S(1)} %get-tuple-element.22.tail, f32[128,512]{1,0:T(8,128)S(1)} %get-tuple-element.23.acc, ...), custom_call_target="tpu_custom_call" | custom-call | flops 3221225472 | bytes 8388608 | tf_op jit(solution)/shard_map/late/pallas_call | solution.py:300
  31.5 10.2 %all_to_all.11 = bf16[8,16,640]{2,1,0:T(8,128)(2,1)S(1)} all-to-all(bf16[8,16,640]{2,1,0:T(8,128)(2,1)S(1)} %bitcast.8), channel_id=1, replica_groups=mesh['groups'=2,'series'=2,'tm'=8] {'tm'}, dimensions={0} | all-to-all | bytes 327680 | tf_op jit(solution)/shard_map/all_to_all | solution.py:314
  41.7 1.0 %final.1 = bf16[16,512]{1,0:T(8,128)(2,1)} custom-call(bf16[128,640]{1,0:T(8,128)(2,1)S(1)} %bitcast.7, bf16[512,512]{1,0:T(8,128)(2,1)S(1)} %get-tuple-element.26.readout), custom_call_target="tpu_custom_call" | custom-call | tf_op jit(solution)/shard_map/final/pallas_call | solution.py:315
  (1 shorter events, 0.0 us)
Async XLA Ops:
  0.0 1.2 %copy-start = (bf16[1,1024,512]{2,1,0:T(8,128)(2,1)S(1)}, bf16[1,1024,512]{2,1,0:T(8,128)(2,1)}, u32[]{:S(2)}) copy-start(bf16[1,1024,512]{2,1,0:T(8,128)(2,1)} %param.8) | copy-start | bytes 3145732
  1.2 5.9 %copy-start.1 = (bf16[1,1024,512]{2,1,0:T(8,128)(2,1)S(1)}, bf16[1,1024,512]{2,1,0:T(8,128)(2,1)}, u32[]{:S(2)}) copy-start(bf16[1,1024,512]{2,1,0:T(8,128)(2,1)} %param.8) | copy-start | bytes 3145732
  1.2 5.9 %copy-start.4 = (bf16[512,1024]{1,0:T(8,128)(2,1)S(1)}, bf16[512,1024]{1,0:T(8,128)(2,1)}, u32[]{:S(2)}) copy-start(bf16[512,1024]{1,0:T(8,128)(2,1)} %refs_2_.1) | copy-start | bytes 3145732
  1.2 5.9 %copy-start.5 = (bf16[512,512]{1,0:T(8,128)(2,1)S(1)}, bf16[512,512]{1,0:T(8,128)(2,1)}, u32[]{:S(2)}) copy-start(bf16[512,512]{1,0:T(8,128)(2,1)} %refs_3_.1) | copy-start | bytes 1572868
  1.3 17.1 %collective-permute-start.1 = (bf16[4,128,512]{2,1,0:T(8,128)(2,1)S(1)}, bf16[4,128,512]{2,1,0:T(8,128)(2,1)S(1)}, u32[]{:S(2)}, u32[]{:S(2)}) collective-permute-start(bf16[4,128,512]{2,1,0:T(8,128)(2,1)S(1)} %pack_swap.1), channel_id=1, source_target_pairs={{0,1},{1,0},{2,3},{3,2},{4,5},{5,4},{6,7},{7,6},{8,9},{9,8},{10,11... | collective-permute-start | bytes 1572872 | tf_op jit(solution)/shard_map/ppermute | solution.py:251
  4.4 13.9 %collective-permute-start.2 = (bf16[3,128,512]{2,1,0:T(8,128)(2,1)S(1)}, bf16[3,128,512]{2,1,0:T(8,128)(2,1)S(1)}, u32[]{:S(2)}, u32[]{:S(2)}) collective-permute-start(bf16[3,128,512]{2,1,0:T(8,128)(2,1)S(1)} %get-tuple-element.18), channel_id=1, source_target_pairs={{1,3},{3,5},{5,7},{2,0},{4,2},{6,4},{9,11},{11,13},{13,15},{10,8},... | collective-permute-start | bytes 1179656 | tf_op jit(solution)/shard_map/ppermute | solution.py:261
  5.7 19.5 %collective-permute-start = (bf16[3,128,512]{2,1,0:T(8,128)(2,1)S(1)}, bf16[3,128,512]{2,1,0:T(8,128)(2,1)S(1)}, u32[]{:S(2)}, u32[]{:S(2)}) collective-permute-start(bf16[3,128,512]{2,1,0:T(8,128)(2,1)S(1)} %get-tuple-element.17), channel_id=1, source_target_pairs={{1,2},{3,4},{5,6},{2,1},{4,3},{6,5},{9,10},{11,12},{13,14},{10,9},... | collective-permute-start | bytes 1179656 | tf_op jit(solution)/shard_map/ppermute | solution.py:262
  7.2 1.6 %copy-start.2 = (bf16[2,512,1024]{2,1,0:T(8,128)(2,1)S(1)}, bf16[2,512,1024]{2,1,0:T(8,128)(2,1)}, u32[]{:S(2)}) copy-start(bf16[2,512,1024]{2,1,0:T(8,128)(2,1)} %refs_0_.1) | copy-start | bytes 6291460
  8.8 1.6 %copy-start.3 = (bf16[2,1024,512]{2,1,0:T(8,128)(2,1)S(1)}, bf16[2,1024,512]{2,1,0:T(8,128)(2,1)}, u32[]{:S(2)}) copy-start(bf16[2,1024,512]{2,1,0:T(8,128)(2,1)} %refs_1_.1) | copy-start | bytes 6291460
  10.4 0.7 %copy-start.6 = (f32[2,512]{1,0:T(2,128)S(1)}, f32[2,512]{1,0:T(2,128)}, u32[]{:S(2)}) copy-start(f32[2,512]{1,0:T(2,128)} %gains.5) | copy-start | bytes 12292
  11.0 7.3 %copy-start.7 = (bf16[128,512]{1,0:T(8,128)(2,1)S(1)}, bf16[128,512]{1,0:T(8,128)(2,1)}, u32[]{:S(2)}) copy-start(bf16[128,512]{1,0:T(8,128)(2,1)} %queries.3) | copy-start | bytes 393220

commit v7 on v6

--- a/solution.py
+++ b/solution.py
@@ -130,10 +130,9 @@
 
     def block_one(refs, first, done_at, tail_at):
         x1[done_at * HALF : (done_at + 2) * HALF, :] = done[...]
-        for j, steps in ((first, 4), (first + 4, 3)):
-            x1[j * HALF : (j + steps) * HALF, :] = mix(
-                chain(*refs), j + 2, steps, 1, taps[0], gains[0:1, :], up_v[0], down_v[0]
-            )
+        x1[first * HALF : (first + 7) * HALF, :] = mix(
+            chain(*refs), first + 2, 7, 1, taps[0], gains[0:1, :], up_v[0], down_v[0]
+        )
         tail[...] = x1[tail_at * HALF : (tail_at + 4) * HALF, :]
 
     @pl.when(lax.rem(here, 2) == 0)
@@ -144,10 +143,7 @@
     def _():
         block_one((near, got, own), 0, 7, 5)
 
-    x2 = jnp.concatenate([
-        mix(groups(x1), 4, 2, 2, taps[1], gains[1:2, :], up_v[1], down_v[1]),
-        mix(groups(x1), 6, 3, 2, taps[1], gains[1:2, :], up_v[1], down_v[1]),
-    ], 0)
+    x2 = mix(groups(x1), 4, 5, 2, taps[1], gains[1:2, :], up_v[1], down_v[1])
     absent = jnp.where(here == count - 2, 2 * HALF, 5 * HALF)
     acc[...], top[...], total[...] = attend(x2, kv_v[...], queries[...], absent)
 

time: 43.1 us -> 43.1 us (level)
  transfers between devices with their start and end apart: 3 -> 3, of which waited for: 1 -> 1; matrix products, arithmetic and copies ran while one was open for 2% -> 2% of each run, Pallas kernels for 20% -> 19%
where the time goes in v7:
time: 43.1 us; the launch traced here: 42.7 us
  Pallas kernels  15.6 us (36%)
  blocking collectives  10.4 us (24%)
  waiting for transfers between devices  6.31 us (15%)
  local copies, waits for them, and re-layouts  5.34 us (12%)
  starting transfers between devices  4.98 us (12%)
    all_to_all x1, blocking collectives, on_device(): parts = lax.all_to_all(payload, 'tm', 0, 0, tiled=True)  10.4 us
    pallas_call x1, Pallas kernels, on_device(): pl.pallas_call(early_kernel, out_shape=[jax.ShapeDtypeStruct((4 * HALF, w...  6.62 us
    ppermute x1, waiting for transfers between devices, on_device(): near = lax.ppermute(near_out, 'tm', near_pairs)  6.3 us
    pallas_call x1, Pallas kernels, on_device(): pl.pallas_call(late_kernel, out_shape=jax.ShapeDtypeStruct((horizon, lane...  6.26 us
    unnamed x17, local copies, waits for them, and re-layouts  5.34 us
    ppermute x1, starting transfers between devices, on_device(): got = lax.ppermute(swap_out, 'tm', swap)  3 us
    ppermute x1, starting transfers between devices, on_device(): near = lax.ppermute(near_out, 'tm', near_pairs)  1.29 us
    pallas_call x1, Pallas kernels, on_device(): pl.pallas_call(final_kernel, out_shape=jax.ShapeDtypeStruct((share, width...  1.04 us
  transfers between devices with their start and end apart: 3, of which 1 were waited for; matrix products, arithmetic and copies ran while one was open for 2% of the time, Pallas kernels for 19%

profile of v7, /device:TPU:0, one launch (start us, length us, event | category | flops | bytes accessed | tf_op | source)
XLA Modules:
  0.0 42.7 jit_solution(14283624659725745942)
XLA Ops:
  0.0 0.0 copy-start
  0.0 1.2 %copy-done = bf16[1,1024,512]{2,1,0:T(8,128)(2,1)S(1)} copy-done((bf16[1,1024,512]{2,1,0:T(8,128)(2,1)S(1)}, bf16[1,1024,512]{2,1,0:T(8,128)(2,1)}, u32[]{:S(2)}) %copy-start) | copy-done | bytes 1048600
  1.2 0.0 copy-start.1
  1.2 0.0 copy-start.4
  1.2 0.0 copy-start.5
  1.3 3.0 %collective-permute-start.1 = (bf16[4,128,512]{2,1,0:T(8,128)(2,1)S(1)}, bf16[4,128,512]{2,1,0:T(8,128)(2,1)S(1)}, u32[]{:S(2)}, u32[]{:S(2)}) collective-permute-start(bf16[4,128,512]{2,1,0:T(8,128)(2,1)S(1)} %pack_swap.1), channel_id=1, source_target_pairs={{0,1},{1,0},{2,3},{3,2},{4,5},{5,4},{6,7},{7,6},{8,9},{9,8},{10,11... | collective-permute-start | bytes 1572872 | tf_op jit(solution)/shard_map/ppermute | solution.py:247
  4.3 0.1 pack_halo.1
  4.4 1.3 %collective-permute-start.2 = (bf16[3,128,512]{2,1,0:T(8,128)(2,1)S(1)}, bf16[3,128,512]{2,1,0:T(8,128)(2,1)S(1)}, u32[]{:S(2)}, u32[]{:S(2)}) collective-permute-start(bf16[3,128,512]{2,1,0:T(8,128)(2,1)S(1)} %get-tuple-element.18), channel_id=1, source_target_pairs={{1,3},{3,5},{5,7},{2,0},{4,2},{6,4},{9,11},{11,13},{13,15},{10,8},... | collective-permute-start | bytes 1179656 | tf_op jit(solution)/shard_map/ppermute | solution.py:257
  5.7 0.7 %collective-permute-start = (bf16[3,128,512]{2,1,0:T(8,128)(2,1)S(1)}, bf16[3,128,512]{2,1,0:T(8,128)(2,1)S(1)}, u32[]{:S(2)}, u32[]{:S(2)}) collective-permute-start(bf16[3,128,512]{2,1,0:T(8,128)(2,1)S(1)} %get-tuple-element.17), channel_id=1, source_target_pairs={{1,2},{3,4},{5,6},{2,1},{4,3},{6,5},{9,10},{11,12},{13,14},{10,9},... | collective-permute-start | bytes 1179656 | tf_op jit(solution)/shard_map/ppermute | solution.py:258
  6.4 0.7 %copy.9.taps = f32[2,3,512]{2,1,0:T(4,128)S(1)} copy(f32[2,3,512]{2,0,1:T(2,128)} %param.9) | data formatting | bytes 24576 | tf_op args[1]
  7.1 0.0 copy-done.1
  7.2 0.0 copy-done.4
  7.2 0.0 copy-done.5
  7.2 0.0 copy-start.2
  7.2 1.6 %copy-done.2 = bf16[2,512,1024]{2,1,0:T(8,128)(2,1)S(1)} copy-done((bf16[2,512,1024]{2,1,0:T(8,128)(2,1)S(1)}, bf16[2,512,1024]{2,1,0:T(8,128)(2,1)}, u32[]{:S(2)}) %copy-start.2) | copy-done | bytes 2097176
  8.8 0.0 copy-start.3
  8.8 1.6 %copy-done.3 = bf16[2,1024,512]{2,1,0:T(8,128)(2,1)S(1)} copy-done((bf16[2,1024,512]{2,1,0:T(8,128)(2,1)S(1)}, bf16[2,1024,512]{2,1,0:T(8,128)(2,1)}, u32[]{:S(2)}) %copy-start.3) | copy-done | bytes 2097176
  10.4 0.0 copy-start.6
  10.4 0.5 %stage.1 = (bf16[4,128,512]{2,1,0:T(8,128)(2,1)S(1)}, bf16[2,512,1024]{2,1,0:T(8,128)(2,1)S(1)}, bf16[2,1024,512]{2,1,0:T(8,128)(2,1)S(1)}, bf16[512,1024]{1,0:T(8,128)(2,1)S(1)}, bf16[512,512]{1,0:T(8,128)(2,1)S(1)}) custom-call(bf16[4,256,512]{2,1,0:T(8,128)(2,1)S(1)} %bitcast.6, bf16[2,512,1024]{2,1,0:T(8,128)(2,1)S(1)} %copy-done.2, ...), custom_call_target="tpu_custom_call" | custom-call | tf_op jit(solution)/shard_map/stage/pallas_call | solution.py:260
  10.8 0.2 copy-done.6
  11.0 0.0 copy-start.7
  11.0 1.0 %own.1.done = bf16[256,512]{1,0:T(8,128)(2,1)S(1)} custom-call(bf16[4,128,512]{2,1,0:T(8,128)(2,1)S(1)} %get-tuple-element.16.own, f32[2,3,512]{2,1,0:T(4,128)S(1)} %copy.9.taps, f32[2,512]{1,0:T(2,128)S(1)} %copy-done.6, bf16[2,512,1024]{2,1,0:T(8,128)(2,1)S(1)} %get-tuple-element.19.up_v, bf16[2,1024,512]{2,1,0:T(8,128)(2,1)S(1)} %get-tuple-element.20.down_v), custom_call_target="tpu_custom_call" | custom-call | flops 536870912 | bytes 4194304 | tf_op jit(solution)/shard_map/own/pallas_call | solution.py:272
  12.1 6.3 %collective-permute-done.2.near = bf16[3,128,512]{2,1,0:T(8,128)(2,1)S(1)} collective-permute-done((bf16[3,128,512]{2,1,0:T(8,128)(2,1)S(1)}, bf16[3,128,512]{2,1,0:T(8,128)(2,1)S(1)}, u32[]{:S(2)}, u32[]{:S(2)}) %collective-permute-start.2) | collective-permute-done | bytes 393248 | tf_op jit(solution)/shard_map/ppermute | solution.py:257
  18.4 0.0 collective-permute-done.1.got
  18.4 0.0 copy-done.7
  18.4 6.6 %early.1 = (bf16[512,512]{1,0:T(8,128)(2,1)S(1)}, f32[128,512]{1,0:T(8,128)S(1)}, f32[128,512]{1,0:T(8,128)S(1)}, f32[128,512]{1,0:T(8,128)S(1)}) custom-call(bf16[4,128,512]{2,1,0:T(8,128)(2,1)S(1)} %get-tuple-element.16.own, bf16[4,128,512]{2,1,0:T(8,128)(2,1)S(1)} %collective-permute-done.1.got, bf16[3,128,512]{2,1,0:T(8,128)(2,1)S(1)} %collective-permute-done.2.near, ...), custom_call_target="tpu_custom_call" | custom-call | flops 6442450944 | bytes 8388608 | tf_op jit(solution)/shard_map/early/pallas_call | solution.py:281
  25.0 0.0 collective-permute-done.far
  25.0 6.3 %late.1 = bf16[128,640]{1,0:T(8,128)(2,1)S(1)} custom-call(bf16[4,128,512]{2,1,0:T(8,128)(2,1)S(1)} %get-tuple-element.16.own, bf16[3,128,512]{2,1,0:T(8,128)(2,1)S(1)} %collective-permute-done.far, bf16[512,512]{1,0:T(8,128)(2,1)S(1)} %get-tuple-element.22.tail, f32[128,512]{1,0:T(8,128)S(1)} %get-tuple-element.23.acc, ...), custom_call_target="tpu_custom_call" | custom-call | flops 3221225472 | bytes 8388608 | tf_op jit(solution)/shard_map/late/pallas_call | solution.py:296
  31.3 10.4 %all_to_all.11 = bf16[8,16,640]{2,1,0:T(8,128)(2,1)S(1)} all-to-all(bf16[8,16,640]{2,1,0:T(8,128)(2,1)S(1)} %bitcast.8), channel_id=1, replica_groups=mesh['groups'=2,'series'=2,'tm'=8] {'tm'}, dimensions={0} | all-to-all | bytes 327680 | tf_op jit(solution)/shard_map/all_to_all | solution.py:310
  41.7 1.0 %final.1 = bf16[16,512]{1,0:T(8,128)(2,1)} custom-call(bf16[128,640]{1,0:T(8,128)(2,1)S(1)} %bitcast.7, bf16[512,512]{1,0:T(8,128)(2,1)S(1)} %get-tuple-element.26.readout), custom_call_target="tpu_custom_call" | custom-call | tf_op jit(solution)/shard_map/final/pallas_call | solution.py:311
  (1 shorter events, 0.0 us)
Async XLA Ops:
  0.0 1.2 %copy-start = (bf16[1,1024,512]{2,1,0:T(8,128)(2,1)S(1)}, bf16[1,1024,512]{2,1,0:T(8,128)(2,1)}, u32[]{:S(2)}) copy-start(bf16[1,1024,512]{2,1,0:T(8,128)(2,1)} %param.8) | copy-start | bytes 3145732
  1.2 5.9 %copy-start.1 = (bf16[1,1024,512]{2,1,0:T(8,128)(2,1)S(1)}, bf16[1,1024,512]{2,1,0:T(8,128)(2,1)}, u32[]{:S(2)}) copy-start(bf16[1,1024,512]{2,1,0:T(8,128)(2,1)} %param.8) | copy-start | bytes 3145732
  1.2 5.9 %copy-start.4 = (bf16[512,1024]{1,0:T(8,128)(2,1)S(1)}, bf16[512,1024]{1,0:T(8,128)(2,1)}, u32[]{:S(2)}) copy-start(bf16[512,1024]{1,0:T(8,128)(2,1)} %refs_2_.1) | copy-start | bytes 3145732
  1.2 5.9 %copy-start.5 = (bf16[512,512]{1,0:T(8,128)(2,1)S(1)}, bf16[512,512]{1,0:T(8,128)(2,1)}, u32[]{:S(2)}) copy-start(bf16[512,512]{1,0:T(8,128)(2,1)} %refs_3_.1) | copy-start | bytes 1572868
  1.3 17.1 %collective-permute-start.1 = (bf16[4,128,512]{2,1,0:T(8,128)(2,1)S(1)}, bf16[4,128,512]{2,1,0:T(8,128)(2,1)S(1)}, u32[]{:S(2)}, u32[]{:S(2)}) collective-permute-start(bf16[4,128,512]{2,1,0:T(8,128)(2,1)S(1)} %pack_swap.1), channel_id=1, source_target_pairs={{0,1},{1,0},{2,3},{3,2},{4,5},{5,4},{6,7},{7,6},{8,9},{9,8},{10,11... | collective-permute-start | bytes 1572872 | tf_op jit(solution)/shard_map/ppermute | solution.py:247
  4.4 13.9 %collective-permute-start.2 = (bf16[3,128,512]{2,1,0:T(8,128)(2,1)S(1)}, bf16[3,128,512]{2,1,0:T(8,128)(2,1)S(1)}, u32[]{:S(2)}, u32[]{:S(2)}) collective-permute-start(bf16[3,128,512]{2,1,0:T(8,128)(2,1)S(1)} %get-tuple-element.18), channel_id=1, source_target_pairs={{1,3},{3,5},{5,7},{2,0},{4,2},{6,4},{9,11},{11,13},{13,15},{10,8},... | collective-permute-start | bytes 1179656 | tf_op jit(solution)/shard_map/ppermute | solution.py:257
  5.7 19.3 %collective-permute-start = (bf16[3,128,512]{2,1,0:T(8,128)(2,1)S(1)}, bf16[3,128,512]{2,1,0:T(8,128)(2,1)S(1)}, u32[]{:S(2)}, u32[]{:S(2)}) collective-permute-start(bf16[3,128,512]{2,1,0:T(8,128)(2,1)S(1)} %get-tuple-element.17), channel_id=1, source_target_pairs={{1,2},{3,4},{5,6},{2,1},{4,3},{6,5},{9,10},{11,12},{13,14},{10,9},... | collective-permute-start | bytes 1179656 | tf_op jit(solution)/shard_map/ppermute | solution.py:258
  7.2 1.6 %copy-start.2 = (bf16[2,512,1024]{2,1,0:T(8,128)(2,1)S(1)}, bf16[2,512,1024]{2,1,0:T(8,128)(2,1)}, u32[]{:S(2)}) copy-start(bf16[2,512,1024]{2,1,0:T(8,128)(2,1)} %refs_0_.1) | copy-start | bytes 6291460
  8.8 1.6 %copy-start.3 = (bf16[2,1024,512]{2,1,0:T(8,128)(2,1)S(1)}, bf16[2,1024,512]{2,1,0:T(8,128)(2,1)}, u32[]{:S(2)}) copy-start(bf16[2,1024,512]{2,1,0:T(8,128)(2,1)} %refs_1_.1) | copy-start | bytes 6291460
  10.4 0.7 %copy-start.6 = (f32[2,512]{1,0:T(2,128)S(1)}, f32[2,512]{1,0:T(2,128)}, u32[]{:S(2)}) copy-start(f32[2,512]{1,0:T(2,128)} %gains.5) | copy-start | bytes 12292
  11.0 7.3 %copy-start.7 = (bf16[128,512]{1,0:T(8,128)(2,1)S(1)}, bf16[128,512]{1,0:T(8,128)(2,1)}, u32[]{:S(2)}) copy-start(bf16[128,512]{1,0:T(8,128)(2,1)} %queries.3) | copy-start | bytes 393220

commit v8 on v7

--- a/solution.py
+++ b/solution.py
@@ -243,7 +243,7 @@
         scratch_shapes=[pltpu.SemaphoreType.DMA((1,))],
         compiler_params=small(),
         name="pack_swap",
-    )(hist)
+    )(pltpu.with_memory_space_constraint(hist, pltpu.HBM))
     got = lax.ppermute(swap_out, "tm", swap)
     near_out, far_out = pl.pallas_call(
         functools.partial(pack_kernel, 1),

time: 43.1 us -> 42.8 us (level)
  local copies, waits for them, and re-layouts: 5.34 us -> 3.41 us
  Pallas kernels: 15.6 us -> 16.8 us
  waiting for transfers between devices: 6.31 us -> 7 us
    unnamed x17, local copies, waits for them, and re-layouts: 5.34 us -> 3.41 us
    pallas_call x1, Pallas kernels: 0.05 us -> 1.21 us  [on_device(): pl.pallas_call(functools.partial(pack_kernel, 0), out_shape=jax.ShapeDtyp...]
    ppermute x1, waiting for transfers between devices: 6.3 us -> 6.99 us  [on_device(): near = lax.ppermute(near_out, 'tm', near_pairs)]
  transfers between devices with their start and end apart: 3 -> 3, of which waited for: 1 -> 1; matrix products, arithmetic and copies ran while one was open for 2% -> 0% of each run, Pallas kernels for 19% -> 19%
where the time goes in v8:
time: 42.8 us; the launch traced here: 42.5 us
  Pallas kernels  16.8 us (39%)
  blocking collectives  10.3 us (24%)
  waiting for transfers between devices  7 us (16%)
  starting transfers between devices  5 us (12%)
  local copies, waits for them, and re-layouts  3.41 us (8%)
    all_to_all x1, blocking collectives, on_device(): parts = lax.all_to_all(payload, 'tm', 0, 0, tiled=True)  10.3 us
    ppermute x1, waiting for transfers between devices, on_device(): near = lax.ppermute(near_out, 'tm', near_pairs)  6.99 us
    pallas_call x1, Pallas kernels, on_device(): pl.pallas_call(early_kernel, out_shape=[jax.ShapeDtypeStruct((4 * HALF, w...  6.62 us
    pallas_call x1, Pallas kernels, on_device(): pl.pallas_call(late_kernel, out_shape=jax.ShapeDtypeStruct((horizon, lane...  6.26 us
    unnamed x17, local copies, waits for them, and re-layouts  3.41 us
    ppermute x1, starting transfers between devices, on_device(): got = lax.ppermute(swap_out, 'tm', swap)  3.02 us
    ppermute x1, starting transfers between devices, on_device(): near = lax.ppermute(near_out, 'tm', near_pairs)  1.29 us
    pallas_call x1, Pallas kernels, on_device(): pl.pallas_call(functools.partial(pack_kernel, 0), out_shape=jax.ShapeDtyp...  1.21 us
  transfers between devices with their start and end apart: 3, of which 1 were waited for; matrix products, arithmetic and copies ran while one was open for 0% of the time, Pallas kernels for 19%

profile of v8, /device:TPU:0, one launch (start us, length us, event | category | flops | bytes accessed | tf_op | source)
XLA Modules:
  0.0 42.5 jit_solution(15259457267631208107)
XLA Ops:
  0.0 0.0 copy-start
  0.0 0.0 copy-start.7
  0.0 0.0 copy-start.4
  0.0 0.0 copy-start.3
  0.0 1.2 %pack_swap.1 = bf16[4,128,512]{2,1,0:T(8,128)(2,1)S(1)} custom-call(bf16[4,256,512]{2,1,0:T(8,128)(2,1)} %bitcast.4), custom_call_target="tpu_custom_call" | custom-call | tf_op jit(solution)/shard_map/pack_swap/pallas_call | solution.py:238
  1.2 3.0 %collective-permute-start.1 = (bf16[4,128,512]{2,1,0:T(8,128)(2,1)S(1)}, bf16[4,128,512]{2,1,0:T(8,128)(2,1)S(1)}, u32[]{:S(2)}, u32[]{:S(2)}) collective-permute-start(bf16[4,128,512]{2,1,0:T(8,128)(2,1)S(1)} %pack_swap.1), channel_id=1, source_target_pairs={{0,1},{1,0},{2,3},{3,2},{4,5},{5,4},{6,7},{7,6},{8,9},{9,8},{10,11... | collective-permute-start | bytes 1572872 | tf_op jit(solution)/shard_map/ppermute | solution.py:247
  4.2 0.0 copy-done
  4.2 0.1 pack_halo.1
  4.4 1.3 %collective-permute-start.2 = (bf16[3,128,512]{2,1,0:T(8,128)(2,1)S(1)}, bf16[3,128,512]{2,1,0:T(8,128)(2,1)S(1)}, u32[]{:S(2)}, u32[]{:S(2)}) collective-permute-start(bf16[3,128,512]{2,1,0:T(8,128)(2,1)S(1)} %get-tuple-element.18), channel_id=1, source_target_pairs={{1,3},{3,5},{5,7},{2,0},{4,2},{6,4},{9,11},{11,13},{13,15},{10,8},... | collective-permute-start | bytes 1179656 | tf_op jit(solution)/shard_map/ppermute | solution.py:257
  5.7 0.7 %collective-permute-start = (bf16[3,128,512]{2,1,0:T(8,128)(2,1)S(1)}, bf16[3,128,512]{2,1,0:T(8,128)(2,1)S(1)}, u32[]{:S(2)}, u32[]{:S(2)}) collective-permute-start(bf16[3,128,512]{2,1,0:T(8,128)(2,1)S(1)} %get-tuple-element.17), channel_id=1, source_target_pairs={{1,2},{3,4},{5,6},{2,1},{4,3},{6,5},{9,10},{11,12},{13,14},{10,9},... | collective-permute-start | bytes 1179656 | tf_op jit(solution)/shard_map/ppermute | solution.py:258
  6.4 0.0 copy-done.7
  6.4 0.0 copy-done.4
  6.4 0.0 copy-done.3
  6.4 0.0 copy-start.1
  6.4 1.6 %copy-done.1 = bf16[2,512,1024]{2,1,0:T(8,128)(2,1)S(1)} copy-done((bf16[2,512,1024]{2,1,0:T(8,128)(2,1)S(1)}, bf16[2,512,1024]{2,1,0:T(8,128)(2,1)}, u32[]{:S(2)}) %copy-start.1) | copy-done | bytes 2097176
  8.0 0.0 copy-start.2
  8.0 1.6 %copy-done.2 = bf16[2,1024,512]{2,1,0:T(8,128)(2,1)S(1)} copy-done((bf16[2,1024,512]{2,1,0:T(8,128)(2,1)S(1)}, bf16[2,1024,512]{2,1,0:T(8,128)(2,1)}, u32[]{:S(2)}) %copy-start.2) | copy-done | bytes 2097176
  9.6 0.0 copy-start.5
  9.6 0.5 %stage.1 = (bf16[4,128,512]{2,1,0:T(8,128)(2,1)S(1)}, bf16[2,512,1024]{2,1,0:T(8,128)(2,1)S(1)}, bf16[2,1024,512]{2,1,0:T(8,128)(2,1)S(1)}, bf16[512,1024]{1,0:T(8,128)(2,1)S(1)}, bf16[512,512]{1,0:T(8,128)(2,1)S(1)}) custom-call(bf16[4,256,512]{2,1,0:T(8,128)(2,1)S(1)} %bitcast.6, bf16[2,512,1024]{2,1,0:T(8,128)(2,1)S(1)} %copy-done.1, ...), custom_call_target="tpu_custom_call" | custom-call | tf_op jit(solution)/shard_map/stage/pallas_call | solution.py:260
  10.1 0.2 copy-done.5
  10.3 0.0 copy-start.6
  10.3 1.0 %own.1.done = bf16[256,512]{1,0:T(8,128)(2,1)S(1)} custom-call(bf16[4,128,512]{2,1,0:T(8,128)(2,1)S(1)} %get-tuple-element.16.own, f32[2,3,512]{2,1,0:T(4,128)S(1)} %copy.9.taps, f32[2,512]{1,0:T(2,128)S(1)} %copy-done.5, bf16[2,512,1024]{2,1,0:T(8,128)(2,1)S(1)} %get-tuple-element.19.up_v, bf16[2,1024,512]{2,1,0:T(8,128)(2,1)S(1)} %get-tuple-element.20.down_v), custom_call_target="tpu_custom_call" | custom-call | flops 536870912 | bytes 4194304 | tf_op jit(solution)/shard_map/own/pallas_call | solution.py:272
  11.3 7.0 %collective-permute-done.2.near = bf16[3,128,512]{2,1,0:T(8,128)(2,1)S(1)} collective-permute-done((bf16[3,128,512]{2,1,0:T(8,128)(2,1)S(1)}, bf16[3,128,512]{2,1,0:T(8,128)(2,1)S(1)}, u32[]{:S(2)}, u32[]{:S(2)}) %collective-permute-start.2) | collective-permute-done | bytes 393248 | tf_op jit(solution)/shard_map/ppermute | solution.py:257
  18.3 0.0 collective-permute-done.1.got
  18.3 0.0 copy-done.6
  18.3 6.6 %early.1 = (bf16[512,512]{1,0:T(8,128)(2,1)S(1)}, f32[128,512]{1,0:T(8,128)S(1)}, f32[128,512]{1,0:T(8,128)S(1)}, f32[128,512]{1,0:T(8,128)S(1)}) custom-call(bf16[4,128,512]{2,1,0:T(8,128)(2,1)S(1)} %get-tuple-element.16.own, bf16[4,128,512]{2,1,0:T(8,128)(2,1)S(1)} %collective-permute-done.1.got, bf16[3,128,512]{2,1,0:T(8,128)(2,1)S(1)} %collective-permute-done.2.near, ...), custom_call_target="tpu_custom_call" | custom-call | flops 6442450944 | bytes 8388608 | tf_op jit(solution)/shard_map/early/pallas_call | solution.py:281
  25.0 0.0 collective-permute-done.far
  25.0 6.3 %late.1 = bf16[128,640]{1,0:T(8,128)(2,1)S(1)} custom-call(bf16[4,128,512]{2,1,0:T(8,128)(2,1)S(1)} %get-tuple-element.16.own, bf16[3,128,512]{2,1,0:T(8,128)(2,1)S(1)} %collective-permute-done.far, bf16[512,512]{1,0:T(8,128)(2,1)S(1)} %get-tuple-element.22.tail, f32[128,512]{1,0:T(8,128)S(1)} %get-tuple-element.23.acc, ...), custom_call_target="tpu_custom_call" | custom-call | flops 3221225472 | bytes 8388608 | tf_op jit(solution)/shard_map/late/pallas_call | solution.py:296
  31.2 10.3 %all_to_all.11 = bf16[8,16,640]{2,1,0:T(8,128)(2,1)S(1)} all-to-all(bf16[8,16,640]{2,1,0:T(8,128)(2,1)S(1)} %bitcast.8), channel_id=1, replica_groups=mesh['groups'=2,'series'=2,'tm'=8] {'tm'}, dimensions={0} | all-to-all | bytes 327680 | tf_op jit(solution)/shard_map/all_to_all | solution.py:310
  41.5 1.0 %final.1 = bf16[16,512]{1,0:T(8,128)(2,1)} custom-call(bf16[128,640]{1,0:T(8,128)(2,1)S(1)} %bitcast.7, bf16[512,512]{1,0:T(8,128)(2,1)S(1)} %get-tuple-element.26.readout), custom_call_target="tpu_custom_call" | custom-call | tf_op jit(solution)/shard_map/final/pallas_call | solution.py:311
  (1 shorter events, 0.0 us)
Async XLA Ops:
  0.0 4.2 %copy-start = (bf16[1,1024,512]{2,1,0:T(8,128)(2,1)S(1)}, bf16[1,1024,512]{2,1,0:T(8,128)(2,1)}, u32[]{:S(2)}) copy-start(bf16[1,1024,512]{2,1,0:T(8,128)(2,1)} %param.8) | copy-start | bytes 3145732
  0.0 6.4 %copy-start.7 = (f32[2,3,512]{2,0,1:T(2,128)S(1)}, f32[2,3,512]{2,0,1:T(2,128)}, u32[]{:S(2)}) copy-start(f32[2,3,512]{2,0,1:T(2,128)} %param.9) | copy-start | bytes 36868
  0.0 6.4 %copy-start.4 = (bf16[512,512]{1,0:T(8,128)(2,1)S(1)}, bf16[512,512]{1,0:T(8,128)(2,1)}, u32[]{:S(2)}) copy-start(bf16[512,512]{1,0:T(8,128)(2,1)} %refs_3_.1) | copy-start | bytes 1572868
  0.0 6.4 %copy-start.3 = (bf16[512,1024]{1,0:T(8,128)(2,1)S(1)}, bf16[512,1024]{1,0:T(8,128)(2,1)}, u32[]{:S(2)}) copy-start(bf16[512,1024]{1,0:T(8,128)(2,1)} %refs_2_.1) | copy-start | bytes 3145732
  1.2 17.1 %collective-permute-start.1 = (bf16[4,128,512]{2,1,0:T(8,128)(2,1)S(1)}, bf16[4,128,512]{2,1,0:T(8,128)(2,1)S(1)}, u32[]{:S(2)}, u32[]{:S(2)}) collective-permute-start(bf16[4,128,512]{2,1,0:T(8,128)(2,1)S(1)} %pack_swap.1), channel_id=1, source_target_pairs={{0,1},{1,0},{2,3},{3,2},{4,5},{5,4},{6,7},{7,6},{8,9},{9,8},{10,11... | collective-permute-start | bytes 1572872 | tf_op jit(solution)/shard_map/ppermute | solution.py:247
  4.4 13.9 %collective-permute-start.2 = (bf16[3,128,512]{2,1,0:T(8,128)(2,1)S(1)}, bf16[3,128,512]{2,1,0:T(8,128)(2,1)S(1)}, u32[]{:S(2)}, u32[]{:S(2)}) collective-permute-start(bf16[3,128,512]{2,1,0:T(8,128)(2,1)S(1)} %get-tuple-element.18), channel_id=1, source_target_pairs={{1,3},{3,5},{5,7},{2,0},{4,2},{6,4},{9,11},{11,13},{13,15},{10,8},... | collective-permute-start | bytes 1179656 | tf_op jit(solution)/shard_map/ppermute | solution.py:257
  5.7 19.3 %collective-permute-start = (bf16[3,128,512]{2,1,0:T(8,128)(2,1)S(1)}, bf16[3,128,512]{2,1,0:T(8,128)(2,1)S(1)}, u32[]{:S(2)}, u32[]{:S(2)}) collective-permute-start(bf16[3,128,512]{2,1,0:T(8,128)(2,1)S(1)} %get-tuple-element.17), channel_id=1, source_target_pairs={{1,2},{3,4},{5,6},{2,1},{4,3},{6,5},{9,10},{11,12},{13,14},{10,9},... | collective-permute-start | bytes 1179656 | tf_op jit(solution)/shard_map/ppermute | solution.py:258
  6.4 1.6 %copy-start.1 = (bf16[2,512,1024]{2,1,0:T(8,128)(2,1)S(1)}, bf16[2,512,1024]{2,1,0:T(8,128)(2,1)}, u32[]{:S(2)}) copy-start(bf16[2,512,1024]{2,1,0:T(8,128)(2,1)} %refs_0_.1) | copy-start | bytes 6291460
  8.0 1.6 %copy-start.2 = (bf16[2,1024,512]{2,1,0:T(8,128)(2,1)S(1)}, bf16[2,1024,512]{2,1,0:T(8,128)(2,1)}, u32[]{:S(2)}) copy-start(bf16[2,1024,512]{2,1,0:T(8,128)(2,1)} %refs_1_.1) | copy-start | bytes 6291460
  9.6 0.7 %copy-start.5 = (f32[2,512]{1,0:T(2,128)S(1)}, f32[2,512]{1,0:T(2,128)}, u32[]{:S(2)}) copy-start(f32[2,512]{1,0:T(2,128)} %gains.5) | copy-start | bytes 12292
  10.3 8.0 %copy-start.6 = (bf16[128,512]{1,0:T(8,128)(2,1)S(1)}, bf16[128,512]{1,0:T(8,128)(2,1)}, u32[]{:S(2)}) copy-start(bf16[128,512]{1,0:T(8,128)(2,1)} %queries.3) | copy-start | bytes 393220
